TPU v7x, 256 devices: a whole 4x4x8 slice. The times are simulated.
256 devices in a mesh: site: 32 (over y, z_lo, core), ev: 8 (over x, z_hi).
Axes of the slice: x: 4, y: 4, z: 8 (z_hi: 2, z_lo: 4; z = z_hi * 4 + z_lo), core: 2. Of those that a mesh axis runs over, the one named last changes fastest.
Arguments:
- eigvecs: float32 [2, 3, 192, 32, 2304], P(None, None, 'ev', 'site'), may hold values from -0.2766705 to 0.2766705
- links: float32 [3, 2, 3, 3, 32, 2304], P(None, None, None, None, 'site'), may hold values from -3.5 to 3.5
- momenta: int32 [4, 3], replicated, may hold values from -2 to 2
- directions: int32 [3], replicated, may hold values from 0 to 2, each once
Outputs:
- elementals: float32 [4, 4, 2, 192, 192], P(None, None, None, 'site', 'ev')
Inputs may be any that keep to these rules, and one draw needn't show every extreme that they name: The three directions are x, y, z in some order.
All inputs are finite; a program needn't handle non-finite values.
Results may differ from a plain program's by a relative error of at most 0.0001.
Values sent between devices are 32-bit elements; how exact they have to be, the bound alone decides.
No kernel may reach another device: no remote copies, remote signals or barrier semaphores. Data moves between devices by JAX's collectives and lax.ppermute only.
A program may use at most 128 MiB of HBM per device.

v0:
```python
import math

import jax
import jax.numpy as jnp
from jax import lax
from jax.sharding import PartitionSpec as P

LX = 48
LY = 48


def passed_along(value, axis, steps):
    count = lax.axis_size(axis)
    pairs = [(source, (source + steps) % count) for source in range(count)]
    return lax.ppermute(value, axis, pairs)


def phases(momenta, zstart, zcount, xycount, ztotal):
    zpos = zstart + jnp.arange(zcount, dtype=jnp.int32)
    plane = jnp.arange(xycount, dtype=jnp.int32)
    xpos = plane // LY
    ypos = plane % LY
    px = momenta[:, 0][:, None, None]
    py = momenta[:, 1][:, None, None]
    pz = momenta[:, 2][:, None, None]
    fracx = jnp.mod(px * xpos[None, None, :], LX).astype(jnp.float32) / LX
    fracy = jnp.mod(py * ypos[None, None, :], LY).astype(jnp.float32) / LY
    fracz = jnp.mod(pz * zpos[None, :, None], ztotal).astype(jnp.float32) / ztotal
    theta = 2.0 * math.pi * (fracx + fracy + fracz)
    return (jnp.cos(theta), jnp.sin(theta))


def transport(link, far):
    real = jnp.sum(link[0][:, :, None] * far[0][None] - link[1][:, :, None] * far[1][None], axis=1)
    imag = jnp.sum(link[0][:, :, None] * far[1][None] + link[1][:, :, None] * far[0][None], axis=1)
    return jnp.stack([real, imag])


def contract(left_vector, right, cosv, sine_phase_value):
    result = []
    for momentum_index in range(cosv.shape[0]):
        cosine_value = cosv[momentum_index]
        sine_value = sine_phase_value[momentum_index]
        left_real = left_vector[0] * cosine_value - left_vector[1] * sine_value
        left_imaginary = -(left_vector[0] * sine_value + left_vector[1] * cosine_value)
        weighted = jnp.stack([left_real, left_imaginary])
        prod = jnp.einsum("acrzs,dbcjzs->abdrj", weighted, right, precision=lax.Precision.HIGHEST)
        result.append(jnp.stack([prod[0, 0] - prod[1, 1], prod[0, 1] + prod[1, 0]], axis=1))
    return jnp.stack(result)


def local(eigvecs, links, momenta, directions):
    local_vecs = eigvecs.shape[2]
    zcount = eigvecs.shape[3]
    plane_size = eigvecs.shape[4]
    ztotal = zcount * lax.axis_size("site")
    zstart = lax.axis_index("site") * zcount
    above = passed_along(eigvecs, "site", -1)
    up_z = jnp.concatenate([eigvecs[:, :, :, 1:, :], above], axis=3)
    grid = eigvecs.reshape(2, 3, local_vecs, zcount, LX, LY)
    up_x = jnp.roll(grid, -1, axis=4).reshape(eigvecs.shape)
    up_y = jnp.roll(grid, -1, axis=5).reshape(eigvecs.shape)
    moved = jnp.stack(
        [transport(links[0], up_x), transport(links[1], up_y), transport(links[2], up_z)]
    )
    select = (directions[:, None] == jnp.arange(3, dtype=jnp.int32)[None, :]).astype(jnp.float32)
    chosen = jnp.einsum("dk,kabjzs->dabjzs", select, moved, precision=lax.Precision.HIGHEST)
    wfield = jnp.concatenate([eigvecs[None], chosen], axis=0)
    cosv, sine_phase_value = phases(momenta, zstart, zcount, plane_size, ztotal)
    partial_sums = contract(
        lax.all_gather(eigvecs, "ev", axis=2, tiled=True), wfield, cosv, sine_phase_value
    )
    return lax.psum_scatter(partial_sums, "site", scatter_dimension=3, tiled=True)


def solution(mesh):
    in_specs = (
        P(None, None, "ev", "site", None),
        P(None, None, None, None, "site", None),
        P(),
        P(),
    )
    out_specs = P(None, None, None, "site", "ev")
    return jax.shard_map(local, mesh=mesh, in_specs=in_specs, out_specs=out_specs, check_vma=False)
```

profile of v0, /device:TPU:1, one launch (start us, length us, event | category | flops | bytes accessed | tf_op | source)
XLA Modules:
  0.0 586.7 jit_solution(8839854640160589138)
XLA Ops:
  6.5 0.0 all-gather.2.cloned.1.call-start
  6.5 2.5 copy.28
  9.1 0.0 all-gather.2.cloned.1.call-update
  9.1 0.0 all-reduce.3.cloned.1.call-start
  9.1 3.3 collective-permute-start
  12.5 5.6 reduce.6
  18.0 3.5 reshape.756
  21.5 2.7 slice.239
  24.2 2.2 slice.235
  26.5 0.7 slice.236
  27.1 0.0 copy-done.10
  27.1 0.2 slice_reduce_fusion.9
  27.4 2.0 fusion.67
  29.3 1.6 sin.11
  30.9 4.8 fusion.22
  35.6 3.1 mul.531
  38.7 2.9 mul.526
  41.6 1.8 fusion.70
  43.5 0.1 copy_bitcast_fusion.4
  43.6 2.0 subtract_reduce_fusion.1
  45.6 1.3 stack.99
  46.9 1.3 stack.98
  48.2 2.3 fusion.23
  50.5 2.3 mul.519
  52.8 2.6 mul.514
  55.4 1.0 copy_bitcast_fusion.6
  56.4 0.6 subtract_reduce_fusion.2
  57.0 0.5 stack.95
  57.4 0.5 stack.94
  57.9 0.1 slice_reduce_fusion.6
  58.0 0.1 slice_reduce_fusion.7
  58.1 1.4 maximum_bitcast_fusion.14
  59.5 1.4 maximum_bitcast_fusion.13
  60.9 0.1 copy_bitcast_fusion.2
  61.0 0.0 collective-permute-done
  61.0 2.2 fusion.69
  63.2 0.0 copy-start.11
  63.2 0.2 copy_bitcast_fusion
  63.4 0.6 subtract_reduce_fusion
  63.9 0.5 stack.103
  64.4 0.5 stack.102
  64.9 1.4 maximum_bitcast_fusion.15
  66.2 0.0 copy-start.1
  66.3 8.9 %fusion.18 = f32[3,2,3,24,1,2304]{5,0,3,2,1,4:T(4,128)S(1)} fusion(f32[1,2,3,24,1,2304]{5,0,3,2,1,4:T(1,128)S(1)} %maximum_bitcast_fusion.15, f32[1,2,3,24,1,2304]{5,0,3,2,1,4:T(1,128)S(1)} %maximum_bitcast_fusion.14, f32[1,2,3,24,1,2304]{5,0,3,2,1,4:T(1,128)S(1)} %maximum_bitcast_fusion.13, s32[3]{0:T(128)S(1)} %copy-done.11), kind=kOutput, calls=%fused_computation.32 | convolution fusion | flops 37822472 | bytes 7962636 | tf_op jit(solution)/shard_map/dk,kabjzs->dabjzs/dot_general | solution.py:67
  75.2 4.8 maximum_bitcast_fusion.10
  80.0 144.7 %all-gather.2.cloned.1.call-done = f32[2,3,192,1,2304]{4,2,1,0,3:T(8,128)} async-done(((f32[2,3,24,1,2304]{4,2,1,0,3:T(8,128)}), f32[2,3,192,1,2304]{4,2,1,0,3:T(8,128)}) %all-gather.2.cloned.1.call-update) | async-done | bytes 10616848 | tf_op jit(solution)/shard_map/all_gather | solution.py:71
  224.7 13.6 %multiply_subtract_fusion.3 = (f32[1,3,192,1,2304]{4,2,1,0,3:T(8,128)}, f32[1,3,192,1,2304]{4,2,1,0,3:T(8,128)}, f32[1,3,192,1,2304]{4,2,1,0,3:T(8,128)}, f32[1,...) fusion(f32[2,3,192,1,2304]{4,2,1,0,3:T(8,128)} %all-gather.2.cloned.1.call-done, ...), kind=kLoop, calls=%fused_computation.31 | loop fusion | flops 27869184 | bytes 42522624 | tf_op jit(solution)/shard_map/sub | solution.py:44
  238.3 0.0 slice-start.2
  238.3 13.0 %fusion.24 = f32[2,2,4,192,24]{3,4,0,1,2:T(8,128)S(1)} fusion(f32[1,3,192,1,2304]{4,2,1,0,3:T(8,128)} %get-tuple-element.25, f32[1,3,192,1,2304]{4,2,1,0,3:T(8,128)} %get-tuple-element.24, f32[4,2,3,24,2304,1]{4,0,3,2,1,5:T(4,128)} %maximum_bitcast_fusion.10), kind=kOutput, calls=%fused_computation.53 | convolution fusion | flops 6117949440 | bytes 16220160 | tf_op jit(solution)/shard_map/acrzs,dbcjzs->abdrj/dot_general | solution.py:47
  251.4 5.2 multiply_subtract_fusion
  256.7 12.9 %fusion.27 = f32[2,2,4,192,24]{3,4,2,1,0:T(8,128)S(1)} fusion(f32[1,3,192,1,2304]{4,2,1,0,3:T(8,128)} %get-tuple-element.31, f32[1,3,192,1,2304]{4,2,1,0,3:T(8,128)} %get-tuple-element.30, f32[4,2,3,24,2304,1]{4,0,3,2,1,5:T(4,128)} %maximum_bitcast_fusion.10), kind=kOutput, calls=%fused_computation.54 | convolution fusion | flops 6117949440 | bytes 16220160 | tf_op jit(solution)/shard_map/acrzs,dbcjzs->abdrj/dot_general | solution.py:47
  269.6 0.0 slice-start.4
  269.6 0.0 slice-start.6
  269.6 0.0 slice-start.8
  269.6 12.3 %fusion.30 = f32[2,2,4,192,24]{3,4,2,1,0:T(8,128)S(1)} fusion(f32[1,3,192,1,2304]{4,2,1,0,3:T(8,128)S(1)} %copy-done.2, f32[1,3,192,1,2304]{4,2,1,0,3:T(8,128)} %get-tuple-element.35, f32[4,2,3,24,2304,1]{4,0,3,2,1,5:T(4,128)} %maximum_bitcast_fusion.10), kind=kOutput, calls=%fused_computation.55 | convolution fusion | flops 6117949440 | bytes 16220160 | tf_op jit(solution)/shard_map/acrzs,dbcjzs->abdrj/dot_general | solution.py:47
  282.0 9.8 %fusion.33 = f32[2,2,4,192,24]{3,4,2,1,0:T(8,128)S(1)} fusion(f32[1,3,192,1,2304]{4,2,1,0,3:T(8,128)S(1)} %bitcast.156, f32[1,3,192,1,2304]{4,2,1,0,3:T(8,128)S(1)} %bitcast.158, f32[4,2,3,24,2304,1]{4,0,3,2,1,5:T(4,128)S(1)} %bitcast.154), kind=kOutput, calls=%fused_computation.56 | convolution fusion | flops 6117949440 | bytes 16220160 | tf_op jit(solution)/shard_map/acrzs,dbcjzs->abdrj/dot_general | solution.py:47
  291.9 0.0 copy-start.12
  292.0 0.1 pad_maximum_fusion.2
  292.1 2.8 copy.38
  294.9 0.0 all-reduce.3.cloned.1.call-update
  294.9 0.6 dynamic-slice
  296.2 281.8 %all-reduce.3.cloned.1.call-done = f32[4,4,2,192,24]{4,1,2,0,3:T(4,128)} async-done(((f32[4,4,2,192,24]{4,1,2,0,3:T(4,128)}), f32[4,4,2,192,24]{4,1,2,0,3:T(4,128)}) %all-reduce.3.cloned.1.call-update) | async-done | bytes 589840
  578.0 0.9 constant_dynamic-slice_fusion
  578.9 0.7 copy.39
  (51 shorter events, 0.3 us)
Async XLA Ops:
  6.5 218.1 %all-gather.2.cloned.1.call-start = ((), (), s32[]{:S(2)}) async-start(), calls=%async_computation | async-start | bytes 11943936 | tf_op jit(solution)/shard_map/all_gather | solution.py:71
  9.1 568.9 %all-reduce.3.cloned.1.call-start = ((), (), s32[]{:S(2)}) async-start(), calls=%async_computation.1 | async-start | bytes 6291456
  9.1 51.8 %collective-permute-start = (f32[2,3,24,1,2304]{4,3,2,1,0:T(1,128)}, f32[2,3,24,1,2304]{4,3,2,1,0:T(1,128)}, u32[]{:S(2)}, u32[]{:S(2)}) collective-permute-start(f32[2,3,24,1,2304]{4,3,2,1,0:T(1,128)} %param.4), channel_id=1, source_target_pairs={{0,248},{8,0},{16,8},{24,16},{32,24},{40,32},{48,40},{56,48},{64,5... | collective-permute-start | bytes 3981320 | tf_op jit(solution)/shard_map/ppermute | solution.py:15
  24.2 2.9 copy-start.10
  35.6 12.5 %copy-start = (f32[2,3,24,1,47,48]{5,4,2,1,0,3:T(8,128)S(1)}, f32[2,3,24,1,47,48]{5,4,2,1,0,3:T(8,128)}, u32[]{:S(2)}) copy-start(f32[2,3,24,1,47,48]{5,4,2,1,0,3:T(8,128)} %slice.235) | copy-start | bytes 3898372
  41.6 6.5 %copy-start.7 = (f32[2,3,24,1,1,48]{5,4,2,1,0,3:T(1,128)S(1)}, f32[2,3,24,1,1,48]{5,4,2,1,0,3:T(1,128)}, u32[]{:S(2)}) copy-start(f32[2,3,24,1,1,48]{5,4,2,1,0,3:T(1,128)} %slice.236) | copy-start | bytes 82948
  50.5 7.4 %copy-start.9 = (f32[4,1,2304]{2,1,0:T(1,128)S(1)}, f32[4,1,2304]{2,1,0:T(1,128)}, u32[]{:S(2)}) copy-start(f32[4,1,2304]{2,1,0:T(1,128)} %sin.11) | copy-start | bytes 110596
  50.5 7.6 %copy-start.8 = (f32[4,1,2304]{2,1,0:T(1,128)S(1)}, f32[4,1,2304]{2,1,0:T(1,128)}, u32[]{:S(2)}) copy-start(f32[4,1,2304]{2,1,0:T(1,128)} %get-tuple-element.22) | copy-start | bytes 110596
  50.5 7.7 %copy-start.3 = (f32[1,3,24,1,2304]{4,3,2,1,0:T(1,128)S(1)}, f32[1,3,24,1,2304]{4,3,2,1,0:T(1,128)}, u32[]{:S(2)}) copy-start(f32[1,3,24,1,2304]{4,3,2,1,0:T(1,128)} %stack.99) | copy-start | bytes 1990660
  50.5 7.7 %copy-start.4 = (f32[1,3,24,1,2304]{4,3,2,1,0:T(1,128)S(1)}, f32[1,3,24,1,2304]{4,3,2,1,0:T(1,128)}, u32[]{:S(2)}) copy-start(f32[1,3,24,1,2304]{4,3,2,1,0:T(1,128)} %stack.98) | copy-start | bytes 1990660
  56.4 4.5 copy-start.5
  56.4 4.5 copy-start.6
  63.2 3.1 copy-start.11
  66.2 8.9 %copy-start.1 = (f32[2,3,24,1,2304]{4,3,2,1,0:T(1,128)S(1)}, f32[2,3,24,1,2304]{4,3,2,1,0:T(1,128)}, u32[]{:S(2)}) copy-start(f32[2,3,24,1,2304]{4,3,2,1,0:T(1,128)} %param.4) | copy-start | bytes 3981316
  238.3 13.1 %slice-start = ((s8[10616832]{0:T(1024)(128)(4,1)}), s8[4194304]{0:T(1024)(128)(4,1)S(1)}, s32[]{:S(2)}) async-start(s8[10616832]{0:T(1024)(128)(4,1)} %bitcast.150), calls=%async_computation.2 | async-start | bytes 8388608
  238.3 13.1 %slice-start.1 = ((s8[10616832]{0:T(1024)(128)(4,1)}), s8[4194304]{0:T(1024)(128)(4,1)S(1)}, s32[]{:S(2)}) async-start(s8[10616832]{0:T(1024)(128)(4,1)} %bitcast.150), calls=%async_computation.3 | async-start | bytes 8388608
  238.3 13.1 %slice-start.2 = ((s8[10616832]{0:T(1024)(128)(4,1)}), s8[2228224]{0:T(1024)(128)(4,1)S(1)}, s32[]{:S(2)}) async-start(s8[10616832]{0:T(1024)(128)(4,1)} %bitcast.150), calls=%async_computation.4 | async-start | bytes 4456448
  256.6 12.9 %copy-start.2 = (f32[1,3,192,1,2304]{4,2,1,0,3:T(8,128)S(1)}, f32[1,3,192,1,2304]{4,2,1,0,3:T(8,128)}, u32[]{:S(2)}) copy-start(f32[1,3,192,1,2304]{4,2,1,0,3:T(8,128)} %get-tuple-element.34) | copy-start | bytes 15925252
  256.6 25.3 %slice-start.3 = ((s8[5308416]{0:T(1024)(128)(4,1)}), s8[4194304]{0:T(1024)(128)(4,1)S(1)}, s32[]{:S(2)}) async-start(s8[5308416]{0:T(1024)(128)(4,1)} %bitcast.153), calls=%async_computation.5 | async-start | bytes 8388608
  256.6 25.3 %slice-start.5 = ((s8[5308416]{0:T(1024)(128)(4,1)}), s8[4194304]{0:T(1024)(128)(4,1)S(1)}, s32[]{:S(2)}) async-start(s8[5308416]{0:T(1024)(128)(4,1)} %bitcast.155), calls=%async_computation.7 | async-start | bytes 8388608
  256.6 25.3 %slice-start.7 = ((s8[5308416]{0:T(1024)(128)(4,1)}), s8[4194304]{0:T(1024)(128)(4,1)S(1)}, s32[]{:S(2)}) async-start(s8[5308416]{0:T(1024)(128)(4,1)} %bitcast.157), calls=%async_computation.9 | async-start | bytes 8388608
  269.6 12.4 %slice-start.4 = ((s8[5308416]{0:T(1024)(128)(4,1)}), s8[1114112]{0:T(1024)(128)(4,1)S(1)}, s32[]{:S(2)}) async-start(s8[5308416]{0:T(1024)(128)(4,1)} %bitcast.153), calls=%async_computation.6 | async-start | bytes 2228224
  269.6 12.4 %slice-start.6 = ((s8[5308416]{0:T(1024)(128)(4,1)}), s8[1114112]{0:T(1024)(128)(4,1)S(1)}, s32[]{:S(2)}) async-start(s8[5308416]{0:T(1024)(128)(4,1)} %bitcast.155), calls=%async_computation.8 | async-start | bytes 2228224
  269.6 12.4 %slice-start.8 = ((s8[5308416]{0:T(1024)(128)(4,1)}), s8[1114112]{0:T(1024)(128)(4,1)S(1)}, s32[]{:S(2)}) async-start(s8[5308416]{0:T(1024)(128)(4,1)} %bitcast.157), calls=%async_computation.10 | async-start | bytes 2228224
  291.9 3.1 copy-start.12
Sparse Core Ops, SparseCore 0:
  10.0 214.6 all-gather.1
  295.0 282.9 all-reduce.2
where the time goes:
time: 591 us; the launch traced here: 587 us
  waiting for transfers between devices  427 us (72%)
  matrix products  56.9 us (10%)
  other arithmetic  45.9 us (8%)
  local copies, waits for them, and re-layouts  39.1 us (7%)
  between operations  14.8 us (3%)
    unnamed x3, waiting for transfers between devices  282 us
    all_gather x1, waiting for transfers between devices, local(): lax.all_gather(eigvecs, 'ev', axis=2, tiled=True)  145 us
    dot_general x4, matrix products, contract(): jnp.einsum('acrzs,dbcjzs->abdrj', weighted, right, precision=lax.Precisio...  48 us
    sub x2, other arithmetic, contract(): left_real = left_vector[0] * cosine_value - left_vector[1] * sine_value  18.8 us
  transfers between devices with their start and end apart: 3, of which 2 were waited for; matrix products, arithmetic and copies ran while one was open for 12% of the time, Pallas kernels for 0%

commit v1 on v0

v1 whole, which is shorter than its diff:
```python
import math

import jax
import jax.numpy as jnp
from jax import lax
from jax.experimental import pallas as pl
from jax.experimental.pallas import tpu as pltpu
from jax.sharding import Mesh
from jax.sharding import PartitionSpec as P

LY = 48
OWN = 288
WIDE = 384
KPART = 3 * WIDE
VMEM_BYTES = 56 * 1024 * 1024


def cut_kernel(vec_ref, link_ref, out_ref, link_out_ref):
    part = lax.axis_index("x") * 2 + lax.axis_index("zh")
    vec = vec_ref[...]
    link = link_ref[...]
    chosen = None
    for other in range(8):
        begin = other * OWN
        here = min(WIDE, 2304 - begin)
        piece = vec[:, begin:begin + here]
        link_piece = link[:, begin:begin + here]
        if here < WIDE:
            piece = jnp.concatenate([piece, vec[:, :WIDE - here]], axis=1)
            link_piece = jnp.concatenate([link_piece, link[:, :WIDE - here]], axis=1)
        out_ref[other] = piece
        chosen = link_piece if chosen is None else jnp.where(part == other, link_piece, chosen)
    link_out_ref[...] = chosen


def wrapped(value, period):
    rest = lax.rem(value, period)
    return jnp.where(rest < 0, rest + period, rest)


def split(value):
    high = value.astype(jnp.bfloat16)
    return high, (value - high.astype(jnp.float32)).astype(jnp.bfloat16)


def main_kernel(mom_ref, buf_ref, above_ref, link_ref, away_ref, stay_ref, whi, wlo, lhi, llo):
    core = lax.axis_index("core")
    part = lax.axis_index("x") * 2 + lax.axis_index("zh")
    zpos = lax.axis_index("y") * 8 + lax.axis_index("zl") * 2 + core
    lane = lax.broadcasted_iota(jnp.int32, (8, WIDE), 1)
    line = jnp.zeros((8, WIDE), jnp.int32)
    for step in range(1, 8):
        line = line + (lane >= step * LY).astype(jnp.int32)
    ypos = lane - line * LY
    xpos = line + part * 6
    own = lane < OWN
    last = jnp.broadcast_to((ypos == LY - 1)[:1], (48, WIDE))

    def rows(ref, xs, field):
        first = ref[2 * xs, field * 24:(field + 1) * 24, :]
        second = ref[2 * xs + 1, field * 24:(field + 1) * 24, :]
        return jnp.concatenate([first, second], axis=0)

    def put(high_ref, low_ref, row, column, value):
        high, low = split(value)
        high_ref[pl.ds(row, 48), column:column + WIDE] = high
        low_ref[pl.ds(row, 48), column:column + WIDE] = low

    def make_fields(xs, carry):
        base = pl.multiple_of(xs * 192, 16)
        plain = [rows(buf_ref, xs, field) for field in range(6)]
        for field in range(6):
            put(whi, wlo, base, field * WIDE, plain[field])
        for direction in range(3):
            if direction == 0:
                far = [pltpu.roll(value, WIDE - LY, 1) for value in plain]
            elif direction == 1:
                far = [
                    jnp.where(last, pltpu.roll(value, LY - 1, 1), pltpu.roll(value, WIDE - 1, 1))
                    for value in plain
                ]
            else:
                far = [rows(above_ref, xs, field) for field in range(6)]
            for row in range(3):
                real = None
                imag = None
                for column in range(3):
                    at = direction * 18 + row * 3 + column
                    ur = link_ref[at:at + 1, :]
                    ui = link_ref[at + 9:at + 10, :]
                    re = ur * far[column] - ui * far[3 + column]
                    im = ur * far[3 + column] + ui * far[column]
                    real = re if real is None else real + re
                    imag = im if imag is None else imag + im
                put(whi, wlo, base + 48 * (direction + 1), row * WIDE, real)
                put(whi, wlo, base + 48 * (direction + 1), KPART + row * WIDE, imag)
        return carry

    lax.fori_loop(0, 4, make_fields, 0)

    def times(left, right):
        return lax.dot_general(
            left, right, (((1,), (1,)), ((), ())), preferred_element_type=jnp.float32
        )

    for group, out_ref in ((0, away_ref), (1, stay_ref)):
        def one_momentum(index, carry, out_ref=out_ref, group=group):
            p = (2 * (1 - core) if group == 0 else 2 * core) + index
            fx = wrapped(mom_ref[p, 0] * xpos, 48).astype(jnp.float32) / 48
            fy = wrapped(mom_ref[p, 1] * ypos, 48).astype(jnp.float32) / 48
            fz = wrapped(jnp.full((8, WIDE), mom_ref[p, 2] * zpos, jnp.int32), 32).astype(jnp.float32) / 32
            theta = (2.0 * math.pi) * (fx + fy + fz)
            cosv = jnp.where(own, jnp.cos(theta), 0.0)[:1]
            sinv = jnp.where(own, jnp.sin(theta), 0.0)[:1]

            def make_left(xs, carry):
                top = pl.multiple_of(xs * 48, 16)
                low = pl.multiple_of(xs * 48 + 192, 16)
                for color in range(3):
                    a = rows(buf_ref, xs, color)
                    b = rows(buf_ref, xs, 3 + color)
                    left_real = a * cosv - b * sinv
                    left_imag = -(a * sinv + b * cosv)
                    high, rest = split(left_real)
                    lhi[pl.ds(top, 48), color * WIDE:(color + 1) * WIDE] = high
                    llo[pl.ds(top, 48), color * WIDE:(color + 1) * WIDE] = rest
                    lhi[pl.ds(low, 48), KPART + color * WIDE:KPART + (color + 1) * WIDE] = high
                    llo[pl.ds(low, 48), KPART + color * WIDE:KPART + (color + 1) * WIDE] = rest
                    high, rest = split(left_imag)
                    lhi[pl.ds(low, 48), color * WIDE:(color + 1) * WIDE] = high
                    llo[pl.ds(low, 48), color * WIDE:(color + 1) * WIDE] = rest
                    lhi[pl.ds(top, 48), KPART + color * WIDE:KPART + (color + 1) * WIDE] = -high
                    llo[pl.ds(top, 48), KPART + color * WIDE:KPART + (color + 1) * WIDE] = -rest
                return carry

            lax.fori_loop(0, 4, make_left, 0)
            left_high = lhi[...]
            left_low = llo[...]
            total = times(left_high, whi[...]) + times(left_high, wlo[...]) + times(left_low, whi[...])
            for xs in range(4):
                both = jnp.concatenate(
                    [total[:192, xs * 192:(xs + 1) * 192], total[192:, xs * 192:(xs + 1) * 192]], axis=1
                )
                for ys in range(4):
                    out_ref[xs, ys, index] = both[ys * 48:(ys + 1) * 48]
            return carry

        lax.fori_loop(0, 2, one_momentum, 0)


def gather_kernel(part_ref, out_ref):
    halves = [[], []]
    for p in range(2):
        total = part_ref[0, p]
        for source in range(1, 16):
            total = total + part_ref[source, p]
        for piece in range(8):
            for zh in range(2):
                begin = piece * 48 + zh * 24
                halves[zh].append(total[:, begin:begin + 24])
    for zh in range(2):
        packed = jnp.concatenate(halves[zh], axis=1)
        for zl in range(4):
            for core in range(2):
                begin = zl * 12 + core * 6
                out_ref[zl * 4 + zh * 2 + core, :6] = packed[begin:begin + 6]
                out_ref[zl * 4 + zh * 2 + core, 6:] = jnp.zeros((2, WIDE), jnp.float32)


def last_kernel(direction_ref, part_ref, out_ref):
    for core in range(2):
        total = part_ref[core]
        for source in range(1, 8):
            total = total + part_ref[2 * source + core]
        for p in range(2):
            for reim in range(2):
                for d in range(4):
                    begin = p * 192 + reim * 96
                    if d == 0:
                        value = total[:6, begin:begin + 24]
                    else:
                        k = direction_ref[d - 1]
                        value = total[:6, begin + 24:begin + 48]
                        for other in range(1, 3):
                            at = begin + 24 + 24 * other
                            value = jnp.where(k == other, total[:6, at:at + 24], value)
                    out_ref[2 * core + p, d, reim] = value


def vmem(count):
    return [pl.BlockSpec(memory_space=pltpu.VMEM)] * count


def local(eigvecs, links, momenta, directions):
    f32 = jnp.float32
    params = pltpu.CompilerParams(vmem_limit_bytes=VMEM_BYTES)
    smem = [pl.BlockSpec(memory_space=pltpu.SMEM)]
    cut, link = pl.pallas_call(
        cut_kernel,
        out_shape=(
            jax.ShapeDtypeStruct((8, 144, WIDE), f32),
            jax.ShapeDtypeStruct((54, WIDE), f32),
        ),
        in_specs=vmem(2),
        out_specs=tuple(vmem(2)),
        compiler_params=params,
        name="cut",
    )(eigvecs.reshape(144, 2304), links.reshape(54, 2304))
    buf = lax.all_to_all(cut, ("x", "zh"), 0, 0)
    site = ("y", "zl", "core")
    above = lax.ppermute(buf, site, [(i, (i - 1) % 32) for i in range(32)])
    away, stay = pl.pallas_call(
        main_kernel,
        out_shape=(
            jax.ShapeDtypeStruct((4, 4, 2, 48, WIDE), f32),
            jax.ShapeDtypeStruct((4, 4, 2, 48, WIDE), f32),
        ),
        in_specs=smem + vmem(3),
        out_specs=tuple(vmem(2)),
        scratch_shapes=[
            pltpu.VMEM((768, 2 * KPART), jnp.bfloat16),
            pltpu.VMEM((768, 2 * KPART), jnp.bfloat16),
            pltpu.VMEM((384, 2 * KPART), jnp.bfloat16),
            pltpu.VMEM((384, 2 * KPART), jnp.bfloat16),
        ],
        compiler_params=params,
        name="contract",
    )(momenta, buf, above, link)
    stay = stay + lax.ppermute(away, "core", [(0, 1), (1, 0)])
    parts = lax.all_to_all(stay.reshape(16, 2, 48, WIDE), ("x", "y"), 0, 0)
    packed = pl.pallas_call(
        gather_kernel,
        out_shape=jax.ShapeDtypeStruct((16, 8, WIDE), f32),
        in_specs=vmem(1),
        out_specs=vmem(1)[0],
        compiler_params=params,
        name="gather",
    )(parts)
    parts = lax.all_to_all(packed, ("zl", "zh", "core"), 0, 0)
    return pl.pallas_call(
        last_kernel,
        out_shape=jax.ShapeDtypeStruct((4, 4, 2, 6, 24), f32),
        in_specs=smem + vmem(1),
        out_specs=vmem(1)[0],
        compiler_params=params,
        name="last",
    )(directions, parts)


def solution(mesh):
    fine = Mesh(mesh.devices.reshape(4, 4, 2, 4, 2), ("y", "zl", "core", "x", "zh"))
    site = ("y", "zl", "core")
    ev = ("x", "zh")
    in_specs = (P(None, None, ev, site, None), P(None, None, None, None, site, None), P(), P())
    out_specs = P(None, None, None, site, ev)
    return jax.shard_map(local, mesh=fine, in_specs=in_specs, out_specs=out_specs, check_vma=False)
```

time: 591 us -> 181 us (0.31)
  waiting for transfers between devices: 427 us -> 39.7 us
  blocking collectives: 0 us -> 93.7 us
  matrix products: 56.9 us -> 0 us
  other arithmetic: 45.9 us -> 4.47 us
  Pallas kernels: 0 us -> 35.8 us
  local copies, waits for them, and re-layouts: 39.1 us -> 5.02 us
  between operations: 14.8 us -> 0.02 us
    unnamed x3 -> x0, waiting for transfers between devices: 282 us -> none
    all_gather x1 -> x0, waiting for transfers between devices: 145 us -> none  [local(): lax.all_gather(eigvecs, 'ev', axis=2, tiled=True)]
    all_to_all x0 -> x3, blocking collectives: none -> 93.7 us  [the longest x1 42.7 us: local(): buf = lax.all_to_all(cut, ('x', 'zh'), 0, 0)]
    dot_general x5 -> x0, matrix products: 56.9 us -> none  [the longest x4 48 us: contract(): jnp.einsum('acrzs,dbcjzs->abdrj', weighted, right, precision=lax.Precisio...]
    ppermute x1 -> x2, waiting for transfers between devices: 0.01 us -> 39.7 us  [the longest x1 35 us: local(): above = lax.ppermute(buf, site, [(i, (i - 1) % 32) for i in range(32)])]
    pallas_call x0 -> x4, Pallas kernels: none -> 35.8 us  [the longest x1 27.9 us: local(): pl.pallas_call(main_kernel, out_shape=(jax.ShapeDtypeStruct((4, 4, 2, 48,...]
    sub x6 -> x0, other arithmetic: 18.9 us -> none  [the longest x2 18.8 us: contract(): left_real = left_vector[0] * cosine_value - left_vector[1] * sine_value]
    mul x4 -> x0, local copies, waits for them, and re-layouts: 10.9 us -> none  [the longest x2 5.48 us: transport(): link[0][:, :, None] * far[0][None] - link[1][:, :, None] * far[1][None]]
  transfers between devices with their start and end apart: 3 -> 2, of which waited for: 2 -> 2; matrix products, arithmetic and copies ran while one was open for 12% -> 0% of each run, Pallas kernels for 0% -> 0%
where the time goes in v1:
time: 181 us
  blocking collectives  93.7 us (52%)
  waiting for transfers between devices  39.7 us (22%)
  Pallas kernels  35.8 us (20%)
  local copies, waits for them, and re-layouts  5.02 us (3%)
  other arithmetic  4.47 us (2%)
  starting transfers between devices  1.95 us (1%)
    all_to_all x1, blocking collectives, local(): buf = lax.all_to_all(cut, ('x', 'zh'), 0, 0)  42.7 us
    all_to_all x1, blocking collectives, local(): parts = lax.all_to_all(stay.reshape(16, 2, 48, WIDE), ('x', 'y'), 0, 0)  35.2 us
    ppermute x1, waiting for transfers between devices, local(): above = lax.ppermute(buf, site, [(i, (i - 1) % 32) for i in range(32)])  35 us
    pallas_call x1, Pallas kernels, local(): pl.pallas_call(main_kernel, out_shape=(jax.ShapeDtypeStruct((4, 4, 2, 48,...  27.9 us
    all_to_all x1, blocking collectives, local(): parts = lax.all_to_all(packed, ('zl', 'zh', 'core'), 0, 0)  15.8 us
    ppermute x1, waiting for transfers between devices, local(): stay = stay + lax.ppermute(away, 'core', [(0, 1), (1, 0)])  4.74 us
  transfers between devices with their start and end apart: 2, of which 2 were waited for; matrix products, arithmetic and copies ran while one was open for 0% of the time, Pallas kernels for 0%

profile of v1, /device:TPU:1, one launch (start us, length us, event | category | flops | bytes accessed | tf_op | source)
XLA Modules:
  0.0 180.6 jit_solution(7310452516828280930)
XLA Ops:
  0.0 0.0 copy-start.2
  0.0 2.5 %reduce = f32[3,2,3,3,2304]{4,3,2,1,0:T(4,128)S(1)} reduce(f32[3,2,3,3,1,2304]{5,4,3,2,1,0:T(1,128)} %param.5, f32[]{:T(128)} %constant.2), dimensions={4}, to_apply=%param.5.reduce_sub_computation | reduce | bytes 995332 | tf_op args[1]
  2.5 1.0 reshape.10.link_ref
  3.5 0.0 copy-done.2
  3.5 1.2 copy.6
  4.7 3.4 %cut.1 = (f32[8,144,384]{2,1,0:T(8,128)}, f32[54,384]{1,0:T(8,128)}) custom-call(f32[144,2304]{1,0:T(8,128)} %bitcast.3, f32[54,2304]{1,0:T(8,128)} %reshape.10.link_ref), custom_call_target="tpu_custom_call" | custom-call | tf_op jit(solution)/shard_map/cut/pallas_call | solution.py:198
  8.1 42.7 %all_to_all.15.buf_ref = f32[8,144,384]{2,1,0:T(8,128)S(1)} all-to-all(f32[8,144,384]{2,1,0:T(8,128)} %get-tuple-element.9), channel_id=1, replica_groups=mesh['y'=4,'zl'=4,'core'=2,'x'=4,'zh'=2] {'x','zh'}, dimensions={0} | all-to-all | bytes 3538944 | tf_op jit(solution)/shard_map/all_to_all | solution.py:209
  50.7 0.0 copy-start
  50.7 2.0 %collective-permute-start = (f32[8,144,384]{2,1,0:T(8,128)S(1)}, f32[8,144,384]{2,1,0:T(8,128)S(1)}, u32[]{:S(2)}, u32[]{:S(2)}) collective-permute-start(f32[8,144,384]{2,1,0:T(8,128)S(1)} %all_to_all.15.buf_ref), channel_id=1, source_target_pairs={{0,248},{8,0},{16,8},{24,16},{32,24},{40,32},{48,40},{56,48},{64,5... | collective-permute-start | bytes 5308424 | tf_op jit(solution)/shard_map/ppermute | solution.py:211
  52.7 35.0 %collective-permute-done.above_ref = f32[8,144,384]{2,1,0:T(8,128)S(1)} collective-permute-done((f32[8,144,384]{2,1,0:T(8,128)S(1)}, f32[8,144,384]{2,1,0:T(8,128)S(1)}, u32[]{:S(2)}, u32[]{:S(2)}) %collective-permute-start) | collective-permute-done | bytes 1769504 | tf_op jit(solution)/shard_map/ppermute | solution.py:211
  87.7 0.0 copy-start.1
  87.7 0.0 copy-done
  87.7 1.2 copy-done.1
  88.9 27.9 %contract.1 = (f32[4,4,2,48,384]{4,3,2,1,0:T(8,128)}, f32[4,4,2,48,384]{4,3,2,1,0:T(8,128)}) custom-call(s32[4,3]{1,0:T(4,128)} %mom_ref.1, f32[8,144,384]{2,1,0:T(8,128)} %copy-done, f32[8,144,384]{2,1,0:T(8,128)} %copy-done.1, f32[54,384]{1,0:T(8,128)} %get-tuple-element.10.link_ref), custom_call_target="tpu_custom_call" | custom-call | tf_op jit(solution)/shard_map/contract/pallas_call | solution.py:212
  116.8 0.0 collective-permute-start.1
  116.8 4.7 %collective-permute-done.1 = f32[4,4,2,48,384]{4,3,2,1,0:T(8,128)S(1)} collective-permute-done((f32[4,4,2,48,384]{4,3,2,1,0:T(8,128)}, f32[4,4,2,48,384]{4,3,2,1,0:T(8,128)S(1)}, u32[]{:S(2)}, u32[]{:S(2)}) %collective-permute-start.1) | collective-permute-done | bytes 2359328 | tf_op jit(solution)/shard_map/ppermute | solution.py:229
  121.6 2.0 %add.3 = f32[4,4,2,48,384]{4,3,2,1,0:T(8,128)S(1)} add(f32[4,4,2,48,384]{4,3,2,1,0:T(8,128)} %get-tuple-element.11, f32[4,4,2,48,384]{4,3,2,1,0:T(8,128)S(1)} %collective-permute-done.1) | non-fusion elementwise | flops 589824 | bytes 7077888 | tf_op jit(solution)/shard_map/add | solution.py:229
  123.6 35.2 %all_to_all.16.part_ref = f32[16,2,48,384]{3,2,1,0:T(8,128)} all-to-all(f32[16,2,48,384]{3,2,1,0:T(8,128)S(1)} %bitcast.2), channel_id=1, replica_groups=mesh['y'=4,'zl'=4,'core'=2,'x'=4,'zh'=2] {'x','y'}, dimensions={0} | all-to-all | bytes 4718592 | tf_op jit(solution)/shard_map/all_to_all | solution.py:230
  158.8 2.6 %gather.1 = f32[16,8,384]{2,1,0:T(8,128)} custom-call(f32[16,2,48,384]{3,2,1,0:T(8,128)} %all_to_all.16.part_ref), custom_call_target="tpu_custom_call" | custom-call | tf_op jit(solution)/shard_map/gather/pallas_call | solution.py:231
  161.3 15.8 %all_to_all.17.part_ref = f32[16,8,384]{2,1,0:T(8,128)} all-to-all(f32[16,8,384]{2,1,0:T(8,128)} %gather.1), channel_id=1, replica_groups=mesh['y'=4,'zl'=4,'core'=2,'x'=4,'zh'=2] {'zl','zh','core'}, dimensions={0} | all-to-all | bytes 393216 | tf_op jit(solution)/shard_map/all_to_all | solution.py:239
  177.2 1.8 %last.1 = f32[4,4,2,6,24]{4,3,2,1,0:T(8,128)} custom-call(s32[3]{0:T(128)} %direction_ref.1, f32[16,8,384]{2,1,0:T(8,128)} %all_to_all.17.part_ref), custom_call_target="tpu_custom_call" | custom-call | tf_op jit(solution)/shard_map/last/pallas_call | solution.py:240
  179.0 1.6 copy.5
Async XLA Ops:
  0.0 3.5 %copy-start.2 = (f32[2,3,24,1,2304]{4,3,2,1,0:T(1,128)S(1)}, f32[2,3,24,1,2304]{4,3,2,1,0:T(1,128)}, u32[]{:S(2)}) copy-start(f32[2,3,24,1,2304]{4,3,2,1,0:T(1,128)} %param.4) | copy-start | bytes 3981316
  50.7 36.9 %copy-start = (f32[8,144,384]{2,1,0:T(8,128)}, f32[8,144,384]{2,1,0:T(8,128)S(1)}, u32[]{:S(2)}) copy-start(f32[8,144,384]{2,1,0:T(8,128)S(1)} %all_to_all.15.buf_ref) | copy-start | bytes 5308420
  50.7 36.9 %collective-permute-start = (f32[8,144,384]{2,1,0:T(8,128)S(1)}, f32[8,144,384]{2,1,0:T(8,128)S(1)}, u32[]{:S(2)}, u32[]{:S(2)}) collective-permute-start(f32[8,144,384]{2,1,0:T(8,128)S(1)} %all_to_all.15.buf_ref), channel_id=1, source_target_pairs={{0,248},{8,0},{16,8},{24,16},{32,24},{40,32},{48,40},{56,48},{64,5... | collective-permute-start | bytes 5308424 | tf_op jit(solution)/shard_map/ppermute | solution.py:211
  87.7 1.2 copy-start.1
  116.8 4.7 %collective-permute-start.1 = (f32[4,4,2,48,384]{4,3,2,1,0:T(8,128)}, f32[4,4,2,48,384]{4,3,2,1,0:T(8,128)S(1)}, u32[]{:S(2)}, u32[]{:S(2)}) collective-permute-start(f32[4,4,2,48,384]{4,3,2,1,0:T(8,128)} %get-tuple-element.12), channel_id=1, source_target_pairs={{0,8},{8,0},{1,9},{9,1},{2,10},{10,2},{3,11},{11,3},{4,12},{12,4},... | collective-permute-start | bytes 7077896 | tf_op jit(solution)/shard_map/ppermute | solution.py:229

commit v2 on v0

v2 whole, which is shorter than its diff:
```python
import math

import jax
import jax.numpy as jnp
from jax import lax
from jax.experimental import pallas as pl
from jax.experimental.pallas import tpu as pltpu
from jax.sharding import Mesh
from jax.sharding import PartitionSpec as P

LY = 48
OWN = 288
TAIL = 32
ROWS = 384
DEPTH = 896
TAIL_ROW = 288
FAR_ROW = 336
VMEM_BYTES = 40 * 1024 * 1024


def cut_kernel(vec_ref, link_ref, out_ref, link_out_ref):
    part = lax.axis_index("x") * 2 + lax.axis_index("zh")
    for other in range(8):
        begin = other * OWN
        halo = (begin + OWN) % 2304
        out_ref[other, 0:144] = vec_ref[:, begin:begin + 128]
        out_ref[other, 144:288] = vec_ref[:, begin + 128:begin + 256]
        for reim in range(2):
            tails = []
            firsts = []
            lasts = []
            for color in range(3):
                row = (reim * 3 + color) * 24
                tails.append(vec_ref[row:row + 24, begin + 256:begin + 288])
                firsts.append(vec_ref[row:row + 24, halo:halo + 16])
                lasts.append(vec_ref[row:row + 24, halo + 16:halo + 48])
            row = TAIL_ROW + reim * 24
            out_ref[other, row:row + 24] = jnp.concatenate(tails + firsts[:2], axis=1)
            row = FAR_ROW + reim * 24
            out_ref[other, row:row + 24] = jnp.concatenate(
                lasts + [firsts[2], firsts[2]], axis=1
            )
    link = link_ref[...]
    chosen = None
    for other in range(8):
        begin = other * OWN
        piece = link[:, begin:begin + OWN]
        chosen = piece if chosen is None else jnp.where(part == other, piece, chosen)
    link_out_ref[0, :54] = chosen[:, :128]
    link_out_ref[1, :54] = chosen[:, 128:256]
    tail = chosen[:, 256:288]
    for first in range(6):
        for turn in range(3):
            pieces = []
            for row in range(3):
                at = first * 9 + row * 3 + (row + turn) % 3
                pieces.append(tail[at:at + 1])
            pieces.append(jnp.zeros((1, 32), jnp.float32))
            at = first * 3 + turn
            link_out_ref[2, at:at + 1] = jnp.concatenate(pieces, axis=1)


def wrapped(value, period):
    rest = lax.rem(value, period)
    return jnp.where(rest < 0, rest + period, rest)


def split(value):
    high = value.astype(jnp.bfloat16)
    return high, (value - high.astype(jnp.float32)).astype(jnp.bfloat16)


def lanes(rows=48):
    return lax.broadcasted_iota(jnp.int32, (rows, 128), 1)


def tiles_of(ref, xs):
    def rows(row):
        return jnp.concatenate([ref[2 * xs, row:row + 24], ref[2 * xs + 1, row:row + 24]], axis=0)

    return [
        [
            [rows((reim * 3 + color) * 24) for color in range(3)]
            + [rows(144 + (reim * 3 + color) * 24) for color in range(3)]
            + [rows(TAIL_ROW + reim * 24)]
        ][0]
        for reim in range(2)
    ]


def put_tiles(high_ref, low_ref, row, tiles):
    for index, value in enumerate(tiles):
        high, low = split(value)
        column = (2 * index if index < 3 else 2 * (index - 3) + 1) * 128 if index < 6 else 768
        high_ref[pl.ds(row, 48), column:column + 128] = high
        low_ref[pl.ds(row, 48), column:column + 128] = low


def beyond_x(tiles, far):
    lane = lanes()
    low, high, tail = tiles[:3], tiles[3:6], tiles[6]
    result = []
    for color in range(3):
        result.append(jnp.where(lane < 80, pltpu.roll(low[color], 80, 1), pltpu.roll(high[color], 80, 1)))
    for color in range(3):
        own = pltpu.roll(tail, (80 - 32 * color) % 128, 1)
        if color == 0:
            first = pltpu.roll(tail, 16, 1)
        elif color == 1:
            first = tail
        else:
            first = pltpu.roll(far, 16, 1)
        value = jnp.where(lane < 80, pltpu.roll(high[color], 80, 1), own)
        result.append(jnp.where(lane < 112, value, first))
    result.append(far)
    return result


def beyond_y(tiles):
    lane = lanes()
    low, high, tail = tiles[:3], tiles[3:6], tiles[6]
    result = []
    for color in range(3):
        value = pltpu.roll(low[color], 127, 1)
        value = jnp.where((lane == 47) | (lane == 95), pltpu.roll(low[color], 47, 1), value)
        result.append(jnp.where(lane == 127, pltpu.roll(high[color], 127, 1), value))
    for color in range(3):
        value = pltpu.roll(high[color], 127, 1)
        value = jnp.where((lane == 63) | (lane == 111), pltpu.roll(high[color], 47, 1), value)
        value = jnp.where(lane == 15, pltpu.roll(low[color], 47, 1), value)
        result.append(jnp.where(lane == 127, pltpu.roll(tail, (127 - 32 * color) % 128, 1), value))
    value = pltpu.roll(tail, 127, 1)
    for color in range(3):
        at = 32 * color + 31
        value = jnp.where(lane == at, pltpu.roll(high[color], (at - 112) % 128, 1), value)
    result.append(value)
    return result


def turned(tail, turn):
    lane = lanes()
    if turn == 0:
        return tail
    if turn == 1:
        return jnp.where(lane < 64, pltpu.roll(tail, 96, 1), pltpu.roll(tail, 64, 1))
    return jnp.where(lane < 32, pltpu.roll(tail, 64, 1), pltpu.roll(tail, 32, 1))


def moved(real, imag, link_ref, direction):
    out_real = []
    out_imag = []
    for half in range(2):
        for row in range(3):
            re = None
            im = None
            for column in range(3):
                at = direction * 18 + row * 3 + column
                ur = link_ref[half, at:at + 1, :]
                ui = link_ref[half, at + 9:at + 10, :]
                fr = real[3 * half + column]
                fi = imag[3 * half + column]
                more_re = ur * fr - ui * fi
                more_im = ur * fi + ui * fr
                re = more_re if re is None else re + more_re
                im = more_im if im is None else im + more_im
            out_real.append(re)
            out_imag.append(im)
    re = None
    im = None
    for turn in range(3):
        at = direction * 6 + turn
        ur = link_ref[2, at:at + 1, :]
        ui = link_ref[2, at + 3:at + 4, :]
        fr = turned(real[6], turn)
        fi = turned(imag[6], turn)
        more_re = ur * fr - ui * fi
        more_im = ur * fi + ui * fr
        re = more_re if re is None else re + more_re
        im = more_im if im is None else im + more_im
    out_real.append(re)
    out_imag.append(im)
    return out_real, out_imag


def contract(chunk, mom_ref, buf_ref, above_ref, link_ref, away_ref, stay_ref, whi, wlo, lhi, llo):
    core = lax.axis_index("core")
    part = lax.axis_index("x") * 2 + lax.axis_index("zh")
    zpos = lax.axis_index("y") * 8 + lax.axis_index("zl") * 2 + core

    def make_fields(xs, carry):
        base = pl.multiple_of(xs * 96, 16)
        real, imag = tiles_of(buf_ref, xs)
        if chunk == 0:
            far = [
                jnp.concatenate([buf_ref[2 * xs, row:row + 24], buf_ref[2 * xs + 1, row:row + 24]], axis=0)
                for row in (FAR_ROW, FAR_ROW + 24)
            ]
            first = (real, imag)
            second = moved(beyond_x(real, far[0]), beyond_x(imag, far[1]), link_ref, 0)
        else:
            first = moved(beyond_y(real), beyond_y(imag), link_ref, 1)
            second = moved(*tiles_of(above_ref, xs), link_ref, 2)
        for k, field in enumerate((first, second)):
            for reim in range(2):
                put_tiles(whi, wlo, base + reim * 384 + k * 48, field[reim])
        return carry

    lax.fori_loop(0, 4, make_fields, 0)

    lane = lanes(8)
    sites = [lane, lane + 128, 256 + lax.rem(lane, 32)]
    lines = []
    for site in sites:
        line = jnp.zeros((8, 128), jnp.int32)
        for step in range(1, 6):
            line = line + (site >= step * LY).astype(jnp.int32)
        lines.append(line)

    def times(left, right):
        return lax.dot_general(
            left, right, (((1,), (1,)), ((), ())), preferred_element_type=jnp.float32
        )

    for group, out_ref in ((0, away_ref), (1, stay_ref)):
        for index in range(2):
            p = (2 * (1 - core) if group == 0 else 2 * core) + index
            phase = []
            for at in range(3):
                xpos = lines[at] + part * 6
                ypos = sites[at] - lines[at] * LY
                fx = wrapped(mom_ref[p, 0] * xpos, 48).astype(jnp.float32) / 48
                fy = wrapped(mom_ref[p, 1] * ypos, 48).astype(jnp.float32) / 48
                fz = wrapped(jnp.full((8, 128), mom_ref[p, 2] * zpos, jnp.int32), 32)
                theta = (2.0 * math.pi) * (fx + fy + fz.astype(jnp.float32) / 32)
                cosv = jnp.cos(theta)
                sinv = jnp.sin(theta)
                if at == 2:
                    cosv = jnp.where(lane < 96, cosv, 0.0)
                    sinv = jnp.where(lane < 96, sinv, 0.0)
                phase.append((cosv[:1], sinv[:1]))

            def make_left(xs, carry, phase=phase):
                top = pl.multiple_of(xs * 48, 16)
                real, imag = tiles_of(buf_ref, xs)
                left_real = []
                left_imag = []
                for at in range(7):
                    cosv, sinv = phase[at // 3]
                    left_real.append(real[at] * cosv - imag[at] * sinv)
                    left_imag.append(-(real[at] * sinv + imag[at] * cosv))
                put_tiles(lhi, llo, top, left_real)
                put_tiles(lhi, llo, top + 192, left_imag)
                return carry

            lax.fori_loop(0, 4, make_left, 0)
            left_high = lhi[...]
            left_low = llo[...]
            total = times(left_high, whi[...]) + times(left_high, wlo[...]) + times(left_low, whi[...])
            product = (
                total[:192, :384] - total[192:, 384:],
                total[192:, :384] + total[:192, 384:],
            )
            for reim in range(2):
                column = (2 * index + reim) * 96
                for xs in range(4):
                    value = product[reim][:, xs * 96:(xs + 1) * 96]
                    for ys in range(4):
                        out_ref[xs, ys, :, column:column + 96] = value[ys * 48:(ys + 1) * 48]


def first_kernel(mom_ref, buf_ref, link_ref, away_ref, stay_ref, *scratch):
    contract(0, mom_ref, buf_ref, None, link_ref, away_ref, stay_ref, *scratch)


def second_kernel(mom_ref, buf_ref, above_ref, link_ref, away_ref, stay_ref, *scratch):
    contract(1, mom_ref, buf_ref, above_ref, link_ref, away_ref, stay_ref, *scratch)


def add_kernel(stay_ref, came_ref, *out_refs):
    mine = {"y": lax.axis_index("y"), "x": lax.axis_index("x")}
    for step in range(4):
        to_y = lax.rem(mine["y"] + step, 4)
        to_x = lax.rem(mine["x"] + step, 4)
        for other in range(4):
            out_refs[step][other] = stay_ref[other, to_y, :24] + came_ref[other, to_y, :24]
            out_refs[4 + step][other] = stay_ref[to_x, other, 24:] + came_ref[to_x, other, 24:]


def sum_kernel(*refs):
    ins, outs = refs[:16], refs[16:]
    mine = (lax.axis_index("x"), lax.axis_index("y"))
    for chunk in range(2):
        for half in range(2):
            group = ins[chunk * 8 + half * 4:chunk * 8 + half * 4 + 4]
            for step in range(4):
                to = lax.rem(mine[half] + step, 4)
                total = group[0][to]
                for source in range(1, 4):
                    total = total + group[source][to]
                outs[half * 4 + step][chunk] = total


def gather_kernel(*refs):
    ins, out_ref = refs[:8], refs[8]
    for half in range(2):
        pieces = [[], []]
        for chunk in range(2):
            total = ins[4 * half][chunk]
            for source in range(1, 4):
                total = total + ins[4 * half + source][chunk]
            for piece in range(8):
                for zh in range(2):
                    begin = piece * 48 + zh * 24
                    pieces[zh].append(total[:, begin:begin + 24])
        for zh in range(2):
            packed = jnp.concatenate(pieces[zh], axis=1)
            for zl in range(2):
                for core in range(2):
                    begin = zl * 12 + core * 6
                    to = (2 * half + zl) * 4 + zh * 2 + core
                    out_ref[to, :6] = packed[begin:begin + 6]
                    out_ref[to, 6:] = jnp.zeros((2, 384), jnp.float32)


def last_kernel(direction_ref, part_ref, out_ref):
    for core in range(2):
        total = part_ref[core]
        for source in range(1, 8):
            total = total + part_ref[2 * source + core]
        total = total[:6]
        for p in range(2):
            for reim in range(2):
                begin = p * 96 + reim * 48
                fields = []
                for field in range(4):
                    at = begin + (field // 2) * 192 + (field % 2) * 24
                    fields.append(total[:, at:at + 24])
                out_ref[2 * core + p, 0, reim] = fields[0]
                for d in range(1, 4):
                    k = direction_ref[d - 1]
                    value = jnp.where(k == 1, fields[2], fields[1])
                    out_ref[2 * core + p, d, reim] = jnp.where(k == 2, fields[3], value)


def vmem(count):
    return [pl.BlockSpec(memory_space=pltpu.VMEM)] * count


def call(kernel, name, out_shapes, operands, scratch=(), scalars=0):
    out_shape = tuple(jax.ShapeDtypeStruct(shape, jnp.float32) for shape in out_shapes)
    return pl.pallas_call(
        kernel,
        out_shape=out_shape,
        in_specs=[pl.BlockSpec(memory_space=pltpu.SMEM)] * scalars + vmem(len(operands) - scalars),
        out_specs=tuple(vmem(len(out_shapes))),
        scratch_shapes=list(scratch),
        compiler_params=pltpu.CompilerParams(vmem_limit_bytes=VMEM_BYTES),
        name=name,
    )(*operands)


def around(value, axis, step):
    return lax.ppermute(value, axis, [(i, (i + step) % 4) for i in range(4)])


def local(eigvecs, links, momenta, directions):
    cut, link = call(
        cut_kernel, "cut", [(8, ROWS, 128), (3, 56, 128)],
        (eigvecs.reshape(144, 2304), links.reshape(54, 2304)),
    )
    buf = lax.all_to_all(cut, ("x", "zh"), 0, 0)
    above = lax.ppermute(buf, ("y", "zl", "core"), [(i, (i - 1) % 32) for i in range(32)])
    scratch = [pltpu.VMEM((768, DEPTH), jnp.bfloat16)] * 2 + [pltpu.VMEM((384, DEPTH), jnp.bfloat16)] * 2
    sums = []
    for chunk in range(2):
        away, stay = call(
            (first_kernel, second_kernel)[chunk], ("contract_vx", "contract_yz")[chunk],
            [(4, 4, 48, 384)] * 2,
            (momenta, buf, link) if chunk == 0 else (momenta, buf, above, link),
            scratch, 1,
        )
        came = lax.ppermute(away, "core", [(0, 1), (1, 0)])
        ready = call(add_kernel, "add", [(4, 24, 384)] * 8, (stay, came))
        sums += [ready[0]] + [around(ready[step], "y", step) for step in range(1, 4)]
        sums += [ready[4]] + [around(ready[4 + step], "x", step) for step in range(1, 4)]
    ready = call(sum_kernel, "sum", [(2, 24, 384)] * 8, sums)
    sums = [ready[0]] + [around(ready[step], "x", step) for step in range(1, 4)]
    sums += [ready[4]] + [around(ready[4 + step], "y", step) for step in range(1, 4)]
    packed, = call(gather_kernel, "gather", [(16, 8, 384)], sums)
    parts = lax.all_to_all(packed, ("zl", "zh", "core"), 0, 0)
    return call(last_kernel, "last", [(4, 4, 2, 6, 24)], (directions, parts), (), 1)[0]


def solution(mesh):
    fine = Mesh(mesh.devices.reshape(4, 4, 2, 4, 2), ("y", "zl", "core", "x", "zh"))
    site = ("y", "zl", "core")
    ev = ("x", "zh")
    in_specs = (P(None, None, ev, site, None), P(None, None, None, None, site, None), P(), P())
    out_specs = P(None, None, None, site, ev)
    return jax.shard_map(local, mesh=fine, in_specs=in_specs, out_specs=out_specs, check_vma=False)
```

time: 591 us -> 153 us (0.26)
  waiting for transfers between devices: 427 us -> 20.6 us
  blocking collectives: 0 us -> 60 us
  matrix products: 56.9 us -> 0 us
  other arithmetic: 45.9 us -> 1.43 us
  Pallas kernels: 0 us -> 42.7 us
  local copies, waits for them, and re-layouts: 39.1 us -> 2.43 us
  starting transfers between devices: 3.36 us -> 25.7 us
  between operations: 14.8 us -> 0.15 us
    unnamed x3 -> x0, waiting for transfers between devices: 282 us -> none
    all_gather x1 -> x0, waiting for transfers between devices: 145 us -> none  [local(): lax.all_gather(eigvecs, 'ev', axis=2, tiled=True)]
    all_to_all x0 -> x2, blocking collectives: none -> 60 us  [the longest x1 39.1 us: local(): buf = lax.all_to_all(cut, ('x', 'zh'), 0, 0)]
    dot_general x5 -> x0, matrix products: 56.9 us -> none  [the longest x4 48 us: contract(): jnp.einsum('acrzs,dbcjzs->abdrj', weighted, right, precision=lax.Precisio...]
    pallas_call x0 -> x8, Pallas kernels: none -> 42.7 us  [call(): pl.pallas_call(kernel, out_shape=out_shape, in_specs=[pl.BlockSpec(memory...]
    ppermute x1 -> x21, starting transfers between devices: 3.32 us -> 25.7 us  [the longest x18 20.7 us: around(): return lax.ppermute(value, axis, [(i, (i + step) % 4) for i in range(4)])]
    ppermute x1 -> x21, waiting for transfers between devices: 0.01 us -> 20.6 us  [the longest x18 11 us: around(): return lax.ppermute(value, axis, [(i, (i + step) % 4) for i in range(4)])]
    sub x6 -> x0, other arithmetic: 18.9 us -> none  [the longest x2 18.8 us: contract(): left_real = left_vector[0] * cosine_value - left_vector[1] * sine_value]
  transfers between devices with their start and end apart: 3 -> 21, of which waited for: 2 -> 8; matrix products, arithmetic and copies ran while one was open for 12% -> 0% of each run, Pallas kernels for 0% -> 26%
where the time goes in v2:
time: 153 us
  blocking collectives  60 us (39%)
  Pallas kernels  42.7 us (28%)
  starting transfers between devices  25.7 us (17%)
  waiting for transfers between devices  20.6 us (13%)
  local copies, waits for them, and re-layouts  2.43 us (2%)
    pallas_call x8, Pallas kernels, call(): pl.pallas_call(kernel, out_shape=out_shape, in_specs=[pl.BlockSpec(memory...  42.7 us
    all_to_all x1, blocking collectives, local(): buf = lax.all_to_all(cut, ('x', 'zh'), 0, 0)  39.1 us
    all_to_all x1, blocking collectives, local(): parts = lax.all_to_all(packed, ('zl', 'zh', 'core'), 0, 0)  20.9 us
    ppermute x18, starting transfers between devices, around(): return lax.ppermute(value, axis, [(i, (i + step) % 4) for i in range(4)])  20.7 us
    ppermute x18, waiting for transfers between devices, around(): return lax.ppermute(value, axis, [(i, (i + step) % 4) for i in range(4)])  11 us
    ppermute x1, waiting for transfers between devices, local(): lax.ppermute(buf, ('y', 'zl', 'core'), [(i, (i - 1) % 32) for i in range(...  9.59 us
    ppermute x1, starting transfers between devices, local(): lax.ppermute(buf, ('y', 'zl', 'core'), [(i, (i - 1) % 32) for i in range(...  3.2 us
  transfers between devices with their start and end apart: 21, of which 8 were waited for; matrix products, arithmetic and copies ran while one was open for 0% of the time, Pallas kernels for 26%

profile of v2, /device:TPU:1, one launch (start us, length us, event | category | flops | bytes accessed | tf_op | source)
XLA Modules:
  0.0 153.0 jit_solution(8591735430731693073)
XLA Ops:
  0.0 0.0 copy-start.2
  0.0 1.5 copy.6
  1.5 0.0 copy-done.2
  1.5 1.4 reduce
  2.9 0.2 reshape.7.link_ref
  3.2 1.4 cut.1
  4.6 0.0 copy-start
  4.6 39.1 %all_to_all.10.buf_ref = f32[8,384,128]{2,1,0:T(8,128)S(1)} all-to-all(f32[8,384,128]{2,1,0:T(8,128)S(1)} %get-tuple-element.35), channel_id=1, replica_groups=mesh['y'=4,'zl'=4,'core'=2,'x'=4,'zh'=2] {'x','zh'}, dimensions={0} | all-to-all | bytes 3145728 | tf_op jit(solution)/shard_map/all_to_all | solution.py:371
  43.7 3.2 %collective-permute-start.7 = (f32[8,384,128]{2,1,0:T(8,128)S(1)}, f32[8,384,128]{2,1,0:T(8,128)S(1)}, u32[]{:S(2)}, u32[]{:S(2)}) collective-permute-start(f32[8,384,128]{2,1,0:T(8,128)S(1)} %all_to_all.10.buf_ref), channel_id=1, source_target_pairs={{0,248},{8,0},{16,8},{24,16},{32,24},{40,32},{48,40},{56,48},{64,5... | collective-permute-start | bytes 4718600 | tf_op jit(solution)/shard_map/ppermute | solution.py:372
  46.9 0.0 copy-done
  46.9 19.5 %contract_vx.1 = (f32[4,4,48,384]{3,2,1,0:T(8,128)S(1)}, f32[4,4,48,384]{3,2,1,0:T(8,128)S(1)}) custom-call(s32[4,3]{1,0:T(4,128)S(1)} %copy-done, f32[8,384,128]{2,1,0:T(8,128)S(1)} %all_to_all.10.buf_ref, f32[3,56,128]{2,1,0:T(8,128)S(1)} %get-tuple-element.36.link_ref), custom_call_target="tpu_custom_call" | custom-call | tf_op jit(solution)/shard_map/contract_vx/pallas_call | solution.py:351
  66.4 1.7 %collective-permute-start = (f32[4,4,48,384]{3,2,1,0:T(8,128)S(1)}, f32[4,4,48,384]{3,2,1,0:T(8,128)S(1)}, u32[]{:S(2)}, u32[]{:S(2)}) collective-permute-start(f32[4,4,48,384]{3,2,1,0:T(8,128)S(1)} %get-tuple-element.38), channel_id=1, source_target_pairs={{0,8},{8,0},{1,9},{9,1},{2,10},{10,2},{3,11},{11,3},{4,12},{12,4},... | collective-permute-start | bytes 3538952 | tf_op jit(solution)/shard_map/ppermute | solution.py:382
  68.1 9.6 %collective-permute-done.7.above_ref = f32[8,384,128]{2,1,0:T(8,128)S(1)} collective-permute-done((f32[8,384,128]{2,1,0:T(8,128)S(1)}, f32[8,384,128]{2,1,0:T(8,128)S(1)}, u32[]{:S(2)}, u32[]{:S(2)}) %collective-permute-start.7) | collective-permute-done | bytes 1572896 | tf_op jit(solution)/shard_map/ppermute | solution.py:372
  77.7 20.4 %contract_yz.1 = (f32[4,4,48,384]{3,2,1,0:T(8,128)S(1)}, f32[4,4,48,384]{3,2,1,0:T(8,128)S(1)}) custom-call(s32[4,3]{1,0:T(4,128)S(1)} %copy-done, f32[8,384,128]{2,1,0:T(8,128)S(1)} %all_to_all.10.buf_ref, f32[8,384,128]{2,1,0:T(8,128)S(1)} %collective-permute-done.7.above_ref, f32[3,56,128]{2,1,0:T(8,128)S(1)} %get-tuple-element.36.link_ref), custom_call_target="tpu_custom_call" | custom-call | tf_op jit(solution)/shard_map/contract_yz/pallas_call | solution.py:351
  98.1 0.1 collective-permute-start.8
  98.2 0.0 collective-permute-done.came_ref
  98.2 0.1 add.3
  98.4 1.4 collective-permute-start.1
  99.8 2.6 %collective-permute-start.2 = (f32[4,24,384]{2,1,0:T(8,128)S(1)}, f32[4,24,384]{2,1,0:T(8,128)S(1)}, u32[]{:S(2)}, u32[]{:S(2)}) collective-permute-start(f32[4,24,384]{2,1,0:T(8,128)S(1)} %get-tuple-element.41), channel_id=1, source_target_pairs={{0,128},{64,192},{128,0},{192,64},{1,129},{65,193},{129,1},{193,65... | collective-permute-start | bytes 442376 | tf_op jit(solution)/shard_map/ppermute | solution.py:363
  102.4 1.1 collective-permute-start.3
  103.4 0.0 collective-permute-start.4
  103.4 0.0 collective-permute-done.8.came_ref
  103.5 1.8 %collective-permute-start.5 = (f32[4,24,384]{2,1,0:T(8,128)S(1)}, f32[4,24,384]{2,1,0:T(8,128)S(1)}, u32[]{:S(2)}, u32[]{:S(2)}) collective-permute-start(f32[4,24,384]{2,1,0:T(8,128)S(1)} %get-tuple-element.45), channel_id=1, source_target_pairs={{0,4},{2,6},{4,0},{6,2},{1,5},{3,7},{5,1},{7,3},{8,12},{10,14},{12... | collective-permute-start | bytes 442376 | tf_op jit(solution)/shard_map/ppermute | solution.py:363
  105.2 0.1 add.4
  105.3 0.0 collective-permute-done.1.refs_1_
  105.3 1.2 collective-permute-start.6
  106.6 2.4 %collective-permute-done.2.refs_2_ = f32[4,24,384]{2,1,0:T(8,128)S(1)} collective-permute-done((f32[4,24,384]{2,1,0:T(8,128)S(1)}, f32[4,24,384]{2,1,0:T(8,128)S(1)}, u32[]{:S(2)}, u32[]{:S(2)}) %collective-permute-start.2) | collective-permute-done | bytes 147488 | tf_op jit(solution)/shard_map/ppermute | solution.py:363
  109.0 0.6 collective-permute-start.10
  109.6 0.0 collective-permute-done.3.refs_3_
  109.6 1.5 collective-permute-start.11
  111.1 0.0 collective-permute-done.4.refs_5_
  111.1 0.0 collective-permute-start.12
  111.1 0.0 collective-permute-done.5.refs_6_
  111.1 1.8 %collective-permute-start.13 = (f32[4,24,384]{2,1,0:T(8,128)S(1)}, f32[4,24,384]{2,1,0:T(8,128)S(1)}, u32[]{:S(2)}, u32[]{:S(2)}) collective-permute-start(f32[4,24,384]{2,1,0:T(8,128)S(1)} %get-tuple-element.55), channel_id=1, source_target_pairs={{0,4},{2,6},{4,0},{6,2},{1,5},{3,7},{5,1},{7,3},{8,12},{10,14},{12... | collective-permute-start | bytes 442376 | tf_op jit(solution)/shard_map/ppermute | solution.py:363
  112.9 0.0 collective-permute-done.6.refs_7_
  112.9 3.0 %collective-permute-start.14 = (f32[4,24,384]{2,1,0:T(8,128)S(1)}, f32[4,24,384]{2,1,0:T(8,128)S(1)}, u32[]{:S(2)}, u32[]{:S(2)}) collective-permute-start(f32[4,24,384]{2,1,0:T(8,128)S(1)} %get-tuple-element.56), channel_id=1, source_target_pairs={{0,6},{2,0},{4,2},{6,4},{1,7},{3,1},{5,3},{7,5},{8,14},{10,8},{12,... | collective-permute-start | bytes 442376 | tf_op jit(solution)/shard_map/ppermute | solution.py:363
  115.9 0.0 collective-permute-done.10.refs_10_
  115.9 0.4 collective-permute-start.9
  116.3 0.0 collective-permute-done.11.refs_11_
  116.3 1.6 %collective-permute-done.12.refs_13_ = f32[4,24,384]{2,1,0:T(8,128)S(1)} collective-permute-done((f32[4,24,384]{2,1,0:T(8,128)S(1)}, f32[4,24,384]{2,1,0:T(8,128)S(1)}, u32[]{:S(2)}, u32[]{:S(2)}) %collective-permute-start.12) | collective-permute-done | bytes 147488 | tf_op jit(solution)/shard_map/ppermute | solution.py:363
  117.9 0.0 collective-permute-done.13.refs_14_
  117.9 0.9 collective-permute-done.14.refs_15_
  118.8 2.6 %collective-permute-done.9.refs_9_ = f32[4,24,384]{2,1,0:T(8,128)S(1)} collective-permute-done((f32[4,24,384]{2,1,0:T(8,128)S(1)}, f32[4,24,384]{2,1,0:T(8,128)S(1)}, u32[]{:S(2)}, u32[]{:S(2)}) %collective-permute-start.9) | collective-permute-done | bytes 147488 | tf_op jit(solution)/shard_map/ppermute | solution.py:363
  121.4 0.1 sum.1
  121.5 0.0 copy-start.1
  121.5 0.1 collective-permute-start.15
  121.6 0.9 collective-permute-start.16
  122.5 1.8 %collective-permute-start.17 = (f32[2,24,384]{2,1,0:T(8,128)S(1)}, f32[2,24,384]{2,1,0:T(8,128)S(1)}, u32[]{:S(2)}, u32[]{:S(2)}) collective-permute-start(f32[2,24,384]{2,1,0:T(8,128)S(1)} %get-tuple-element.60), channel_id=1, source_target_pairs={{0,6},{2,0},{4,2},{6,4},{1,7},{3,1},{5,3},{7,5},{8,14},{10,8},{12,... | collective-permute-start | bytes 221192 | tf_op jit(solution)/shard_map/ppermute | solution.py:363
  124.3 0.0 collective-permute-start.18
  124.3 2.6 %collective-permute-start.19 = (f32[2,24,384]{2,1,0:T(8,128)S(1)}, f32[2,24,384]{2,1,0:T(8,128)S(1)}, u32[]{:S(2)}, u32[]{:S(2)}) collective-permute-start(f32[2,24,384]{2,1,0:T(8,128)S(1)} %get-tuple-element.63), channel_id=1, source_target_pairs={{0,128},{64,192},{128,0},{192,64},{1,129},{65,193},{129,1},{193,65... | collective-permute-start | bytes 221192 | tf_op jit(solution)/shard_map/ppermute | solution.py:363
  126.8 0.0 collective-permute-done.15.refs_1_
  126.8 0.1 collective-permute-start.20
  126.9 0.0 collective-permute-done.16.refs_2_
  127.0 0.4 collective-permute-done.17.refs_3_
  127.4 2.4 %collective-permute-done.18.refs_5_ = f32[2,24,384]{2,1,0:T(8,128)S(1)} collective-permute-done((f32[2,24,384]{2,1,0:T(8,128)S(1)}, f32[2,24,384]{2,1,0:T(8,128)S(1)}, u32[]{:S(2)}, u32[]{:S(2)}) %collective-permute-start.18) | collective-permute-done | bytes 73760 | tf_op jit(solution)/shard_map/ppermute | solution.py:363
  129.8 0.0 collective-permute-done.19.refs_6_
  129.8 0.6 collective-permute-done.20.refs_7_
  130.3 0.2 gather.1
  130.6 20.9 %all_to_all.11.part_ref = f32[16,8,384]{2,1,0:T(8,128)S(1)} all-to-all(f32[16,8,384]{2,1,0:T(8,128)S(1)} %gather.1), channel_id=1, replica_groups=mesh['y'=4,'zl'=4,'core'=2,'x'=4,'zh'=2] {'zl','zh','core'}, dimensions={0} | all-to-all | bytes 393216 | tf_op jit(solution)/shard_map/all_to_all | solution.py:390
  151.5 0.0 copy-done.1
  151.5 0.8 last.1
  152.3 0.7 copy.5
Async XLA Ops:
  0.0 1.5 copy-start.2
  4.6 42.3 %copy-start = (s32[4,3]{1,0:T(4,128)S(1)}, s32[4,3]{1,0:T(4,128)}, u32[]{:S(2)}) copy-start(s32[4,3]{1,0:T(4,128)} %mom_ref.3) | copy-start | bytes 148
  43.7 34.0 %collective-permute-start.7 = (f32[8,384,128]{2,1,0:T(8,128)S(1)}, f32[8,384,128]{2,1,0:T(8,128)S(1)}, u32[]{:S(2)}, u32[]{:S(2)}) collective-permute-start(f32[8,384,128]{2,1,0:T(8,128)S(1)} %all_to_all.10.buf_ref), channel_id=1, source_target_pairs={{0,248},{8,0},{16,8},{24,16},{32,24},{40,32},{48,40},{56,48},{64,5... | collective-permute-start | bytes 4718600 | tf_op jit(solution)/shard_map/ppermute | solution.py:372
  66.4 31.8 %collective-permute-start = (f32[4,4,48,384]{3,2,1,0:T(8,128)S(1)}, f32[4,4,48,384]{3,2,1,0:T(8,128)S(1)}, u32[]{:S(2)}, u32[]{:S(2)}) collective-permute-start(f32[4,4,48,384]{3,2,1,0:T(8,128)S(1)} %get-tuple-element.38), channel_id=1, source_target_pairs={{0,8},{8,0},{1,9},{9,1},{2,10},{10,2},{3,11},{11,3},{4,12},{12,4},... | collective-permute-start | bytes 3538952 | tf_op jit(solution)/shard_map/ppermute | solution.py:382
  98.1 5.3 %collective-permute-start.8 = (f32[4,4,48,384]{3,2,1,0:T(8,128)S(1)}, f32[4,4,48,384]{3,2,1,0:T(8,128)S(1)}, u32[]{:S(2)}, u32[]{:S(2)}) collective-permute-start(f32[4,4,48,384]{3,2,1,0:T(8,128)S(1)} %get-tuple-element.48), channel_id=1, source_target_pairs={{0,8},{8,0},{1,9},{9,1},{2,10},{10,2},{3,11},{11,3},{4,12},{12,4},... | collective-permute-start | bytes 3538952 | tf_op jit(solution)/shard_map/ppermute | solution.py:382
  98.4 7.0 %collective-permute-start.1 = (f32[4,24,384]{2,1,0:T(8,128)S(1)}, f32[4,24,384]{2,1,0:T(8,128)S(1)}, u32[]{:S(2)}, u32[]{:S(2)}) collective-permute-start(f32[4,24,384]{2,1,0:T(8,128)S(1)} %get-tuple-element.40), channel_id=1, source_target_pairs={{0,64},{64,128},{128,192},{192,0},{1,65},{65,129},{129,193},{193,1... | collective-permute-start | bytes 442376 | tf_op jit(solution)/shard_map/ppermute | solution.py:363
  99.8 9.3 %collective-permute-start.2 = (f32[4,24,384]{2,1,0:T(8,128)S(1)}, f32[4,24,384]{2,1,0:T(8,128)S(1)}, u32[]{:S(2)}, u32[]{:S(2)}) collective-permute-start(f32[4,24,384]{2,1,0:T(8,128)S(1)} %get-tuple-element.41), channel_id=1, source_target_pairs={{0,128},{64,192},{128,0},{192,64},{1,129},{65,193},{129,1},{193,65... | collective-permute-start | bytes 442376 | tf_op jit(solution)/shard_map/ppermute | solution.py:363
  102.4 7.3 %collective-permute-start.3 = (f32[4,24,384]{2,1,0:T(8,128)S(1)}, f32[4,24,384]{2,1,0:T(8,128)S(1)}, u32[]{:S(2)}, u32[]{:S(2)}) collective-permute-start(f32[4,24,384]{2,1,0:T(8,128)S(1)} %get-tuple-element.42), channel_id=1, source_target_pairs={{0,192},{64,0},{128,64},{192,128},{1,193},{65,1},{129,65},{193,129... | collective-permute-start | bytes 442376 | tf_op jit(solution)/shard_map/ppermute | solution.py:363
  103.4 7.7 %collective-permute-start.4 = (f32[4,24,384]{2,1,0:T(8,128)S(1)}, f32[4,24,384]{2,1,0:T(8,128)S(1)}, u32[]{:S(2)}, u32[]{:S(2)}) collective-permute-start(f32[4,24,384]{2,1,0:T(8,128)S(1)} %get-tuple-element.44), channel_id=1, source_target_pairs={{0,2},{2,4},{4,6},{6,0},{1,3},{3,5},{5,7},{7,1},{8,10},{10,12},{12... | collective-permute-start | bytes 442376 | tf_op jit(solution)/shard_map/ppermute | solution.py:363
  103.5 7.7 %collective-permute-start.5 = (f32[4,24,384]{2,1,0:T(8,128)S(1)}, f32[4,24,384]{2,1,0:T(8,128)S(1)}, u32[]{:S(2)}, u32[]{:S(2)}) collective-permute-start(f32[4,24,384]{2,1,0:T(8,128)S(1)} %get-tuple-element.45), channel_id=1, source_target_pairs={{0,4},{2,6},{4,0},{6,2},{1,5},{3,7},{5,1},{7,3},{8,12},{10,14},{12... | collective-permute-start | bytes 442376 | tf_op jit(solution)/shard_map/ppermute | solution.py:363
  105.3 7.6 %collective-permute-start.6 = (f32[4,24,384]{2,1,0:T(8,128)S(1)}, f32[4,24,384]{2,1,0:T(8,128)S(1)}, u32[]{:S(2)}, u32[]{:S(2)}) collective-permute-start(f32[4,24,384]{2,1,0:T(8,128)S(1)} %get-tuple-element.46), channel_id=1, source_target_pairs={{0,6},{2,0},{4,2},{6,4},{1,7},{3,1},{5,3},{7,5},{8,14},{10,8},{12,... | collective-permute-start | bytes 442376 | tf_op jit(solution)/shard_map/ppermute | solution.py:363
  109.0 6.9 %collective-permute-start.10 = (f32[4,24,384]{2,1,0:T(8,128)S(1)}, f32[4,24,384]{2,1,0:T(8,128)S(1)}, u32[]{:S(2)}, u32[]{:S(2)}) collective-permute-start(f32[4,24,384]{2,1,0:T(8,128)S(1)} %get-tuple-element.51), channel_id=1, source_target_pairs={{0,128},{64,192},{128,0},{192,64},{1,129},{65,193},{129,1},{193,65... | collective-permute-start | bytes 442376 | tf_op jit(solution)/shard_map/ppermute | solution.py:363
  109.6 6.6 %collective-permute-start.11 = (f32[4,24,384]{2,1,0:T(8,128)S(1)}, f32[4,24,384]{2,1,0:T(8,128)S(1)}, u32[]{:S(2)}, u32[]{:S(2)}) collective-permute-start(f32[4,24,384]{2,1,0:T(8,128)S(1)} %get-tuple-element.52), channel_id=1, source_target_pairs={{0,192},{64,0},{128,64},{192,128},{1,193},{65,1},{129,65},{193,129... | collective-permute-start | bytes 442376 | tf_op jit(solution)/shard_map/ppermute | solution.py:363
  111.1 6.8 %collective-permute-start.12 = (f32[4,24,384]{2,1,0:T(8,128)S(1)}, f32[4,24,384]{2,1,0:T(8,128)S(1)}, u32[]{:S(2)}, u32[]{:S(2)}) collective-permute-start(f32[4,24,384]{2,1,0:T(8,128)S(1)} %get-tuple-element.54), channel_id=1, source_target_pairs={{0,2},{2,4},{4,6},{6,0},{1,3},{3,5},{5,7},{7,1},{8,10},{10,12},{12... | collective-permute-start | bytes 442376 | tf_op jit(solution)/shard_map/ppermute | solution.py:363
  111.1 6.8 %collective-permute-start.13 = (f32[4,24,384]{2,1,0:T(8,128)S(1)}, f32[4,24,384]{2,1,0:T(8,128)S(1)}, u32[]{:S(2)}, u32[]{:S(2)}) collective-permute-start(f32[4,24,384]{2,1,0:T(8,128)S(1)} %get-tuple-element.55), channel_id=1, source_target_pairs={{0,4},{2,6},{4,0},{6,2},{1,5},{3,7},{5,1},{7,3},{8,12},{10,14},{12... | collective-permute-start | bytes 442376 | tf_op jit(solution)/shard_map/ppermute | solution.py:363
  112.9 5.9 %collective-permute-start.14 = (f32[4,24,384]{2,1,0:T(8,128)S(1)}, f32[4,24,384]{2,1,0:T(8,128)S(1)}, u32[]{:S(2)}, u32[]{:S(2)}) collective-permute-start(f32[4,24,384]{2,1,0:T(8,128)S(1)} %get-tuple-element.56), channel_id=1, source_target_pairs={{0,6},{2,0},{4,2},{6,4},{1,7},{3,1},{5,3},{7,5},{8,14},{10,8},{12,... | collective-permute-start | bytes 442376 | tf_op jit(solution)/shard_map/ppermute | solution.py:363
  115.9 5.5 %collective-permute-start.9 = (f32[4,24,384]{2,1,0:T(8,128)S(1)}, f32[4,24,384]{2,1,0:T(8,128)S(1)}, u32[]{:S(2)}, u32[]{:S(2)}) collective-permute-start(f32[4,24,384]{2,1,0:T(8,128)S(1)} %get-tuple-element.50), channel_id=1, source_target_pairs={{0,64},{64,128},{128,192},{192,0},{1,65},{65,129},{129,193},{193,1... | collective-permute-start | bytes 442376 | tf_op jit(solution)/shard_map/ppermute | solution.py:363
  121.5 30.0 %copy-start.1 = (s32[3]{0:T(128)S(1)}, s32[3]{0:T(128)}, u32[]{:S(2)}) copy-start(s32[3]{0:T(128)} %direction_ref.1) | copy-start | bytes 40
  121.5 5.3 %collective-permute-start.15 = (f32[2,24,384]{2,1,0:T(8,128)S(1)}, f32[2,24,384]{2,1,0:T(8,128)S(1)}, u32[]{:S(2)}, u32[]{:S(2)}) collective-permute-start(f32[2,24,384]{2,1,0:T(8,128)S(1)} %get-tuple-element.58), channel_id=1, source_target_pairs={{0,2},{2,4},{4,6},{6,0},{1,3},{3,5},{5,7},{7,1},{8,10},{10,12},{12... | collective-permute-start | bytes 221192 | tf_op jit(solution)/shard_map/ppermute | solution.py:363
  121.6 5.4 %collective-permute-start.16 = (f32[2,24,384]{2,1,0:T(8,128)S(1)}, f32[2,24,384]{2,1,0:T(8,128)S(1)}, u32[]{:S(2)}, u32[]{:S(2)}) collective-permute-start(f32[2,24,384]{2,1,0:T(8,128)S(1)} %get-tuple-element.59), channel_id=1, source_target_pairs={{0,4},{2,6},{4,0},{6,2},{1,5},{3,7},{5,1},{7,3},{8,12},{10,14},{12... | collective-permute-start | bytes 221192 | tf_op jit(solution)/shard_map/ppermute | solution.py:363
  122.5 4.9 %collective-permute-start.17 = (f32[2,24,384]{2,1,0:T(8,128)S(1)}, f32[2,24,384]{2,1,0:T(8,128)S(1)}, u32[]{:S(2)}, u32[]{:S(2)}) collective-permute-start(f32[2,24,384]{2,1,0:T(8,128)S(1)} %get-tuple-element.60), channel_id=1, source_target_pairs={{0,6},{2,0},{4,2},{6,4},{1,7},{3,1},{5,3},{7,5},{8,14},{10,8},{12,... | collective-permute-start | bytes 221192 | tf_op jit(solution)/shard_map/ppermute | solution.py:363
  124.3 5.5 %collective-permute-start.18 = (f32[2,24,384]{2,1,0:T(8,128)S(1)}, f32[2,24,384]{2,1,0:T(8,128)S(1)}, u32[]{:S(2)}, u32[]{:S(2)}) collective-permute-start(f32[2,24,384]{2,1,0:T(8,128)S(1)} %get-tuple-element.62), channel_id=1, source_target_pairs={{0,64},{64,128},{128,192},{192,0},{1,65},{65,129},{129,193},{193,1... | collective-permute-start | bytes 221192 | tf_op jit(solution)/shard_map/ppermute | solution.py:363
  124.3 5.5 %collective-permute-start.19 = (f32[2,24,384]{2,1,0:T(8,128)S(1)}, f32[2,24,384]{2,1,0:T(8,128)S(1)}, u32[]{:S(2)}, u32[]{:S(2)}) collective-permute-start(f32[2,24,384]{2,1,0:T(8,128)S(1)} %get-tuple-element.63), channel_id=1, source_target_pairs={{0,128},{64,192},{128,0},{192,64},{1,129},{65,193},{129,1},{193,65... | collective-permute-start | bytes 221192 | tf_op jit(solution)/shard_map/ppermute | solution.py:363
  126.8 3.5 %collective-permute-start.20 = (f32[2,24,384]{2,1,0:T(8,128)S(1)}, f32[2,24,384]{2,1,0:T(8,128)S(1)}, u32[]{:S(2)}, u32[]{:S(2)}) collective-permute-start(f32[2,24,384]{2,1,0:T(8,128)S(1)} %get-tuple-element.64), channel_id=1, source_target_pairs={{0,192},{64,0},{128,64},{192,128},{1,193},{65,1},{129,65},{193,129... | collective-permute-start | bytes 221192 | tf_op jit(solution)/shard_map/ppermute | solution.py:363

commit v3 on v2

--- a/solution.py
+++ b/solution.py
@@ -207,65 +207,65 @@
 
     lax.fori_loop(0, 4, make_fields, 0)
 
-    lane = lanes(8)
-    sites = [lane, lane + 128, 256 + lax.rem(lane, 32)]
-    lines = []
-    for site in sites:
-        line = jnp.zeros((8, 128), jnp.int32)
-        for step in range(1, 6):
-            line = line + (site >= step * LY).astype(jnp.int32)
-        lines.append(line)
+    row = lax.broadcasted_iota(jnp.int32, (16, 128), 0)
+    lane = lanes(16)
+    site = jnp.where(row < 4, lane, jnp.where(row < 8, lane + 128, 256 + (lane & 31)))
+    line = jnp.zeros((16, 128), jnp.int32)
+    for step in range(1, 6):
+        line = line + (site >= step * LY).astype(jnp.int32)
+    momentum = []
+    for axis in range(3):
+        value = jnp.zeros((16, 128), jnp.int32)
+        for at in range(12):
+            p = (2 * (1 - core) if at % 4 < 2 else 2 * core) + at % 2
+            value = jnp.where(row == at, mom_ref[p, axis], value)
+        momentum.append(value)
+    fx = wrapped(momentum[0] * (line + part * 6), 48).astype(jnp.float32) / 48
+    fy = wrapped(momentum[1] * (site - line * LY), 48).astype(jnp.float32) / 48
+    fz = wrapped(momentum[2] * zpos, 32).astype(jnp.float32) / 32
+    theta = (2.0 * math.pi) * (fx + fy + fz)
+    used = (row < 8) | (lane < 96)
+    cosines = jnp.where(used, jnp.cos(theta), 0.0)
+    sines = jnp.where(used, jnp.sin(theta), 0.0)
+
+    def make_left(xs, carry):
+        top = pl.multiple_of(xs * 48, 16)
+        real, imag = tiles_of(buf_ref, xs)
+        for index in range(4):
+            left_real = []
+            left_imag = []
+            for at in range(7):
+                row = 4 * (at // 3) + index
+                cosv = cosines[row:row + 1]
+                sinv = sines[row:row + 1]
+                left_real.append(real[at] * cosv - imag[at] * sinv)
+                left_imag.append(-(real[at] * sinv + imag[at] * cosv))
+            put_tiles(lhi.at[index], llo.at[index], top, left_real)
+            put_tiles(lhi.at[index], llo.at[index], top + 192, left_imag)
+        return carry
+
+    lax.fori_loop(0, 4, make_left, 0)
 
     def times(left, right):
         return lax.dot_general(
             left, right, (((1,), (1,)), ((), ())), preferred_element_type=jnp.float32
         )
 
-    for group, out_ref in ((0, away_ref), (1, stay_ref)):
-        for index in range(2):
-            p = (2 * (1 - core) if group == 0 else 2 * core) + index
-            phase = []
-            for at in range(3):
-                xpos = lines[at] + part * 6
-                ypos = sites[at] - lines[at] * LY
-                fx = wrapped(mom_ref[p, 0] * xpos, 48).astype(jnp.float32) / 48
-                fy = wrapped(mom_ref[p, 1] * ypos, 48).astype(jnp.float32) / 48
-                fz = wrapped(jnp.full((8, 128), mom_ref[p, 2] * zpos, jnp.int32), 32)
-                theta = (2.0 * math.pi) * (fx + fy + fz.astype(jnp.float32) / 32)
-                cosv = jnp.cos(theta)
-                sinv = jnp.sin(theta)
-                if at == 2:
-                    cosv = jnp.where(lane < 96, cosv, 0.0)
-                    sinv = jnp.where(lane < 96, sinv, 0.0)
-                phase.append((cosv[:1], sinv[:1]))
-
-            def make_left(xs, carry, phase=phase):
-                top = pl.multiple_of(xs * 48, 16)
-                real, imag = tiles_of(buf_ref, xs)
-                left_real = []
-                left_imag = []
-                for at in range(7):
-                    cosv, sinv = phase[at // 3]
-                    left_real.append(real[at] * cosv - imag[at] * sinv)
-                    left_imag.append(-(real[at] * sinv + imag[at] * cosv))
-                put_tiles(lhi, llo, top, left_real)
-                put_tiles(lhi, llo, top + 192, left_imag)
-                return carry
-
-            lax.fori_loop(0, 4, make_left, 0)
-            left_high = lhi[...]
-            left_low = llo[...]
-            total = times(left_high, whi[...]) + times(left_high, wlo[...]) + times(left_low, whi[...])
-            product = (
-                total[:192, :384] - total[192:, 384:],
-                total[192:, :384] + total[:192, 384:],
-            )
-            for reim in range(2):
-                column = (2 * index + reim) * 96
-                for xs in range(4):
-                    value = product[reim][:, xs * 96:(xs + 1) * 96]
-                    for ys in range(4):
-                        out_ref[xs, ys, :, column:column + 96] = value[ys * 48:(ys + 1) * 48]
+    for index in range(4):
+        out_ref = (away_ref, stay_ref)[index // 2]
+        total = (
+            times(lhi[index], whi[...]) + times(lhi[index], wlo[...]) + times(llo[index], whi[...])
+        )
+        product = (
+            total[:192, :384] - total[192:, 384:],
+            total[192:, :384] + total[:192, 384:],
+        )
+        for reim in range(2):
+            column = (2 * (index % 2) + reim) * 96
+            for xs in range(4):
+                value = product[reim][:, xs * 96:(xs + 1) * 96]
+                for ys in range(4):
+                    out_ref[xs, ys, :, column:column + 96] = value[ys * 48:(ys + 1) * 48]
 
 
 def first_kernel(mom_ref, buf_ref, link_ref, away_ref, stay_ref, *scratch):
@@ -370,7 +370,7 @@
     )
     buf = lax.all_to_all(cut, ("x", "zh"), 0, 0)
     above = lax.ppermute(buf, ("y", "zl", "core"), [(i, (i - 1) % 32) for i in range(32)])
-    scratch = [pltpu.VMEM((768, DEPTH), jnp.bfloat16)] * 2 + [pltpu.VMEM((384, DEPTH), jnp.bfloat16)] * 2
+    scratch = [pltpu.VMEM((768, DEPTH), jnp.bfloat16)] * 2 + [pltpu.VMEM((4, 384, DEPTH), jnp.bfloat16)] * 2
     sums = []
     for chunk in range(2):
         away, stay = call(

time: 153 us -> 143 us (0.935)
  Pallas kernels: 42.7 us -> 26.9 us
  waiting for transfers between devices: 20.6 us -> 28.5 us
  blocking collectives: 60 us -> 58.1 us
    pallas_call x8, Pallas kernels: 42.7 us -> 26.9 us  [call(): pl.pallas_call(kernel, out_shape=out_shape, in_specs=[pl.BlockSpec(memory...]
    ppermute x1, waiting for transfers between devices: 9.59 us -> 17.6 us  [local(): lax.ppermute(buf, ('y', 'zl', 'core'), [(i, (i - 1) % 32) for i in range(...]
    all_to_all x1, blocking collectives: 20.9 us -> 19 us  [local(): parts = lax.all_to_all(packed, ('zl', 'zh', 'core'), 0, 0)]
  transfers between devices with their start and end apart: 21 -> 21, of which waited for: 8 -> 8; matrix products, arithmetic and copies ran while one was open for 0% -> 0% of each run, Pallas kernels for 26% -> 17%
where the time goes in v3:
time: 143 us
  blocking collectives  58.1 us (41%)
  waiting for transfers between devices  28.5 us (20%)
  Pallas kernels  26.9 us (19%)
  starting transfers between devices  25.6 us (18%)
  local copies, waits for them, and re-layouts  2.43 us (2%)
  other arithmetic  1.43 us (1%)
    all_to_all x1, blocking collectives, local(): buf = lax.all_to_all(cut, ('x', 'zh'), 0, 0)  39.1 us
    pallas_call x8, Pallas kernels, call(): pl.pallas_call(kernel, out_shape=out_shape, in_specs=[pl.BlockSpec(memory...  26.9 us
    ppermute x18, starting transfers between devices, around(): return lax.ppermute(value, axis, [(i, (i + step) % 4) for i in range(4)])  20.7 us
    all_to_all x1, blocking collectives, local(): parts = lax.all_to_all(packed, ('zl', 'zh', 'core'), 0, 0)  19 us
    ppermute x1, waiting for transfers between devices, local(): lax.ppermute(buf, ('y', 'zl', 'core'), [(i, (i - 1) % 32) for i in range(...  17.6 us
    ppermute x18, waiting for transfers between devices, around(): return lax.ppermute(value, axis, [(i, (i + step) % 4) for i in range(4)])  11 us
    ppermute x1, starting transfers between devices, local(): lax.ppermute(buf, ('y', 'zl', 'core'), [(i, (i - 1) % 32) for i in range(...  3.2 us
  transfers between devices with their start and end apart: 21, of which 8 were waited for; matrix products, arithmetic and copies ran while one was open for 0% of the time, Pallas kernels for 17%

profile of v3, /device:TPU:1, one launch (start us, length us, event | category | flops | bytes accessed | tf_op | source)
XLA Modules:
  0.0 143.2 jit_solution(1063621938168781517)
XLA Ops:
  0.0 0.0 copy-start.2
  0.0 1.5 %copy.6 = f32[2,3,24,1,2304]{4,2,3,1,0:T(8,128)S(1)} copy(f32[2,3,24,1,2304]{4,3,2,1,0:T(1,128)} %param.4) | data formatting | bytes 2654208
  1.5 0.0 copy-done.2
  1.5 1.4 reduce
  2.9 0.2 reshape.7.link_ref
  3.2 1.4 %cut.1 = (f32[8,384,128]{2,1,0:T(8,128)S(1)}, f32[3,56,128]{2,1,0:T(8,128)S(1)}) custom-call(f32[144,2304]{1,0:T(8,128)S(1)} %bitcast.1, f32[54,2304]{1,0:T(8,128)S(1)} %reshape.7.link_ref), custom_call_target="tpu_custom_call" | custom-call | tf_op jit(solution)/shard_map/cut/pallas_call | solution.py:351
  4.6 0.0 copy-start
  4.6 39.1 %all_to_all.10.buf_ref = f32[8,384,128]{2,1,0:T(8,128)S(1)} all-to-all(f32[8,384,128]{2,1,0:T(8,128)S(1)} %get-tuple-element.35), channel_id=1, replica_groups=mesh['y'=4,'zl'=4,'core'=2,'x'=4,'zh'=2] {'x','zh'}, dimensions={0} | all-to-all | bytes 3145728 | tf_op jit(solution)/shard_map/all_to_all | solution.py:371
  43.7 3.2 %collective-permute-start.7 = (f32[8,384,128]{2,1,0:T(8,128)S(1)}, f32[8,384,128]{2,1,0:T(8,128)S(1)}, u32[]{:S(2)}, u32[]{:S(2)}) collective-permute-start(f32[8,384,128]{2,1,0:T(8,128)S(1)} %all_to_all.10.buf_ref), channel_id=1, source_target_pairs={{0,248},{8,0},{16,8},{24,16},{32,24},{40,32},{48,40},{56,48},{64,5... | collective-permute-start | bytes 4718600 | tf_op jit(solution)/shard_map/ppermute | solution.py:372
  46.9 0.0 copy-done
  46.9 11.6 %contract_vx.1 = (f32[4,4,48,384]{3,2,1,0:T(8,128)S(1)}, f32[4,4,48,384]{3,2,1,0:T(8,128)S(1)}) custom-call(s32[4,3]{1,0:T(4,128)S(1)} %copy-done, f32[8,384,128]{2,1,0:T(8,128)S(1)} %all_to_all.10.buf_ref, f32[3,56,128]{2,1,0:T(8,128)S(1)} %get-tuple-element.36.link_ref), custom_call_target="tpu_custom_call" | custom-call | tf_op jit(solution)/shard_map/contract_vx/pallas_call | solution.py:351
  58.5 1.6 %collective-permute-start = (f32[4,4,48,384]{3,2,1,0:T(8,128)S(1)}, f32[4,4,48,384]{3,2,1,0:T(8,128)S(1)}, u32[]{:S(2)}, u32[]{:S(2)}) collective-permute-start(f32[4,4,48,384]{3,2,1,0:T(8,128)S(1)} %get-tuple-element.38), channel_id=1, source_target_pairs={{0,8},{8,0},{1,9},{9,1},{2,10},{10,2},{3,11},{11,3},{4,12},{12,4},... | collective-permute-start | bytes 3538952 | tf_op jit(solution)/shard_map/ppermute | solution.py:382
  60.1 17.6 %collective-permute-done.7.above_ref = f32[8,384,128]{2,1,0:T(8,128)S(1)} collective-permute-done((f32[8,384,128]{2,1,0:T(8,128)S(1)}, f32[8,384,128]{2,1,0:T(8,128)S(1)}, u32[]{:S(2)}, u32[]{:S(2)}) %collective-permute-start.7) | collective-permute-done | bytes 1572896 | tf_op jit(solution)/shard_map/ppermute | solution.py:372
  77.7 12.5 %contract_yz.1 = (f32[4,4,48,384]{3,2,1,0:T(8,128)S(1)}, f32[4,4,48,384]{3,2,1,0:T(8,128)S(1)}) custom-call(s32[4,3]{1,0:T(4,128)S(1)} %copy-done, f32[8,384,128]{2,1,0:T(8,128)S(1)} %all_to_all.10.buf_ref, f32[8,384,128]{2,1,0:T(8,128)S(1)} %collective-permute-done.7.above_ref, f32[3,56,128]{2,1,0:T(8,128)S(1)} %get-tuple-element.36.link_ref), custom_call_target="tpu_custom_call" | custom-call | tf_op jit(solution)/shard_map/contract_yz/pallas_call | solution.py:351
  90.2 0.1 collective-permute-start.8
  90.3 0.0 collective-permute-done.came_ref
  90.3 0.1 add.3
  90.5 1.4 collective-permute-start.1
  91.8 2.6 %collective-permute-start.2 = (f32[4,24,384]{2,1,0:T(8,128)S(1)}, f32[4,24,384]{2,1,0:T(8,128)S(1)}, u32[]{:S(2)}, u32[]{:S(2)}) collective-permute-start(f32[4,24,384]{2,1,0:T(8,128)S(1)} %get-tuple-element.41), channel_id=1, source_target_pairs={{0,128},{64,192},{128,0},{192,64},{1,129},{65,193},{129,1},{193,65... | collective-permute-start | bytes 442376 | tf_op jit(solution)/shard_map/ppermute | solution.py:363
  94.5 1.1 collective-permute-start.3
  95.5 0.0 collective-permute-start.4
  95.5 0.0 collective-permute-done.8.came_ref
  95.5 1.8 %collective-permute-start.5 = (f32[4,24,384]{2,1,0:T(8,128)S(1)}, f32[4,24,384]{2,1,0:T(8,128)S(1)}, u32[]{:S(2)}, u32[]{:S(2)}) collective-permute-start(f32[4,24,384]{2,1,0:T(8,128)S(1)} %get-tuple-element.45), channel_id=1, source_target_pairs={{0,4},{2,6},{4,0},{6,2},{1,5},{3,7},{5,1},{7,3},{8,12},{10,14},{12... | collective-permute-start | bytes 442376 | tf_op jit(solution)/shard_map/ppermute | solution.py:363
  97.3 0.1 add.4
  97.4 0.0 collective-permute-done.1.refs_1_
  97.4 1.2 collective-permute-start.6
  98.7 2.5 %collective-permute-done.2.refs_2_ = f32[4,24,384]{2,1,0:T(8,128)S(1)} collective-permute-done((f32[4,24,384]{2,1,0:T(8,128)S(1)}, f32[4,24,384]{2,1,0:T(8,128)S(1)}, u32[]{:S(2)}, u32[]{:S(2)}) %collective-permute-start.2) | collective-permute-done | bytes 147488 | tf_op jit(solution)/shard_map/ppermute | solution.py:363
  101.1 0.6 collective-permute-start.10
  101.7 0.0 collective-permute-done.3.refs_3_
  101.7 1.5 %collective-permute-start.11 = (f32[4,24,384]{2,1,0:T(8,128)S(1)}, f32[4,24,384]{2,1,0:T(8,128)S(1)}, u32[]{:S(2)}, u32[]{:S(2)}) collective-permute-start(f32[4,24,384]{2,1,0:T(8,128)S(1)} %get-tuple-element.52), channel_id=1, source_target_pairs={{0,192},{64,0},{128,64},{192,128},{1,193},{65,1},{129,65},{193,129... | collective-permute-start | bytes 442376 | tf_op jit(solution)/shard_map/ppermute | solution.py:363
  103.2 0.0 collective-permute-done.4.refs_5_
  103.2 0.0 collective-permute-start.12
  103.2 0.0 collective-permute-done.5.refs_6_
  103.2 1.8 %collective-permute-start.13 = (f32[4,24,384]{2,1,0:T(8,128)S(1)}, f32[4,24,384]{2,1,0:T(8,128)S(1)}, u32[]{:S(2)}, u32[]{:S(2)}) collective-permute-start(f32[4,24,384]{2,1,0:T(8,128)S(1)} %get-tuple-element.55), channel_id=1, source_target_pairs={{0,4},{2,6},{4,0},{6,2},{1,5},{3,7},{5,1},{7,3},{8,12},{10,14},{12... | collective-permute-start | bytes 442376 | tf_op jit(solution)/shard_map/ppermute | solution.py:363
  105.0 0.0 collective-permute-done.6.refs_7_
  105.0 3.0 %collective-permute-start.14 = (f32[4,24,384]{2,1,0:T(8,128)S(1)}, f32[4,24,384]{2,1,0:T(8,128)S(1)}, u32[]{:S(2)}, u32[]{:S(2)}) collective-permute-start(f32[4,24,384]{2,1,0:T(8,128)S(1)} %get-tuple-element.56), channel_id=1, source_target_pairs={{0,6},{2,0},{4,2},{6,4},{1,7},{3,1},{5,3},{7,5},{8,14},{10,8},{12,... | collective-permute-start | bytes 442376 | tf_op jit(solution)/shard_map/ppermute | solution.py:363
  108.0 0.0 collective-permute-done.10.refs_10_
  108.0 0.4 collective-permute-start.9
  108.4 0.0 collective-permute-done.11.refs_11_
  108.4 1.6 %collective-permute-done.12.refs_13_ = f32[4,24,384]{2,1,0:T(8,128)S(1)} collective-permute-done((f32[4,24,384]{2,1,0:T(8,128)S(1)}, f32[4,24,384]{2,1,0:T(8,128)S(1)}, u32[]{:S(2)}, u32[]{:S(2)}) %collective-permute-start.12) | collective-permute-done | bytes 147488 | tf_op jit(solution)/shard_map/ppermute | solution.py:363
  110.0 0.0 collective-permute-done.13.refs_14_
  110.0 0.9 collective-permute-done.14.refs_15_
  110.9 2.6 %collective-permute-done.9.refs_9_ = f32[4,24,384]{2,1,0:T(8,128)S(1)} collective-permute-done((f32[4,24,384]{2,1,0:T(8,128)S(1)}, f32[4,24,384]{2,1,0:T(8,128)S(1)}, u32[]{:S(2)}, u32[]{:S(2)}) %collective-permute-start.9) | collective-permute-done | bytes 147488 | tf_op jit(solution)/shard_map/ppermute | solution.py:363
  113.5 0.1 sum.1
  113.6 0.0 copy-start.1
  113.6 0.1 collective-permute-start.15
  113.7 0.9 collective-permute-start.16
  114.6 1.8 %collective-permute-start.17 = (f32[2,24,384]{2,1,0:T(8,128)S(1)}, f32[2,24,384]{2,1,0:T(8,128)S(1)}, u32[]{:S(2)}, u32[]{:S(2)}) collective-permute-start(f32[2,24,384]{2,1,0:T(8,128)S(1)} %get-tuple-element.60), channel_id=1, source_target_pairs={{0,6},{2,0},{4,2},{6,4},{1,7},{3,1},{5,3},{7,5},{8,14},{10,8},{12,... | collective-permute-start | bytes 221192 | tf_op jit(solution)/shard_map/ppermute | solution.py:363
  116.4 0.0 collective-permute-start.18
  116.4 2.6 %collective-permute-start.19 = (f32[2,24,384]{2,1,0:T(8,128)S(1)}, f32[2,24,384]{2,1,0:T(8,128)S(1)}, u32[]{:S(2)}, u32[]{:S(2)}) collective-permute-start(f32[2,24,384]{2,1,0:T(8,128)S(1)} %get-tuple-element.63), channel_id=1, source_target_pairs={{0,128},{64,192},{128,0},{192,64},{1,129},{65,193},{129,1},{193,65... | collective-permute-start | bytes 221192 | tf_op jit(solution)/shard_map/ppermute | solution.py:363
  118.9 0.0 collective-permute-done.15.refs_1_
  118.9 0.1 collective-permute-start.20
  119.0 0.0 collective-permute-done.16.refs_2_
  119.0 0.4 collective-permute-done.17.refs_3_
  119.5 2.4 %collective-permute-done.18.refs_5_ = f32[2,24,384]{2,1,0:T(8,128)S(1)} collective-permute-done((f32[2,24,384]{2,1,0:T(8,128)S(1)}, f32[2,24,384]{2,1,0:T(8,128)S(1)}, u32[]{:S(2)}, u32[]{:S(2)}) %collective-permute-start.18) | collective-permute-done | bytes 73760 | tf_op jit(solution)/shard_map/ppermute | solution.py:363
  121.9 0.0 collective-permute-done.19.refs_6_
  121.9 0.6 collective-permute-done.20.refs_7_
  122.4 0.2 gather.1
  122.6 19.0 %all_to_all.11.part_ref = f32[16,8,384]{2,1,0:T(8,128)S(1)} all-to-all(f32[16,8,384]{2,1,0:T(8,128)S(1)} %gather.1), channel_id=1, replica_groups=mesh['y'=4,'zl'=4,'core'=2,'x'=4,'zh'=2] {'zl','zh','core'}, dimensions={0} | all-to-all | bytes 393216 | tf_op jit(solution)/shard_map/all_to_all | solution.py:390
  141.7 0.0 copy-done.1
  141.7 0.8 last.1
  142.5 0.7 copy.5
Async XLA Ops:
  0.0 1.5 %copy-start.2 = (f32[3,2,3,3,1,2304]{5,4,3,2,1,0:T(1,128)S(1)}, f32[3,2,3,3,1,2304]{5,4,3,2,1,0:T(1,128)}, u32[]{:S(2)}) copy-start(f32[3,2,3,3,1,2304]{5,4,3,2,1,0:T(1,128)} %param.5) | copy-start | bytes 1492996
  4.6 42.3 %copy-start = (s32[4,3]{1,0:T(4,128)S(1)}, s32[4,3]{1,0:T(4,128)}, u32[]{:S(2)}) copy-start(s32[4,3]{1,0:T(4,128)} %mom_ref.3) | copy-start | bytes 148
  43.7 34.0 %collective-permute-start.7 = (f32[8,384,128]{2,1,0:T(8,128)S(1)}, f32[8,384,128]{2,1,0:T(8,128)S(1)}, u32[]{:S(2)}, u32[]{:S(2)}) collective-permute-start(f32[8,384,128]{2,1,0:T(8,128)S(1)} %all_to_all.10.buf_ref), channel_id=1, source_target_pairs={{0,248},{8,0},{16,8},{24,16},{32,24},{40,32},{48,40},{56,48},{64,5... | collective-permute-start | bytes 4718600 | tf_op jit(solution)/shard_map/ppermute | solution.py:372
  58.5 31.8 %collective-permute-start = (f32[4,4,48,384]{3,2,1,0:T(8,128)S(1)}, f32[4,4,48,384]{3,2,1,0:T(8,128)S(1)}, u32[]{:S(2)}, u32[]{:S(2)}) collective-permute-start(f32[4,4,48,384]{3,2,1,0:T(8,128)S(1)} %get-tuple-element.38), channel_id=1, source_target_pairs={{0,8},{8,0},{1,9},{9,1},{2,10},{10,2},{3,11},{11,3},{4,12},{12,4},... | collective-permute-start | bytes 3538952 | tf_op jit(solution)/shard_map/ppermute | solution.py:382
  90.2 5.3 %collective-permute-start.8 = (f32[4,4,48,384]{3,2,1,0:T(8,128)S(1)}, f32[4,4,48,384]{3,2,1,0:T(8,128)S(1)}, u32[]{:S(2)}, u32[]{:S(2)}) collective-permute-start(f32[4,4,48,384]{3,2,1,0:T(8,128)S(1)} %get-tuple-element.48), channel_id=1, source_target_pairs={{0,8},{8,0},{1,9},{9,1},{2,10},{10,2},{3,11},{11,3},{4,12},{12,4},... | collective-permute-start | bytes 3538952 | tf_op jit(solution)/shard_map/ppermute | solution.py:382
  90.5 7.0 %collective-permute-start.1 = (f32[4,24,384]{2,1,0:T(8,128)S(1)}, f32[4,24,384]{2,1,0:T(8,128)S(1)}, u32[]{:S(2)}, u32[]{:S(2)}) collective-permute-start(f32[4,24,384]{2,1,0:T(8,128)S(1)} %get-tuple-element.40), channel_id=1, source_target_pairs={{0,64},{64,128},{128,192},{192,0},{1,65},{65,129},{129,193},{193,1... | collective-permute-start | bytes 442376 | tf_op jit(solution)/shard_map/ppermute | solution.py:363
  91.8 9.3 %collective-permute-start.2 = (f32[4,24,384]{2,1,0:T(8,128)S(1)}, f32[4,24,384]{2,1,0:T(8,128)S(1)}, u32[]{:S(2)}, u32[]{:S(2)}) collective-permute-start(f32[4,24,384]{2,1,0:T(8,128)S(1)} %get-tuple-element.41), channel_id=1, source_target_pairs={{0,128},{64,192},{128,0},{192,64},{1,129},{65,193},{129,1},{193,65... | collective-permute-start | bytes 442376 | tf_op jit(solution)/shard_map/ppermute | solution.py:363
  94.5 7.3 %collective-permute-start.3 = (f32[4,24,384]{2,1,0:T(8,128)S(1)}, f32[4,24,384]{2,1,0:T(8,128)S(1)}, u32[]{:S(2)}, u32[]{:S(2)}) collective-permute-start(f32[4,24,384]{2,1,0:T(8,128)S(1)} %get-tuple-element.42), channel_id=1, source_target_pairs={{0,192},{64,0},{128,64},{192,128},{1,193},{65,1},{129,65},{193,129... | collective-permute-start | bytes 442376 | tf_op jit(solution)/shard_map/ppermute | solution.py:363
  95.5 7.7 %collective-permute-start.4 = (f32[4,24,384]{2,1,0:T(8,128)S(1)}, f32[4,24,384]{2,1,0:T(8,128)S(1)}, u32[]{:S(2)}, u32[]{:S(2)}) collective-permute-start(f32[4,24,384]{2,1,0:T(8,128)S(1)} %get-tuple-element.44), channel_id=1, source_target_pairs={{0,2},{2,4},{4,6},{6,0},{1,3},{3,5},{5,7},{7,1},{8,10},{10,12},{12... | collective-permute-start | bytes 442376 | tf_op jit(solution)/shard_map/ppermute | solution.py:363
  95.5 7.7 %collective-permute-start.5 = (f32[4,24,384]{2,1,0:T(8,128)S(1)}, f32[4,24,384]{2,1,0:T(8,128)S(1)}, u32[]{:S(2)}, u32[]{:S(2)}) collective-permute-start(f32[4,24,384]{2,1,0:T(8,128)S(1)} %get-tuple-element.45), channel_id=1, source_target_pairs={{0,4},{2,6},{4,0},{6,2},{1,5},{3,7},{5,1},{7,3},{8,12},{10,14},{12... | collective-permute-start | bytes 442376 | tf_op jit(solution)/shard_map/ppermute | solution.py:363
  97.4 7.6 %collective-permute-start.6 = (f32[4,24,384]{2,1,0:T(8,128)S(1)}, f32[4,24,384]{2,1,0:T(8,128)S(1)}, u32[]{:S(2)}, u32[]{:S(2)}) collective-permute-start(f32[4,24,384]{2,1,0:T(8,128)S(1)} %get-tuple-element.46), channel_id=1, source_target_pairs={{0,6},{2,0},{4,2},{6,4},{1,7},{3,1},{5,3},{7,5},{8,14},{10,8},{12,... | collective-permute-start | bytes 442376 | tf_op jit(solution)/shard_map/ppermute | solution.py:363
  101.1 6.9 %collective-permute-start.10 = (f32[4,24,384]{2,1,0:T(8,128)S(1)}, f32[4,24,384]{2,1,0:T(8,128)S(1)}, u32[]{:S(2)}, u32[]{:S(2)}) collective-permute-start(f32[4,24,384]{2,1,0:T(8,128)S(1)} %get-tuple-element.51), channel_id=1, source_target_pairs={{0,128},{64,192},{128,0},{192,64},{1,129},{65,193},{129,1},{193,65... | collective-permute-start | bytes 442376 | tf_op jit(solution)/shard_map/ppermute | solution.py:363
  101.7 6.7 %collective-permute-start.11 = (f32[4,24,384]{2,1,0:T(8,128)S(1)}, f32[4,24,384]{2,1,0:T(8,128)S(1)}, u32[]{:S(2)}, u32[]{:S(2)}) collective-permute-start(f32[4,24,384]{2,1,0:T(8,128)S(1)} %get-tuple-element.52), channel_id=1, source_target_pairs={{0,192},{64,0},{128,64},{192,128},{1,193},{65,1},{129,65},{193,129... | collective-permute-start | bytes 442376 | tf_op jit(solution)/shard_map/ppermute | solution.py:363
  103.2 6.8 %collective-permute-start.12 = (f32[4,24,384]{2,1,0:T(8,128)S(1)}, f32[4,24,384]{2,1,0:T(8,128)S(1)}, u32[]{:S(2)}, u32[]{:S(2)}) collective-permute-start(f32[4,24,384]{2,1,0:T(8,128)S(1)} %get-tuple-element.54), channel_id=1, source_target_pairs={{0,2},{2,4},{4,6},{6,0},{1,3},{3,5},{5,7},{7,1},{8,10},{10,12},{12... | collective-permute-start | bytes 442376 | tf_op jit(solution)/shard_map/ppermute | solution.py:363
  103.2 6.8 %collective-permute-start.13 = (f32[4,24,384]{2,1,0:T(8,128)S(1)}, f32[4,24,384]{2,1,0:T(8,128)S(1)}, u32[]{:S(2)}, u32[]{:S(2)}) collective-permute-start(f32[4,24,384]{2,1,0:T(8,128)S(1)} %get-tuple-element.55), channel_id=1, source_target_pairs={{0,4},{2,6},{4,0},{6,2},{1,5},{3,7},{5,1},{7,3},{8,12},{10,14},{12... | collective-permute-start | bytes 442376 | tf_op jit(solution)/shard_map/ppermute | solution.py:363
  105.0 5.9 %collective-permute-start.14 = (f32[4,24,384]{2,1,0:T(8,128)S(1)}, f32[4,24,384]{2,1,0:T(8,128)S(1)}, u32[]{:S(2)}, u32[]{:S(2)}) collective-permute-start(f32[4,24,384]{2,1,0:T(8,128)S(1)} %get-tuple-element.56), channel_id=1, source_target_pairs={{0,6},{2,0},{4,2},{6,4},{1,7},{3,1},{5,3},{7,5},{8,14},{10,8},{12,... | collective-permute-start | bytes 442376 | tf_op jit(solution)/shard_map/ppermute | solution.py:363
  108.0 5.5 %collective-permute-start.9 = (f32[4,24,384]{2,1,0:T(8,128)S(1)}, f32[4,24,384]{2,1,0:T(8,128)S(1)}, u32[]{:S(2)}, u32[]{:S(2)}) collective-permute-start(f32[4,24,384]{2,1,0:T(8,128)S(1)} %get-tuple-element.50), channel_id=1, source_target_pairs={{0,64},{64,128},{128,192},{192,0},{1,65},{65,129},{129,193},{193,1... | collective-permute-start | bytes 442376 | tf_op jit(solution)/shard_map/ppermute | solution.py:363
  113.6 28.1 %copy-start.1 = (s32[3]{0:T(128)S(1)}, s32[3]{0:T(128)}, u32[]{:S(2)}) copy-start(s32[3]{0:T(128)} %direction_ref.1) | copy-start | bytes 40
  113.6 5.3 %collective-permute-start.15 = (f32[2,24,384]{2,1,0:T(8,128)S(1)}, f32[2,24,384]{2,1,0:T(8,128)S(1)}, u32[]{:S(2)}, u32[]{:S(2)}) collective-permute-start(f32[2,24,384]{2,1,0:T(8,128)S(1)} %get-tuple-element.58), channel_id=1, source_target_pairs={{0,2},{2,4},{4,6},{6,0},{1,3},{3,5},{5,7},{7,1},{8,10},{10,12},{12... | collective-permute-start | bytes 221192 | tf_op jit(solution)/shard_map/ppermute | solution.py:363
  113.7 5.4 %collective-permute-start.16 = (f32[2,24,384]{2,1,0:T(8,128)S(1)}, f32[2,24,384]{2,1,0:T(8,128)S(1)}, u32[]{:S(2)}, u32[]{:S(2)}) collective-permute-start(f32[2,24,384]{2,1,0:T(8,128)S(1)} %get-tuple-element.59), channel_id=1, source_target_pairs={{0,4},{2,6},{4,0},{6,2},{1,5},{3,7},{5,1},{7,3},{8,12},{10,14},{12... | collective-permute-start | bytes 221192 | tf_op jit(solution)/shard_map/ppermute | solution.py:363
  114.6 4.9 %collective-permute-start.17 = (f32[2,24,384]{2,1,0:T(8,128)S(1)}, f32[2,24,384]{2,1,0:T(8,128)S(1)}, u32[]{:S(2)}, u32[]{:S(2)}) collective-permute-start(f32[2,24,384]{2,1,0:T(8,128)S(1)} %get-tuple-element.60), channel_id=1, source_target_pairs={{0,6},{2,0},{4,2},{6,4},{1,7},{3,1},{5,3},{7,5},{8,14},{10,8},{12,... | collective-permute-start | bytes 221192 | tf_op jit(solution)/shard_map/ppermute | solution.py:363
  116.4 5.5 %collective-permute-start.18 = (f32[2,24,384]{2,1,0:T(8,128)S(1)}, f32[2,24,384]{2,1,0:T(8,128)S(1)}, u32[]{:S(2)}, u32[]{:S(2)}) collective-permute-start(f32[2,24,384]{2,1,0:T(8,128)S(1)} %get-tuple-element.62), channel_id=1, source_target_pairs={{0,64},{64,128},{128,192},{192,0},{1,65},{65,129},{129,193},{193,1... | collective-permute-start | bytes 221192 | tf_op jit(solution)/shard_map/ppermute | solution.py:363
  116.4 5.5 %collective-permute-start.19 = (f32[2,24,384]{2,1,0:T(8,128)S(1)}, f32[2,24,384]{2,1,0:T(8,128)S(1)}, u32[]{:S(2)}, u32[]{:S(2)}) collective-permute-start(f32[2,24,384]{2,1,0:T(8,128)S(1)} %get-tuple-element.63), channel_id=1, source_target_pairs={{0,128},{64,192},{128,0},{192,64},{1,129},{65,193},{129,1},{193,65... | collective-permute-start | bytes 221192 | tf_op jit(solution)/shard_map/ppermute | solution.py:363
  118.9 3.5 %collective-permute-start.20 = (f32[2,24,384]{2,1,0:T(8,128)S(1)}, f32[2,24,384]{2,1,0:T(8,128)S(1)}, u32[]{:S(2)}, u32[]{:S(2)}) collective-permute-start(f32[2,24,384]{2,1,0:T(8,128)S(1)} %get-tuple-element.64), channel_id=1, source_target_pairs={{0,192},{64,0},{128,64},{192,128},{1,193},{65,1},{129,65},{193,129... | collective-permute-start | bytes 221192 | tf_op jit(solution)/shard_map/ppermute | solution.py:363

commit v4 on v0

v4 whole, which is shorter than its diff:
```python
import math

import jax
import jax.numpy as jnp
from jax import lax
from jax.experimental import pallas as pl
from jax.experimental.pallas import tpu as pltpu
from jax.sharding import Mesh
from jax.sharding import PartitionSpec as P

LY = 48
HALF = 1152
TILES = 9
ROWS = 1296
DEPTH = 3456
SITE = ("y", "zl", "core")
VMEM_BYTES = 44 * 1024 * 1024


def cut_kernel(vec_ref, link_ref, keep_ref, send_ref, halo_ref, halo_send_ref, link_out_ref):
    zh = lax.axis_index("zh")
    for out_ref, other_ref, begin in ((keep_ref, halo_send_ref, zh), (send_ref, halo_ref, 1 - zh)):
        for tile in range(TILES):
            at = pl.ds(pl.multiple_of(begin * HALF + tile * 128, 128), 128)
            for reim in range(2):
                row = reim * 648 + tile * 72
                out_ref[row:row + 72] = vec_ref[reim * 72:reim * 72 + 72, at]
        lane = lax.broadcasted_iota(jnp.int32, (24, 128), 1)
        at = pl.ds(pl.multiple_of(begin * HALF, 128), 128)
        for pair in range(3):
            even = vec_ref[pair * 48:pair * 48 + 24, at]
            odd = vec_ref[pair * 48 + 24:pair * 48 + 48, at]
            other_ref[pair * 24:pair * 24 + 24] = jnp.where(lane < LY, even, pltpu.roll(odd, LY, 1))
    for tile in range(TILES):
        at = pl.ds(pl.multiple_of(zh * HALF + tile * 128, 128), 128)
        link_out_ref[tile, :54] = link_ref[:, at]


def wrapped(value, period):
    rest = lax.rem(value, period)
    return jnp.where(rest < 0, rest + period, rest)


def phase_kernel(mom_ref, out_ref):
    core = lax.axis_index("core")
    zpos = lax.axis_index("y") * 8 + lax.axis_index("zl") * 2 + core
    row = lax.broadcasted_iota(jnp.int32, (40, 128), 0)
    site = lax.broadcasted_iota(jnp.int32, (40, 128), 1) + 128 * (row >> 2)
    line = jnp.floor((site.astype(jnp.float32) + 0.5) * (1.0 / LY)).astype(jnp.int32)
    momentum = []
    for axis in range(3):
        value = jnp.zeros((40, 128), jnp.int32)
        for index in range(4):
            p = (2 * (1 - core) if index < 2 else 2 * core) + index % 2
            value = jnp.where((row & 3) == index, mom_ref[p, axis], value)
        momentum.append(value)
    fx = wrapped(momentum[0] * (line + 24 * lax.axis_index("zh")), 48).astype(jnp.float32) / 48
    fy = wrapped(momentum[1] * (site - line * LY), 48).astype(jnp.float32) / 48
    fz = wrapped(momentum[2] * zpos, 32).astype(jnp.float32) / 32
    theta = (2.0 * math.pi) * (fx + fy + fz)
    cosines = jnp.cos(theta)
    sines = jnp.sin(theta)
    for tile in range(TILES):
        out_ref[tile, :4] = cosines[4 * tile:4 * tile + 4]
        out_ref[tile, 4:] = sines[4 * tile:4 * tile + 4]


def split(value):
    high = value.astype(jnp.bfloat16)
    return high, (value - high.astype(jnp.float32)).astype(jnp.bfloat16)


def build_right(keep_ref, came_ref, halo_ref, halo_came_ref, zkeep_ref, zcame_ref, link_ref, right_ref):
    lane = lax.broadcasted_iota(jnp.int32, (48, 128), 1)

    def load(first_ref, second_ref, reim, tile, color):
        row = reim * 648 + tile * 72 + color * 24
        return jnp.concatenate([first_ref[row:row + 24], second_ref[row:row + 24]], axis=0)

    def beyond_x(reim, tile, color):
        here = pltpu.roll(load(keep_ref, came_ref, reim, tile, color), 80, 1)
        if tile + 1 < TILES:
            after = pltpu.roll(load(keep_ref, came_ref, reim, tile + 1, color), 80, 1)
        else:
            field = reim * 3 + color
            row = field // 2 * 24
            after = jnp.concatenate([halo_ref[row:row + 24], halo_came_ref[row:row + 24]], axis=0)
            after = pltpu.roll(after, 80 - LY * (field % 2), 1)
        return jnp.where(lane < 80, here, after)

    def beyond_y(reim, tile, color):
        here = load(keep_ref, came_ref, reim, tile, color)
        value = pltpu.roll(here, 127, 1)
        back = pltpu.roll(here, 47, 1)
        for at in range(128):
            if (tile * 128 + at) % LY == LY - 1:
                if at >= 47:
                    value = jnp.where(lane == at, back, value)
                else:
                    before = pltpu.roll(load(keep_ref, came_ref, reim, tile - 1, color), 47, 1)
                    value = jnp.where(lane == at, before, value)
        if (tile * 128 + 127) % LY != LY - 1:
            after = pltpu.roll(load(keep_ref, came_ref, reim, tile + 1, color), 127, 1)
            value = jnp.where(lane == 127, after, value)
        return value

    def beyond_z(reim, tile, color):
        return load(zkeep_ref, zcame_ref, reim, tile, color)

    def put(reim, k, tile, color, value):
        row = reim * 192 + k * 48
        column = (tile * 3 + color) * 128
        high, low = split(value)
        right_ref[row:row + 48, column:column + 128] = high
        right_ref[384 + row:384 + row + 48, column:column + 128] = low

    for tile in range(TILES):
        for color in range(3):
            for reim in range(2):
                put(reim, 0, tile, color, load(keep_ref, came_ref, reim, tile, color))
        for direction, beyond in enumerate((beyond_x, beyond_y, beyond_z)):
            far = [[beyond(reim, tile, color) for color in range(3)] for reim in range(2)]
            for row in range(3):
                re = None
                im = None
                for column in range(3):
                    at = direction * 18 + row * 3 + column
                    ur = link_ref[tile, at:at + 1, :]
                    ui = link_ref[tile, at + 9:at + 10, :]
                    more_re = ur * far[0][column] - ui * far[1][column]
                    more_im = ur * far[1][column] + ui * far[0][column]
                    re = more_re if re is None else re + more_re
                    im = more_im if im is None else im + more_im
                put(0, direction + 1, tile, row, re)
                put(1, direction + 1, tile, row, im)


def multiply(blocks, phase_ref, right_ref, away_ref, stay_ref, high_ref, low_ref):
    count = len(blocks)
    rows = 24 * count

    def make_left(tile, carry):
        real = []
        imag = []
        for block in blocks:
            if len(block) == 1:
                real.append(block[0][pl.ds(pl.multiple_of(tile * 72, 8), 72)])
                imag.append(block[0][pl.ds(pl.multiple_of(tile * 72 + 648, 8), 72)])
            else:
                real.append(block[0][pl.ds(pl.multiple_of(tile * 72, 8), 72)])
                imag.append(block[1][pl.ds(pl.multiple_of(tile * 72, 8), 72)])
        for index in range(4):
            cosv = phase_ref[tile, index:index + 1, :]
            sinv = phase_ref[tile, 4 + index:5 + index, :]
            left_real = [a * cosv - b * sinv for a, b in zip(real, imag)]
            left_imag = [-(a * sinv + b * cosv) for a, b in zip(real, imag)]
            for color in range(3):
                value = jnp.concatenate(
                    [part[color * 24:color * 24 + 24] for part in left_real + left_imag], axis=0
                )
                high, low = split(value)
                column = pl.ds(pl.multiple_of(tile * 384 + color * 128, 128), 128)
                high_ref[2 * rows * index:2 * rows * (index + 1), column] = high
                low_ref[2 * rows * index:2 * rows * (index + 1), column] = low
        return carry

    lax.fori_loop(0, TILES, make_left, 0)

    def times(left, right):
        return lax.dot_general(
            left, right, (((1,), (1,)), ((), ())), preferred_element_type=jnp.float32
        )

    both = times(high_ref[...], right_ref[...])
    total = both[:, :384] + both[:, 384:] + times(low_ref[...], right_ref[:384])
    for index in range(4):
        out_ref = (away_ref, stay_ref)[index // 2]
        base = 2 * rows * index
        top = total[base:base + rows]
        low = total[base + rows:base + 2 * rows]
        product = (top[:, :192] - low[:, 192:], low[:, :192] + top[:, 192:])
        for reim in range(2):
            column = (2 * (index % 2) + reim) * 192
            for sub in range(count):
                out_ref[sub, :, column:column + 192] = product[reim][sub * 24:sub * 24 + 24]


def own_kernel(keep, came, halo, halo_came, zkeep, zcame, link, phase, right, away, stay, high, low):
    build_right(keep, came, halo, halo_came, zkeep, zcame, link, right)
    multiply([(keep,), (came,)], phase, right, away, stay, high, low)


def kept_kernel(after, before, far_real, far_imag, phase, right, away, stay, high, low):
    multiply([(after,), (before,), (far_real, far_imag)], phase, right, away, stay, high, low)


def came_kernel(after, before, phase, right, away, stay, high, low):
    multiply([(after,), (before,)], phase, right, away, stay, high, low)


def far_kernel(far_real, far_imag, phase, right, away, stay, high, low):
    multiply([(far_real, far_imag)], phase, right, away, stay, high, low)


def add_kernel(*refs):
    x = lax.axis_index("x")
    zh = lax.axis_index("zh")
    out_ref = refs[8]
    order = (((0, 0), (0, 1)), ((1, 0), (3, 0), (2, 0)), ((1, 1), (3, 1)), ((2, 1),))
    for call_at, blocks in enumerate(order):
        for sub, (distance, came) in enumerate(blocks):
            to = lax.rem(x + distance, 4)
            half = 1 - zh if came else zh
            out_ref[to, pl.ds(pl.multiple_of(half * 24, 8), 24)] = (
                refs[2 * call_at][sub] + refs[2 * call_at + 1][sub]
            )


def pack_kernel(part_ref, out_ref):
    zh = lax.axis_index("zh")
    total = part_ref[0] + part_ref[1] + part_ref[2] + part_ref[3]
    for came in range(2):
        pieces = []
        for piece in range(16):
            begin = piece * 48 + came * 24
            pieces.append(total[:, begin:begin + 24])
        packed = jnp.concatenate(pieces, axis=1)
        half = 1 - zh if came else zh
        for zl in range(4):
            for core in range(2):
                begin = zl * 12 + core * 6
                to = zl * 4 + half * 2 + core
                out_ref[to, :6] = packed[begin:begin + 6]
                out_ref[to, 6:] = jnp.zeros((2, 384), jnp.float32)


def last_kernel(direction_ref, part_ref, out_ref):
    for core in range(2):
        total = part_ref[core]
        for source in range(1, 8):
            total = total + part_ref[2 * source + core]
        total = total[:6]
        for p in range(2):
            for reim in range(2):
                begin = p * 192 + reim * 96
                fields = [total[:, begin + 24 * k:begin + 24 * k + 24] for k in range(4)]
                out_ref[2 * core + p, 0, reim] = fields[0]
                for d in range(1, 4):
                    k = direction_ref[d - 1]
                    value = jnp.where(k == 1, fields[2], fields[1])
                    out_ref[2 * core + p, d, reim] = jnp.where(k == 2, fields[3], value)


def vmem(count):
    return [pl.BlockSpec(memory_space=pltpu.VMEM)] * count


def call(kernel, name, outs, operands, scratch=(), scalars=0):
    out_shape = tuple(
        jax.ShapeDtypeStruct(shape, jnp.bfloat16 if shape == (768, DEPTH) else jnp.float32) for shape in outs
    )
    return pl.pallas_call(
        kernel,
        out_shape=out_shape,
        in_specs=[pl.BlockSpec(memory_space=pltpu.SMEM)] * scalars + vmem(len(operands) - scalars),
        out_specs=tuple(vmem(len(outs))),
        scratch_shapes=list(scratch),
        compiler_params=pltpu.CompilerParams(vmem_limit_bytes=VMEM_BYTES),
        name=name,
    )(*operands)


def along(value, axis, step):
    count = lax.axis_size(axis)
    return lax.ppermute(value, axis, [(i, (i + step) % count) for i in range(count)])


def left_scratch(count):
    return [pltpu.VMEM((192 * count, DEPTH), jnp.bfloat16)] * 2


def local(eigvecs, links, momenta, directions):
    flat = (ROWS, 128)
    keep, send, halo, halo_send, link = call(
        cut_kernel, "cut", [flat, flat, (72, 128), (72, 128), (TILES, 56, 128)],
        (eigvecs.reshape(144, 2304), links.reshape(54, 2304)),
    )
    came = along(send, "zh", 1)
    halo_came = along(halo_send, "zh", 1)
    keep_after = along(keep, "x", -1)
    keep_before = along(keep, "x", 1)
    zkeep = along(keep, SITE, -1)
    phase, = call(phase_kernel, "phase", [(TILES, 8, 128)], (momenta,), (), 1)
    keep_far = (along(keep_after[:648], "x", -1), along(keep_before[648:], "x", 1))
    zcame = along(came, SITE, -1)
    came_after = along(came, "x", -1)
    came_before = along(came, "x", 1)
    came_far = (along(came_after[:648], "x", -1), along(came_before[648:], "x", 1))

    def parts(count):
        return [(count, 24, 768)] * 2

    right, away, stay = call(
        own_kernel, "own", [(768, DEPTH)] + parts(2),
        (keep, came, halo, halo_came, zkeep, zcame, link, phase), left_scratch(2),
    )
    products = [(away, stay)]
    products.append(call(
        kept_kernel, "kept", parts(3), (keep_after, keep_before, *keep_far, phase, right), left_scratch(3)
    ))
    products.append(call(
        came_kernel, "came", parts(2), (came_after, came_before, phase, right), left_scratch(2)
    ))
    products.append(call(far_kernel, "far", parts(1), (*came_far, phase, right), left_scratch(1)))
    terms = []
    for away, stay in products:
        terms += [stay, along(away, "core", 1)]
    ready, = call(add_kernel, "add", [(4, 48, 768)], terms)
    packed, = call(pack_kernel, "pack", [(16, 8, 384)], (lax.all_to_all(ready, "y", 0, 0),))
    mixed = lax.all_to_all(packed, ("zl", "zh", "core"), 0, 0)
    return call(last_kernel, "last", [(4, 4, 2, 6, 24)], (directions, mixed), (), 1)[0]


def solution(mesh):
    fine = Mesh(mesh.devices.reshape(4, 4, 2, 4, 2), ("y", "zl", "core", "x", "zh"))
    ev = ("x", "zh")
    in_specs = (P(None, None, ev, SITE, None), P(None, None, None, None, SITE, None), P(), P())
    out_specs = P(None, None, None, SITE, ev)
    return jax.shard_map(local, mesh=fine, in_specs=in_specs, out_specs=out_specs, check_vma=False)
```

time: 591 us -> 134 us (0.23)
  waiting for transfers between devices: 427 us -> 23.6 us
  matrix products: 56.9 us -> 0 us
  other arithmetic: 45.9 us -> 1.43 us
  starting transfers between devices: 3.36 us -> 43.9 us
  local copies, waits for them, and re-layouts: 39.1 us -> 2.51 us
  blocking collectives: 0 us -> 34.2 us
  Pallas kernels: 0 us -> 28.3 us
  between operations: 14.8 us -> 0.14 us
    unnamed x3 -> x0, waiting for transfers between devices: 282 us -> none
    all_gather x1 -> x0, waiting for transfers between devices: 145 us -> none  [local(): lax.all_gather(eigvecs, 'ev', axis=2, tiled=True)]
    dot_general x5 -> x0, matrix products: 56.9 us -> none  [the longest x4 48 us: contract(): jnp.einsum('acrzs,dbcjzs->abdrj', weighted, right, precision=lax.Precisio...]
    ppermute x1 -> x16, starting transfers between devices: 3.32 us -> 43.9 us  [along(): lax.ppermute(value, axis, [(i, (i + step) % count) for i in range(count)])]
    all_to_all x0 -> x2, blocking collectives: none -> 34.2 us  [the longest x1 20.5 us: local(): mixed = lax.all_to_all(packed, ('zl', 'zh', 'core'), 0, 0)]
    pallas_call x0 -> x9, Pallas kernels: none -> 28.3 us  [call(): pl.pallas_call(kernel, out_shape=out_shape, in_specs=[pl.BlockSpec(memory...]
    ppermute x1 -> x16, waiting for transfers between devices: 0.01 us -> 23.6 us  [along(): lax.ppermute(value, axis, [(i, (i + step) % count) for i in range(count)])]
    sub x6 -> x0, other arithmetic: 18.9 us -> none  [the longest x2 18.8 us: contract(): left_real = left_vector[0] * cosine_value - left_vector[1] * sine_value]
  transfers between devices with their start and end apart: 3 -> 16, of which waited for: 2 -> 5; matrix products, arithmetic and copies ran while one was open for 12% -> 0% of each run, Pallas kernels for 0% -> 20%
where the time goes in v4:
time: 134 us
  starting transfers between devices  43.9 us (33%)
  blocking collectives  34.2 us (26%)
  Pallas kernels  28.3 us (21%)
  waiting for transfers between devices  23.6 us (18%)
  local copies, waits for them, and re-layouts  2.51 us (2%)
  other arithmetic  1.43 us (1%)
    ppermute x16, starting transfers between devices, along(): lax.ppermute(value, axis, [(i, (i + step) % count) for i in range(count)])  43.9 us
    pallas_call x9, Pallas kernels, call(): pl.pallas_call(kernel, out_shape=out_shape, in_specs=[pl.BlockSpec(memory...  28.3 us
    ppermute x16, waiting for transfers between devices, along(): lax.ppermute(value, axis, [(i, (i + step) % count) for i in range(count)])  23.6 us
    all_to_all x1, blocking collectives, local(): mixed = lax.all_to_all(packed, ('zl', 'zh', 'core'), 0, 0)  20.5 us
    all_to_all x1, blocking collectives, local(): lax.all_to_all(ready, 'y', 0, 0)  13.6 us
  transfers between devices with their start and end apart: 16, of which 5 were waited for; matrix products, arithmetic and copies ran while one was open for 0% of the time, Pallas kernels for 20%

profile of v4, /device:TPU:1, one launch (start us, length us, event | category | flops | bytes accessed | tf_op | source)
XLA Modules:
  0.0 134.2 jit_solution(5444114658753898788)
XLA Ops:
  0.0 0.0 copy-start.2
  0.0 1.5 %copy.6 = f32[2,3,24,1,2304]{4,2,3,1,0:T(8,128)S(1)} copy(f32[2,3,24,1,2304]{4,3,2,1,0:T(1,128)} %param.4) | data formatting | bytes 2654208
  1.5 0.0 copy-done.2
  1.5 1.4 %reduce = f32[3,2,3,3,2304]{4,3,2,1,0:T(4,128)S(1)} reduce(f32[3,2,3,3,1,2304]{5,4,3,2,1,0:T(1,128)S(1)} %copy-done.2, f32[]{:T(128)} %constant.2), dimensions={4}, to_apply=%param.5.reduce_sub_computation | reduce | bytes 995332 | tf_op args[1]
  2.9 0.2 reshape.7.link_ref
  3.2 0.2 cut.1
  3.3 7.8 %collective-permute-start = (f32[1296,128]{1,0:T(8,128)S(1)}, f32[1296,128]{1,0:T(8,128)S(1)}, u32[]{:S(2)}, u32[]{:S(2)}) collective-permute-start(f32[1296,128]{1,0:T(8,128)S(1)} %get-tuple-element.20), channel_id=1, source_target_pairs={{0,1},{1,0},{2,3},{3,2},{4,5},{5,4},{6,7},{7,6},{8,9},{9,8},{10,11... | collective-permute-start | bytes 1990664 | tf_op jit(solution)/shard_map/ppermute | solution.py:275
  11.2 0.0 copy-start
  11.2 2.5 %collective-permute-start.5 = (f32[1296,128]{1,0:T(8,128)S(1)}, f32[1296,128]{1,0:T(8,128)S(1)}, u32[]{:S(2)}, u32[]{:S(2)}) collective-permute-start(f32[1296,128]{1,0:T(8,128)S(1)} %get-tuple-element.19.keep), channel_id=1, source_target_pairs={{0,6},{2,0},{4,2},{6,4},{1,7},{3,1},{5,3},{7,5},{8,14},{10,8},{12,... | collective-permute-start | bytes 1990664 | tf_op jit(solution)/shard_map/ppermute | solution.py:275
  13.6 0.0 collective-permute-start.6
  13.7 14.9 %collective-permute-done.came = f32[1296,128]{1,0:T(8,128)S(1)} collective-permute-done((f32[1296,128]{1,0:T(8,128)S(1)}, f32[1296,128]{1,0:T(8,128)S(1)}, u32[]{:S(2)}, u32[]{:S(2)}) %collective-permute-start) | collective-permute-done | bytes 663584 | tf_op jit(solution)/shard_map/ppermute | solution.py:275
  28.6 3.0 %collective-permute-start.10 = (f32[1296,128]{1,0:T(8,128)S(1)}, f32[1296,128]{1,0:T(8,128)S(1)}, u32[]{:S(2)}, u32[]{:S(2)}) collective-permute-start(f32[1296,128]{1,0:T(8,128)S(1)} %collective-permute-done.came), channel_id=1, source_target_pairs={{0,6},{2,0},{4,2},{6,4},{1,7},{3,1},{5,3},{7,5},{8,14},{10,8},{12,... | collective-permute-start | bytes 1990664 | tf_op jit(solution)/shard_map/ppermute | solution.py:275
  31.6 0.0 collective-permute-start.11
  31.6 1.7 %collective-permute-start.2 = (f32[1296,128]{1,0:T(8,128)S(1)}, f32[1296,128]{1,0:T(8,128)S(1)}, u32[]{:S(2)}, u32[]{:S(2)}) collective-permute-start(f32[1296,128]{1,0:T(8,128)S(1)} %get-tuple-element.19.keep), channel_id=1, source_target_pairs={{0,248},{8,0},{16,8},{24,16},{32,24},{40,32},{48,40},{56,48},{64,5... | collective-permute-start | bytes 1990664 | tf_op jit(solution)/shard_map/ppermute | solution.py:275
  33.3 0.0 collective-permute-done.5.after
  33.3 8.7 %collective-permute-start.3 = (f32[1296,128]{1,0:T(8,128)S(1)}, f32[1296,128]{1,0:T(8,128)S(1)}, u32[]{:S(2)}, u32[]{:S(2)}) collective-permute-start(f32[1296,128]{1,0:T(8,128)S(1)} %collective-permute-done.came), channel_id=1, source_target_pairs={{0,248},{8,0},{16,8},{24,16},{32,24},{40,32},{48,40},{56,48},{64,5... | collective-permute-start | bytes 1990664 | tf_op jit(solution)/shard_map/ppermute | solution.py:275
  42.0 0.0 collective-permute-done.6.before
  42.0 2.8 %collective-permute-start.7 = (f32[648,128]{1,0:T(8,128)S(1)}, f32[648,128]{1,0:T(8,128)S(1)}, u32[]{:S(2)}, u32[]{:S(2)}) collective-permute-start(f32[648,128]{1,0:T(8,128)S(1)} %slice.16), channel_id=1, source_target_pairs={{0,6},{2,0},{4,2},{6,4},{1,7},{3,1},{5,3},{7,5},{8,14},{10,8},{12,... | collective-permute-start | bytes 995336 | tf_op jit(solution)/shard_map/ppermute | solution.py:275
  44.8 0.0 collective-permute-done.10.after
  44.8 0.5 collective-permute-start.8
  45.3 2.2 %collective-permute-done.11.before = f32[1296,128]{1,0:T(8,128)S(1)} collective-permute-done((f32[1296,128]{1,0:T(8,128)S(1)}, f32[1296,128]{1,0:T(8,128)S(1)}, u32[]{:S(2)}, u32[]{:S(2)}) %collective-permute-start.11) | collective-permute-done | bytes 663584 | tf_op jit(solution)/shard_map/ppermute | solution.py:275
  47.5 4.6 %collective-permute-start.1 = (f32[72,128]{1,0:T(8,128)S(1)}, f32[72,128]{1,0:T(8,128)S(1)}, u32[]{:S(2)}, u32[]{:S(2)}) collective-permute-start(f32[72,128]{1,0:T(8,128)S(1)} %get-tuple-element.22), channel_id=1, source_target_pairs={{0,1},{1,0},{2,3},{3,2},{4,5},{5,4},{6,7},{7,6},{8,9},{9,8},{10,11... | collective-permute-start | bytes 110600 | tf_op jit(solution)/shard_map/ppermute | solution.py:275
  52.2 2.5 %collective-permute-done.1.halo_came = f32[72,128]{1,0:T(8,128)S(1)} collective-permute-done((f32[72,128]{1,0:T(8,128)S(1)}, f32[72,128]{1,0:T(8,128)S(1)}, u32[]{:S(2)}, u32[]{:S(2)}) %collective-permute-start.1) | collective-permute-done | bytes 36896 | tf_op jit(solution)/shard_map/ppermute | solution.py:275
  54.7 1.8 %collective-permute-start.13 = (f32[648,128]{1,0:T(8,128)S(1)}, f32[648,128]{1,0:T(8,128)S(1)}, u32[]{:S(2)}, u32[]{:S(2)}) collective-permute-start(f32[648,128]{1,0:T(8,128)S(1)} %slice.18), channel_id=1, source_target_pairs={{0,6},{2,0},{4,2},{6,4},{1,7},{3,1},{5,3},{7,5},{8,14},{10,8},{12,... | collective-permute-start | bytes 995336 | tf_op jit(solution)/shard_map/ppermute | solution.py:275
  56.5 0.0 collective-permute-done.2.zkeep
  56.5 0.0 collective-permute-start.14
  56.5 0.0 copy-done
  56.5 0.7 phase.1
  57.2 3.0 %collective-permute-done.3.zcame = f32[1296,128]{1,0:T(8,128)S(1)} collective-permute-done((f32[1296,128]{1,0:T(8,128)S(1)}, f32[1296,128]{1,0:T(8,128)S(1)}, u32[]{:S(2)}, u32[]{:S(2)}) %collective-permute-start.3) | collective-permute-done | bytes 663584 | tf_op jit(solution)/shard_map/ppermute | solution.py:275
  60.3 8.8 %own.1 = (bf16[768,3456]{1,0:T(8,128)(2,1)S(1)}, f32[2,24,768]{2,1,0:T(8,128)S(1)}, f32[2,24,768]{2,1,0:T(8,128)S(1)}) custom-call(f32[1296,128]{1,0:T(8,128)S(1)} %get-tuple-element.19.keep, f32[1296,128]{1,0:T(8,128)S(1)} %collective-permute-done.came, f32[72,128]{1,0:T(8,128)S(1)} %get-tuple-element.21.halo, ...), custom_call_target="tpu_custom_call" | custom-call | tf_op jit(solution)/shard_map/own/pallas_call | solution.py:262
  69.1 0.0 collective-permute-done.7.far_real
  69.1 0.0 collective-permute-done.8.far_imag
  69.1 8.4 %kept.1 = (f32[3,24,768]{2,1,0:T(8,128)S(1)}, f32[3,24,768]{2,1,0:T(8,128)S(1)}) custom-call(f32[1296,128]{1,0:T(8,128)S(1)} %collective-permute-done.5.after, f32[1296,128]{1,0:T(8,128)S(1)} %collective-permute-done.6.before, f32[648,128]{1,0:T(8,128)S(1)} %collective-permute-done.7.far_real, f32[648,128]{1,0:T(8,128)S(1)} %collective-permute-done.8.far_imag, ...), custom_call_target="tpu_custom_call" | custom-call | tf_op jit(solution)/shard_map/kept/pallas_call | solution.py:262
  77.5 9.5 %collective-permute-start.9 = (f32[3,24,768]{2,1,0:T(8,128)S(1)}, f32[3,24,768]{2,1,0:T(8,128)S(1)}, u32[]{:S(2)}, u32[]{:S(2)}) collective-permute-start(f32[3,24,768]{2,1,0:T(8,128)S(1)} %get-tuple-element.28), channel_id=1, source_target_pairs={{0,8},{8,0},{1,9},{9,1},{2,10},{10,2},{3,11},{11,3},{4,12},{12,4},... | collective-permute-start | bytes 663560 | tf_op jit(solution)/shard_map/ppermute | solution.py:275
  87.0 0.3 collective-permute-start.4
  87.3 5.6 %came.1 = (f32[2,24,768]{2,1,0:T(8,128)S(1)}, f32[2,24,768]{2,1,0:T(8,128)S(1)}) custom-call(f32[1296,128]{1,0:T(8,128)S(1)} %collective-permute-done.10.after, f32[1296,128]{1,0:T(8,128)S(1)} %collective-permute-done.11.before, f32[9,8,128]{2,1,0:T(8,128)S(1)} %phase.1, bf16[768,3456]{1,0:T(8,128)(2,1)S(1)} %get-tuple-element.26.right), custom_call_target="tpu_custom_call" | custom-call | tf_op jit(solution)/shard_map/came/pallas_call | solution.py:262
  92.9 0.3 collective-permute-start.12
  93.2 0.0 collective-permute-done.13.far_real
  93.2 0.0 collective-permute-done.14.far_imag
  93.2 3.7 %far.1 = (f32[1,24,768]{2,1,0:T(8,128)S(1)}, f32[1,24,768]{2,1,0:T(8,128)S(1)}) custom-call(f32[648,128]{1,0:T(8,128)S(1)} %collective-permute-done.13.far_real, f32[648,128]{1,0:T(8,128)S(1)} %collective-permute-done.14.far_imag, f32[9,8,128]{2,1,0:T(8,128)S(1)} %phase.1, bf16[768,3456]{1,0:T(8,128)(2,1)S(1)} %get-tuple-element.26.right), custom_call_target="tpu_custom_call" | custom-call | tf_op jit(solution)/shard_map/far/pallas_call | solution.py:262
  96.9 0.4 collective-permute-start.15
  97.3 0.0 collective-permute-done.4.refs_1_
  97.3 0.0 collective-permute-done.12.refs_5_
  97.3 0.0 collective-permute-done.9.refs_3_
  97.3 0.9 collective-permute-done.15.refs_7_
  98.2 0.1 add.2
  98.3 0.0 copy-start.1
  98.3 13.6 %all_to_all.10.part_ref = f32[4,48,768]{2,1,0:T(8,128)S(1)} all-to-all(f32[4,48,768]{2,1,0:T(8,128)S(1)} %add.2), channel_id=1, replica_groups=mesh['y'=4,'zl'=4,'core'=2,'x'=4,'zh'=2] {'y'}, dimensions={0} | all-to-all | bytes 1179648 | tf_op jit(solution)/shard_map/all_to_all | solution.py:319
  112.0 0.2 pack.1
  112.2 20.5 %all_to_all.11.part_ref = f32[16,8,384]{2,1,0:T(8,128)S(1)} all-to-all(f32[16,8,384]{2,1,0:T(8,128)S(1)} %pack.1), channel_id=1, replica_groups=mesh['y'=4,'zl'=4,'core'=2,'x'=4,'zh'=2] {'zl','zh','core'}, dimensions={0} | all-to-all | bytes 393216 | tf_op jit(solution)/shard_map/all_to_all | solution.py:320
  132.7 0.0 copy-done.1
  132.7 0.8 last.1
  133.5 0.7 copy.5
  (4 shorter events, 0.1 us)
Async XLA Ops:
  0.0 1.5 %copy-start.2 = (f32[3,2,3,3,1,2304]{5,4,3,2,1,0:T(1,128)S(1)}, f32[3,2,3,3,1,2304]{5,4,3,2,1,0:T(1,128)}, u32[]{:S(2)}) copy-start(f32[3,2,3,3,1,2304]{5,4,3,2,1,0:T(1,128)} %param.5) | copy-start | bytes 1492996
  3.3 25.2 %collective-permute-start = (f32[1296,128]{1,0:T(8,128)S(1)}, f32[1296,128]{1,0:T(8,128)S(1)}, u32[]{:S(2)}, u32[]{:S(2)}) collective-permute-start(f32[1296,128]{1,0:T(8,128)S(1)} %get-tuple-element.20), channel_id=1, source_target_pairs={{0,1},{1,0},{2,3},{3,2},{4,5},{5,4},{6,7},{7,6},{8,9},{9,8},{10,11... | collective-permute-start | bytes 1990664 | tf_op jit(solution)/shard_map/ppermute | solution.py:275
  11.2 45.3 %copy-start = (s32[4,3]{1,0:T(4,128)S(1)}, s32[4,3]{1,0:T(4,128)}, u32[]{:S(2)}) copy-start(s32[4,3]{1,0:T(4,128)} %mom_ref.1) | copy-start | bytes 148
  11.2 22.1 %collective-permute-start.5 = (f32[1296,128]{1,0:T(8,128)S(1)}, f32[1296,128]{1,0:T(8,128)S(1)}, u32[]{:S(2)}, u32[]{:S(2)}) collective-permute-start(f32[1296,128]{1,0:T(8,128)S(1)} %get-tuple-element.19.keep), channel_id=1, source_target_pairs={{0,6},{2,0},{4,2},{6,4},{1,7},{3,1},{5,3},{7,5},{8,14},{10,8},{12,... | collective-permute-start | bytes 1990664 | tf_op jit(solution)/shard_map/ppermute | solution.py:275
  13.6 28.4 %collective-permute-start.6 = (f32[1296,128]{1,0:T(8,128)S(1)}, f32[1296,128]{1,0:T(8,128)S(1)}, u32[]{:S(2)}, u32[]{:S(2)}) collective-permute-start(f32[1296,128]{1,0:T(8,128)S(1)} %get-tuple-element.19.keep), channel_id=1, source_target_pairs={{0,2},{2,4},{4,6},{6,0},{1,3},{3,5},{5,7},{7,1},{8,10},{10,12},{12... | collective-permute-start | bytes 1990664 | tf_op jit(solution)/shard_map/ppermute | solution.py:275
  28.6 16.2 %collective-permute-start.10 = (f32[1296,128]{1,0:T(8,128)S(1)}, f32[1296,128]{1,0:T(8,128)S(1)}, u32[]{:S(2)}, u32[]{:S(2)}) collective-permute-start(f32[1296,128]{1,0:T(8,128)S(1)} %collective-permute-done.came), channel_id=1, source_target_pairs={{0,6},{2,0},{4,2},{6,4},{1,7},{3,1},{5,3},{7,5},{8,14},{10,8},{12,... | collective-permute-start | bytes 1990664 | tf_op jit(solution)/shard_map/ppermute | solution.py:275
  31.6 15.9 %collective-permute-start.11 = (f32[1296,128]{1,0:T(8,128)S(1)}, f32[1296,128]{1,0:T(8,128)S(1)}, u32[]{:S(2)}, u32[]{:S(2)}) collective-permute-start(f32[1296,128]{1,0:T(8,128)S(1)} %collective-permute-done.came), channel_id=1, source_target_pairs={{0,2},{2,4},{4,6},{6,0},{1,3},{3,5},{5,7},{7,1},{8,10},{10,12},{12... | collective-permute-start | bytes 1990664 | tf_op jit(solution)/shard_map/ppermute | solution.py:275
  31.6 24.9 %collective-permute-start.2 = (f32[1296,128]{1,0:T(8,128)S(1)}, f32[1296,128]{1,0:T(8,128)S(1)}, u32[]{:S(2)}, u32[]{:S(2)}) collective-permute-start(f32[1296,128]{1,0:T(8,128)S(1)} %get-tuple-element.19.keep), channel_id=1, source_target_pairs={{0,248},{8,0},{16,8},{24,16},{32,24},{40,32},{48,40},{56,48},{64,5... | collective-permute-start | bytes 1990664 | tf_op jit(solution)/shard_map/ppermute | solution.py:275
  33.3 27.0 %collective-permute-start.3 = (f32[1296,128]{1,0:T(8,128)S(1)}, f32[1296,128]{1,0:T(8,128)S(1)}, u32[]{:S(2)}, u32[]{:S(2)}) collective-permute-start(f32[1296,128]{1,0:T(8,128)S(1)} %collective-permute-done.came), channel_id=1, source_target_pairs={{0,248},{8,0},{16,8},{24,16},{32,24},{40,32},{48,40},{56,48},{64,5... | collective-permute-start | bytes 1990664 | tf_op jit(solution)/shard_map/ppermute | solution.py:275
  42.0 27.0 %collective-permute-start.7 = (f32[648,128]{1,0:T(8,128)S(1)}, f32[648,128]{1,0:T(8,128)S(1)}, u32[]{:S(2)}, u32[]{:S(2)}) collective-permute-start(f32[648,128]{1,0:T(8,128)S(1)} %slice.16), channel_id=1, source_target_pairs={{0,6},{2,0},{4,2},{6,4},{1,7},{3,1},{5,3},{7,5},{8,14},{10,8},{12,... | collective-permute-start | bytes 995336 | tf_op jit(solution)/shard_map/ppermute | solution.py:275
  44.8 24.3 %collective-permute-start.8 = (f32[648,128]{1,0:T(8,128)S(1)}, f32[648,128]{1,0:T(8,128)S(1)}, u32[]{:S(2)}, u32[]{:S(2)}) collective-permute-start(f32[648,128]{1,0:T(8,128)S(1)} %slice.17), channel_id=1, source_target_pairs={{0,2},{2,4},{4,6},{6,0},{1,3},{3,5},{5,7},{7,1},{8,10},{10,12},{12... | collective-permute-start | bytes 995336 | tf_op jit(solution)/shard_map/ppermute | solution.py:275
  47.5 7.2 %collective-permute-start.1 = (f32[72,128]{1,0:T(8,128)S(1)}, f32[72,128]{1,0:T(8,128)S(1)}, u32[]{:S(2)}, u32[]{:S(2)}) collective-permute-start(f32[72,128]{1,0:T(8,128)S(1)} %get-tuple-element.22), channel_id=1, source_target_pairs={{0,1},{1,0},{2,3},{3,2},{4,5},{5,4},{6,7},{7,6},{8,9},{9,8},{10,11... | collective-permute-start | bytes 110600 | tf_op jit(solution)/shard_map/ppermute | solution.py:275
  54.7 38.5 %collective-permute-start.13 = (f32[648,128]{1,0:T(8,128)S(1)}, f32[648,128]{1,0:T(8,128)S(1)}, u32[]{:S(2)}, u32[]{:S(2)}) collective-permute-start(f32[648,128]{1,0:T(8,128)S(1)} %slice.18), channel_id=1, source_target_pairs={{0,6},{2,0},{4,2},{6,4},{1,7},{3,1},{5,3},{7,5},{8,14},{10,8},{12,... | collective-permute-start | bytes 995336 | tf_op jit(solution)/shard_map/ppermute | solution.py:275
  56.5 36.7 %collective-permute-start.14 = (f32[648,128]{1,0:T(8,128)S(1)}, f32[648,128]{1,0:T(8,128)S(1)}, u32[]{:S(2)}, u32[]{:S(2)}) collective-permute-start(f32[648,128]{1,0:T(8,128)S(1)} %slice.19), channel_id=1, source_target_pairs={{0,2},{2,4},{4,6},{6,0},{1,3},{3,5},{5,7},{7,1},{8,10},{10,12},{12... | collective-permute-start | bytes 995336 | tf_op jit(solution)/shard_map/ppermute | solution.py:275
  77.5 19.8 %collective-permute-start.9 = (f32[3,24,768]{2,1,0:T(8,128)S(1)}, f32[3,24,768]{2,1,0:T(8,128)S(1)}, u32[]{:S(2)}, u32[]{:S(2)}) collective-permute-start(f32[3,24,768]{2,1,0:T(8,128)S(1)} %get-tuple-element.28), channel_id=1, source_target_pairs={{0,8},{8,0},{1,9},{9,1},{2,10},{10,2},{3,11},{11,3},{4,12},{12,4},... | collective-permute-start | bytes 663560 | tf_op jit(solution)/shard_map/ppermute | solution.py:275
  87.0 10.3 %collective-permute-start.4 = (f32[2,24,768]{2,1,0:T(8,128)S(1)}, f32[2,24,768]{2,1,0:T(8,128)S(1)}, u32[]{:S(2)}, u32[]{:S(2)}) collective-permute-start(f32[2,24,768]{2,1,0:T(8,128)S(1)} %get-tuple-element.25), channel_id=1, source_target_pairs={{0,8},{8,0},{1,9},{9,1},{2,10},{10,2},{3,11},{11,3},{4,12},{12,4},... | collective-permute-start | bytes 442376 | tf_op jit(solution)/shard_map/ppermute | solution.py:275
  92.9 4.4 %collective-permute-start.12 = (f32[2,24,768]{2,1,0:T(8,128)S(1)}, f32[2,24,768]{2,1,0:T(8,128)S(1)}, u32[]{:S(2)}, u32[]{:S(2)}) collective-permute-start(f32[2,24,768]{2,1,0:T(8,128)S(1)} %get-tuple-element.30), channel_id=1, source_target_pairs={{0,8},{8,0},{1,9},{9,1},{2,10},{10,2},{3,11},{11,3},{4,12},{12,4},... | collective-permute-start | bytes 442376 | tf_op jit(solution)/shard_map/ppermute | solution.py:275
  96.9 1.4 %collective-permute-start.15 = (f32[1,24,768]{2,1,0:T(8,128)S(1)}, f32[1,24,768]{2,1,0:T(8,128)S(1)}, u32[]{:S(2)}, u32[]{:S(2)}) collective-permute-start(f32[1,24,768]{2,1,0:T(8,128)S(1)} %get-tuple-element.32), channel_id=1, source_target_pairs={{0,8},{8,0},{1,9},{9,1},{2,10},{10,2},{3,11},{11,3},{4,12},{12,4},... | collective-permute-start | bytes 221192 | tf_op jit(solution)/shard_map/ppermute | solution.py:275
  98.3 34.4 %copy-start.1 = (s32[3]{0:T(128)S(1)}, s32[3]{0:T(128)}, u32[]{:S(2)}) copy-start(s32[3]{0:T(128)} %direction_ref.1) | copy-start | bytes 40

commit v5 on v4

--- a/solution.py
+++ b/solution.py
@@ -17,9 +17,9 @@
 VMEM_BYTES = 44 * 1024 * 1024
 
 
-def cut_kernel(vec_ref, link_ref, keep_ref, send_ref, halo_ref, halo_send_ref, link_out_ref):
+def cut_kernel(vec_ref, link_ref, keep_ref, send_ref, halo_ref, link_out_ref):
     zh = lax.axis_index("zh")
-    for out_ref, other_ref, begin in ((keep_ref, halo_send_ref, zh), (send_ref, halo_ref, 1 - zh)):
+    for out_ref, other_ref, begin in ((keep_ref, send_ref.at[ROWS:], zh), (send_ref, halo_ref, 1 - zh)):
         for tile in range(TILES):
             at = pl.ds(pl.multiple_of(begin * HALF + tile * 128, 128), 128)
             for reim in range(2):
@@ -70,7 +70,7 @@
     return high, (value - high.astype(jnp.float32)).astype(jnp.bfloat16)
 
 
-def build_right(keep_ref, came_ref, halo_ref, halo_came_ref, zkeep_ref, zcame_ref, link_ref, right_ref):
+def build_right(keep_ref, came_ref, halo_ref, zkeep_ref, zcame_ref, link_ref, right_ref):
     lane = lax.broadcasted_iota(jnp.int32, (48, 128), 1)
 
     def load(first_ref, second_ref, reim, tile, color):
@@ -84,7 +84,8 @@
         else:
             field = reim * 3 + color
             row = field // 2 * 24
-            after = jnp.concatenate([halo_ref[row:row + 24], halo_came_ref[row:row + 24]], axis=0)
+            at = ROWS + row
+            after = jnp.concatenate([halo_ref[row:row + 24], came_ref[at:at + 24]], axis=0)
             after = pltpu.roll(after, 80 - LY * (field % 2), 1)
         return jnp.where(lane < 80, here, after)
 
@@ -114,7 +115,7 @@
         right_ref[row:row + 48, column:column + 128] = high
         right_ref[384 + row:384 + row + 48, column:column + 128] = low
 
-    for tile in range(TILES):
+    def build(tile):
         for color in range(3):
             for reim in range(2):
                 put(reim, 0, tile, color, load(keep_ref, came_ref, reim, tile, color))
@@ -134,45 +135,51 @@
                 put(0, direction + 1, tile, row, re)
                 put(1, direction + 1, tile, row, im)
 
-
-def multiply(blocks, phase_ref, right_ref, away_ref, stay_ref, high_ref, low_ref):
+    return build
+
+
+def multiply(blocks, phase_ref, right_ref, away_ref, stay_ref, high_ref, low_ref, build=None):
     count = len(blocks)
     rows = 24 * count
 
-    def make_left(tile, carry):
-        real = []
-        imag = []
-        for block in blocks:
-            if len(block) == 1:
-                real.append(block[0][pl.ds(pl.multiple_of(tile * 72, 8), 72)])
-                imag.append(block[0][pl.ds(pl.multiple_of(tile * 72 + 648, 8), 72)])
-            else:
-                real.append(block[0][pl.ds(pl.multiple_of(tile * 72, 8), 72)])
-                imag.append(block[1][pl.ds(pl.multiple_of(tile * 72, 8), 72)])
+    def make_left(tile):
         for index in range(4):
             cosv = phase_ref[tile, index:index + 1, :]
             sinv = phase_ref[tile, 4 + index:5 + index, :]
-            left_real = [a * cosv - b * sinv for a, b in zip(real, imag)]
-            left_imag = [-(a * sinv + b * cosv) for a, b in zip(real, imag)]
             for color in range(3):
-                value = jnp.concatenate(
-                    [part[color * 24:color * 24 + 24] for part in left_real + left_imag], axis=0
-                )
-                high, low = split(value)
-                column = pl.ds(pl.multiple_of(tile * 384 + color * 128, 128), 128)
-                high_ref[2 * rows * index:2 * rows * (index + 1), column] = high
-                low_ref[2 * rows * index:2 * rows * (index + 1), column] = low
-        return carry
-
-    lax.fori_loop(0, TILES, make_left, 0)
+                row = tile * 72 + color * 24
+                left_real = []
+                left_imag = []
+                for block in blocks:
+                    a = block[row:row + 24]
+                    b = block[row + 648:row + 672]
+                    left_real.append(a * cosv - b * sinv)
+                    left_imag.append(-(a * sinv + b * cosv))
+                high, low = split(jnp.concatenate(left_real + left_imag, axis=0))
+                column = tile * 384 + color * 128
+                high_ref[2 * rows * index:2 * rows * (index + 1), column:column + 128] = high
+                low_ref[2 * rows * index:2 * rows * (index + 1), column:column + 128] = low
+
+    def prepare(chunk):
+        for tile in range(3 * chunk, 3 * chunk + 3):
+            if build is not None:
+                build(tile)
+            make_left(tile)
 
     def times(left, right):
         return lax.dot_general(
             left, right, (((1,), (1,)), ((), ())), preferred_element_type=jnp.float32
         )
 
-    both = times(high_ref[...], right_ref[...])
-    total = both[:, :384] + both[:, 384:] + times(low_ref[...], right_ref[:384])
+    prepare(0)
+    total = None
+    for chunk in range(3):
+        if chunk < 2:
+            prepare(chunk + 1)
+        part = slice(chunk * HALF, (chunk + 1) * HALF)
+        both = times(high_ref[:, part], right_ref[:, part])
+        more = both[:, :384] + both[:, 384:] + times(low_ref[:, part], right_ref[:384, part])
+        total = more if total is None else total + more
     for index in range(4):
         out_ref = (away_ref, stay_ref)[index // 2]
         base = 2 * rows * index
@@ -185,21 +192,21 @@
                 out_ref[sub, :, column:column + 192] = product[reim][sub * 24:sub * 24 + 24]
 
 
-def own_kernel(keep, came, halo, halo_came, zkeep, zcame, link, phase, right, away, stay, high, low):
-    build_right(keep, came, halo, halo_came, zkeep, zcame, link, right)
-    multiply([(keep,), (came,)], phase, right, away, stay, high, low)
-
-
-def kept_kernel(after, before, far_real, far_imag, phase, right, away, stay, high, low):
-    multiply([(after,), (before,), (far_real, far_imag)], phase, right, away, stay, high, low)
+def own_kernel(keep, came, halo, zkeep, zcame, link, phase, right, away, stay, high, low):
+    build = build_right(keep, came, halo, zkeep, zcame, link, right)
+    multiply([keep, came], phase, right, away, stay, high, low, build)
+
+
+def kept_kernel(after, before, far, phase, right, away, stay, high, low):
+    multiply([after, before, far], phase, right, away, stay, high, low)
 
 
 def came_kernel(after, before, phase, right, away, stay, high, low):
-    multiply([(after,), (before,)], phase, right, away, stay, high, low)
-
-
-def far_kernel(far_real, far_imag, phase, right, away, stay, high, low):
-    multiply([(far_real, far_imag)], phase, right, away, stay, high, low)
+    multiply([after, before], phase, right, away, stay, high, low)
+
+
+def far_kernel(far, phase, right, away, stay, high, low):
+    multiply([far], phase, right, away, stay, high, low)
 
 
 def add_kernel(*refs):
@@ -255,7 +262,7 @@
     return [pl.BlockSpec(memory_space=pltpu.VMEM)] * count
 
 
-def call(kernel, name, outs, operands, scratch=(), scalars=0):
+def call(kernel, name, outs, operands, scratch=(), scalars=0, micros=1):
     out_shape = tuple(
         jax.ShapeDtypeStruct(shape, jnp.bfloat16 if shape == (768, DEPTH) else jnp.float32) for shape in outs
     )
@@ -266,6 +273,9 @@
         out_specs=tuple(vmem(len(outs))),
         scratch_shapes=list(scratch),
         compiler_params=pltpu.CompilerParams(vmem_limit_bytes=VMEM_BYTES),
+        cost_estimate=pl.CostEstimate(
+            flops=int(micros * 0.3e9), bytes_accessed=int(micros * 0.3 * 3.0e6), transcendentals=0
+        ),
         name=name,
     )(*operands)
 
@@ -281,37 +291,37 @@
 
 def local(eigvecs, links, momenta, directions):
     flat = (ROWS, 128)
-    keep, send, halo, halo_send, link = call(
-        cut_kernel, "cut", [flat, flat, (72, 128), (72, 128), (TILES, 56, 128)],
+    keep, send, halo, link = call(
+        cut_kernel, "cut", [flat, (ROWS + 72, 128), (72, 128), (TILES, 56, 128)],
         (eigvecs.reshape(144, 2304), links.reshape(54, 2304)),
     )
     came = along(send, "zh", 1)
-    halo_came = along(halo_send, "zh", 1)
     keep_after = along(keep, "x", -1)
     keep_before = along(keep, "x", 1)
     zkeep = along(keep, SITE, -1)
     phase, = call(phase_kernel, "phase", [(TILES, 8, 128)], (momenta,), (), 1)
-    keep_far = (along(keep_after[:648], "x", -1), along(keep_before[648:], "x", 1))
+    keep_far = along(keep, "x", 2)
+    came, keep_after, keep_before, keep_far = lax.optimization_barrier((came, keep_after, keep_before, keep_far))
     zcame = along(came, SITE, -1)
     came_after = along(came, "x", -1)
     came_before = along(came, "x", 1)
-    came_far = (along(came_after[:648], "x", -1), along(came_before[648:], "x", 1))
+    came_far = along(came, "x", 2)
 
     def parts(count):
         return [(count, 24, 768)] * 2
 
     right, away, stay = call(
         own_kernel, "own", [(768, DEPTH)] + parts(2),
-        (keep, came, halo, halo_came, zkeep, zcame, link, phase), left_scratch(2),
+        (keep, came, halo, zkeep, zcame, link, phase), left_scratch(2), 0, 9,
     )
     products = [(away, stay)]
     products.append(call(
-        kept_kernel, "kept", parts(3), (keep_after, keep_before, *keep_far, phase, right), left_scratch(3)
+        kept_kernel, "kept", parts(3), (keep_after, keep_before, keep_far, phase, right), left_scratch(3), 0, 8
     ))
     products.append(call(
-        came_kernel, "came", parts(2), (came_after, came_before, phase, right), left_scratch(2)
+        came_kernel, "came", parts(2), (came_after, came_before, phase, right), left_scratch(2), 0, 6
     ))
-    products.append(call(far_kernel, "far", parts(1), (*came_far, phase, right), left_scratch(1)))
+    products.append(call(far_kernel, "far", parts(1), (came_far, phase, right), left_scratch(1), 0, 4))
     terms = []
     for away, stay in products:
         terms += [stay, along(away, "core", 1)]

time: 134 us -> 122 us (0.910)
  starting transfers between devices: 43.9 us -> 21.3 us
  waiting for transfers between devices: 23.6 us -> 40.6 us
  Pallas kernels: 28.3 us -> 22.4 us
    ppermute x16 -> x13, starting transfers between devices: 43.9 us -> 21.3 us  [along(): lax.ppermute(value, axis, [(i, (i + step) % count) for i in range(count)])]
    ppermute x16 -> x13, waiting for transfers between devices: 23.6 us -> 40.6 us  [along(): lax.ppermute(value, axis, [(i, (i + step) % count) for i in range(count)])]
    pallas_call x9, Pallas kernels: 28.3 us -> 22.4 us  [call(): pl.pallas_call(kernel, out_shape=out_shape, in_specs=[pl.BlockSpec(memory...]
    all_to_all x1, blocking collectives: 20.5 us -> 16.9 us  [local(): mixed = lax.all_to_all(packed, ('zl', 'zh', 'core'), 0, 0)]
    all_to_all x1, blocking collectives: 13.6 us -> 17.1 us  [local(): lax.all_to_all(ready, 'y', 0, 0)]
  transfers between devices with their start and end apart: 16 -> 13, of which waited for: 5 -> 5; matrix products, arithmetic and copies ran while one was open for 0% -> 0% of each run, Pallas kernels for 20% -> 17%
where the time goes in v5:
time: 122 us
  waiting for transfers between devices  40.6 us (33%)
  blocking collectives  34 us (28%)
  Pallas kernels  22.4 us (18%)
  starting transfers between devices  21.3 us (17%)
  local copies, waits for them, and re-layouts  2.43 us (2%)
  other arithmetic  1.43 us (1%)
    ppermute x13, waiting for transfers between devices, along(): lax.ppermute(value, axis, [(i, (i + step) % count) for i in range(count)])  40.6 us
    pallas_call x9, Pallas kernels, call(): pl.pallas_call(kernel, out_shape=out_shape, in_specs=[pl.BlockSpec(memory...  22.4 us
    ppermute x13, starting transfers between devices, along(): lax.ppermute(value, axis, [(i, (i + step) % count) for i in range(count)])  21.3 us
    all_to_all x1, blocking collectives, local(): lax.all_to_all(ready, 'y', 0, 0)  17.1 us
    all_to_all x1, blocking collectives, local(): mixed = lax.all_to_all(packed, ('zl', 'zh', 'core'), 0, 0)  16.9 us
  transfers between devices with their start and end apart: 13, of which 5 were waited for; matrix products, arithmetic and copies ran while one was open for 0% of the time, Pallas kernels for 17%

profile of v5, /device:TPU:1, one launch (start us, length us, event | category | flops | bytes accessed | tf_op | source)
XLA Modules:
  0.0 122.3 jit_solution(7589625751636501524)
XLA Ops:
  0.0 0.0 copy-start.2
  0.0 1.5 %copy.6 = f32[2,3,24,1,2304]{4,2,3,1,0:T(8,128)S(1)} copy(f32[2,3,24,1,2304]{4,3,2,1,0:T(1,128)} %param.4) | data formatting | bytes 2654208
  1.5 0.0 copy-done.2
  1.5 1.4 %reduce = f32[3,2,3,3,2304]{4,3,2,1,0:T(4,128)S(1)} reduce(f32[3,2,3,3,1,2304]{5,4,3,2,1,0:T(1,128)S(1)} %copy-done.2, f32[]{:T(128)} %constant.2), dimensions={4}, to_apply=%param.5.reduce_sub_computation | reduce | bytes 995332 | tf_op args[1]
  2.9 0.0 copy-start
  2.9 0.2 reshape.7.link_ref
  3.2 0.2 cut.1
  3.4 7.8 %collective-permute-start = (f32[1368,128]{1,0:T(8,128)S(1)}, f32[1368,128]{1,0:T(8,128)S(1)}, u32[]{:S(2)}, u32[]{:S(2)}) collective-permute-start(f32[1368,128]{1,0:T(8,128)S(1)} %get-tuple-element.23), channel_id=1, source_target_pairs={{0,1},{1,0},{2,3},{3,2},{4,5},{5,4},{6,7},{7,6},{8,9},{9,8},{10,11... | collective-permute-start | bytes 2101256 | tf_op jit(solution)/shard_map/ppermute | solution.py:285
  11.2 2.5 %collective-permute-start.1 = (f32[1296,128]{1,0:T(8,128)S(1)}, f32[1296,128]{1,0:T(8,128)S(1)}, u32[]{:S(2)}, u32[]{:S(2)}) collective-permute-start(f32[1296,128]{1,0:T(8,128)S(1)} %get-tuple-element.22.keep), channel_id=1, source_target_pairs={{0,6},{2,0},{4,2},{6,4},{1,7},{3,1},{5,3},{7,5},{8,14},{10,8},{12,... | collective-permute-start | bytes 1990664 | tf_op jit(solution)/shard_map/ppermute | solution.py:285
  13.7 0.0 collective-permute-start.2
  13.7 1.7 %collective-permute-start.3 = (f32[1296,128]{1,0:T(8,128)S(1)}, f32[1296,128]{1,0:T(8,128)S(1)}, u32[]{:S(2)}, u32[]{:S(2)}) collective-permute-start(f32[1296,128]{1,0:T(8,128)S(1)} %get-tuple-element.22.keep), channel_id=1, source_target_pairs={{0,4},{2,6},{4,0},{6,2},{1,5},{3,7},{5,1},{7,3},{8,12},{10,14},{12... | collective-permute-start | bytes 1990664 | tf_op jit(solution)/shard_map/ppermute | solution.py:285
  15.4 12.3 %collective-permute-done.1.after = f32[1296,128]{1,0:T(8,128)S(1)} collective-permute-done((f32[1296,128]{1,0:T(8,128)S(1)}, f32[1296,128]{1,0:T(8,128)S(1)}, u32[]{:S(2)}, u32[]{:S(2)}) %collective-permute-start.1) | collective-permute-done | bytes 663584 | tf_op jit(solution)/shard_map/ppermute | solution.py:285
  27.7 3.3 %collective-permute-done.2.before = f32[1296,128]{1,0:T(8,128)S(1)} collective-permute-done((f32[1296,128]{1,0:T(8,128)S(1)}, f32[1296,128]{1,0:T(8,128)S(1)}, u32[]{:S(2)}, u32[]{:S(2)}) %collective-permute-start.2) | collective-permute-done | bytes 663584 | tf_op jit(solution)/shard_map/ppermute | solution.py:285
  31.0 12.4 %collective-permute-done.3.far = f32[1296,128]{1,0:T(8,128)S(1)} collective-permute-done((f32[1296,128]{1,0:T(8,128)S(1)}, f32[1296,128]{1,0:T(8,128)S(1)}, u32[]{:S(2)}, u32[]{:S(2)}) %collective-permute-start.3) | collective-permute-done | bytes 663584 | tf_op jit(solution)/shard_map/ppermute | solution.py:285
  43.3 0.0 collective-permute-done.came
  43.4 3.1 %collective-permute-start.5 = (f32[1368,128]{1,0:T(8,128)S(1)}, f32[1368,128]{1,0:T(8,128)S(1)}, u32[]{:S(2)}, u32[]{:S(2)}) collective-permute-start(f32[1368,128]{1,0:T(8,128)S(1)} %collective-permute-done.came), channel_id=1, source_target_pairs={{0,248},{8,0},{16,8},{24,16},{32,24},{40,32},{48,40},{56,48},{64,5... | collective-permute-start | bytes 2101256 | tf_op jit(solution)/shard_map/ppermute | solution.py:285
  46.4 1.4 %collective-permute-start.4 = (f32[1296,128]{1,0:T(8,128)S(1)}, f32[1296,128]{1,0:T(8,128)S(1)}, u32[]{:S(2)}, u32[]{:S(2)}) collective-permute-start(f32[1296,128]{1,0:T(8,128)S(1)} %get-tuple-element.22.keep), channel_id=1, source_target_pairs={{0,248},{8,0},{16,8},{24,16},{32,24},{40,32},{48,40},{56,48},{64,5... | collective-permute-start | bytes 1990664 | tf_op jit(solution)/shard_map/ppermute | solution.py:285
  47.8 0.0 collective-permute-start.8
  47.9 1.5 %collective-permute-start.9 = (f32[1368,128]{1,0:T(8,128)S(1)}, f32[1368,128]{1,0:T(8,128)S(1)}, u32[]{:S(2)}, u32[]{:S(2)}) collective-permute-start(f32[1368,128]{1,0:T(8,128)S(1)} %collective-permute-done.came), channel_id=1, source_target_pairs={{0,2},{2,4},{4,6},{6,0},{1,3},{3,5},{5,7},{7,1},{8,10},{10,12},{12... | collective-permute-start | bytes 2101256 | tf_op jit(solution)/shard_map/ppermute | solution.py:285
  49.3 1.5 %collective-permute-start.11 = (f32[1368,128]{1,0:T(8,128)S(1)}, f32[1368,128]{1,0:T(8,128)S(1)}, u32[]{:S(2)}, u32[]{:S(2)}) collective-permute-start(f32[1368,128]{1,0:T(8,128)S(1)} %collective-permute-done.came), channel_id=1, source_target_pairs={{0,4},{2,6},{4,0},{6,2},{1,5},{3,7},{5,1},{7,3},{8,12},{10,14},{12... | collective-permute-start | bytes 2101256 | tf_op jit(solution)/shard_map/ppermute | solution.py:285
  50.8 0.0 copy-done
  50.8 0.7 phase.1
  51.5 11.7 %collective-permute-done.4.zkeep = f32[1296,128]{1,0:T(8,128)S(1)} collective-permute-done((f32[1296,128]{1,0:T(8,128)S(1)}, f32[1296,128]{1,0:T(8,128)S(1)}, u32[]{:S(2)}, u32[]{:S(2)}) %collective-permute-start.4) | collective-permute-done | bytes 663584 | tf_op jit(solution)/shard_map/ppermute | solution.py:285
  63.2 0.0 collective-permute-done.5.zcame
  63.2 6.6 %own.1 = (bf16[768,3456]{1,0:T(8,128)(2,1)S(1)}, f32[2,24,768]{2,1,0:T(8,128)S(1)}, f32[2,24,768]{2,1,0:T(8,128)S(1)}) custom-call(f32[1296,128]{1,0:T(8,128)S(1)} %get-tuple-element.22.keep, f32[1368,128]{1,0:T(8,128)S(1)} %collective-permute-done.came, f32[72,128]{1,0:T(8,128)S(1)} %get-tuple-element.25.halo, ...), custom_call_target="tpu_custom_call" | custom-call | flops 2700000000 | bytes 8099999 | tf_op jit(solution)/shard_map/own/pallas_call | solution.py:269
  69.9 6.4 %kept.1 = (f32[3,24,768]{2,1,0:T(8,128)S(1)}, f32[3,24,768]{2,1,0:T(8,128)S(1)}) custom-call(f32[1296,128]{1,0:T(8,128)S(1)} %collective-permute-done.1.after, f32[1296,128]{1,0:T(8,128)S(1)} %collective-permute-done.2.before, f32[1296,128]{1,0:T(8,128)S(1)} %collective-permute-done.3.far, f32[9,8,128]{2,1,0:T(8,128)S(1)} %phase.1, ...), custom_call_target="tpu_custom_call" | custom-call | flops 2400000000 | bytes 7200000 | tf_op jit(solution)/shard_map/kept/pallas_call | solution.py:269
  76.3 0.7 collective-permute-start.7
  76.9 0.0 collective-permute-done.8.after
  76.9 0.0 collective-permute-done.9.before
  76.9 4.4 %came.1 = (f32[2,24,768]{2,1,0:T(8,128)S(1)}, f32[2,24,768]{2,1,0:T(8,128)S(1)}) custom-call(f32[1368,128]{1,0:T(8,128)S(1)} %collective-permute-done.8.after, f32[1368,128]{1,0:T(8,128)S(1)} %collective-permute-done.9.before, f32[9,8,128]{2,1,0:T(8,128)S(1)} %phase.1, bf16[768,3456]{1,0:T(8,128)(2,1)S(1)} %get-tuple-element.32.right), custom_call_target="tpu_custom_call" | custom-call | flops 1800000000 | bytes 5399999 | tf_op jit(solution)/shard_map/came/pallas_call | solution.py:269
  81.3 0.3 collective-permute-start.10
  81.6 0.3 collective-permute-start.6
  81.9 0.0 collective-permute-done.11.far
  81.9 3.0 %far.1 = (f32[1,24,768]{2,1,0:T(8,128)S(1)}, f32[1,24,768]{2,1,0:T(8,128)S(1)}) custom-call(f32[1368,128]{1,0:T(8,128)S(1)} %collective-permute-done.11.far, f32[9,8,128]{2,1,0:T(8,128)S(1)} %phase.1, bf16[768,3456]{1,0:T(8,128)(2,1)S(1)} %get-tuple-element.32.right), custom_call_target="tpu_custom_call" | custom-call | flops 1200000000 | bytes 3600000 | tf_op jit(solution)/shard_map/far/pallas_call | solution.py:269
  85.0 0.6 collective-permute-start.12
  85.6 0.9 collective-permute-done.12.refs_7_
  86.5 0.0 collective-permute-done.10.refs_5_
  86.5 0.0 collective-permute-done.6.refs_1_
  86.5 0.0 collective-permute-done.7.refs_3_
  86.5 0.1 add.2
  86.6 0.0 copy-start.1
  86.6 17.1 %all_to_all.10.part_ref = f32[4,48,768]{2,1,0:T(8,128)S(1)} all-to-all(f32[4,48,768]{2,1,0:T(8,128)S(1)} %add.2), channel_id=1, replica_groups=mesh['y'=4,'zl'=4,'core'=2,'x'=4,'zh'=2] {'y'}, dimensions={0} | all-to-all | bytes 1179648 | tf_op jit(solution)/shard_map/all_to_all | solution.py:329
  103.7 0.2 pack.1
  103.9 16.9 %all_to_all.11.part_ref = f32[16,8,384]{2,1,0:T(8,128)S(1)} all-to-all(f32[16,8,384]{2,1,0:T(8,128)S(1)} %pack.1), channel_id=1, replica_groups=mesh['y'=4,'zl'=4,'core'=2,'x'=4,'zh'=2] {'zl','zh','core'}, dimensions={0} | all-to-all | bytes 393216 | tf_op jit(solution)/shard_map/all_to_all | solution.py:330
  120.8 0.0 copy-done.1
  120.8 0.8 last.1
  121.6 0.7 copy.5
Async XLA Ops:
  0.0 1.5 %copy-start.2 = (f32[3,2,3,3,1,2304]{5,4,3,2,1,0:T(1,128)S(1)}, f32[3,2,3,3,1,2304]{5,4,3,2,1,0:T(1,128)}, u32[]{:S(2)}) copy-start(f32[3,2,3,3,1,2304]{5,4,3,2,1,0:T(1,128)} %param.5) | copy-start | bytes 1492996
  2.9 47.9 %copy-start = (s32[4,3]{1,0:T(4,128)S(1)}, s32[4,3]{1,0:T(4,128)}, u32[]{:S(2)}) copy-start(s32[4,3]{1,0:T(4,128)} %mom_ref.1) | copy-start | bytes 148
  3.4 40.0 %collective-permute-start = (f32[1368,128]{1,0:T(8,128)S(1)}, f32[1368,128]{1,0:T(8,128)S(1)}, u32[]{:S(2)}, u32[]{:S(2)}) collective-permute-start(f32[1368,128]{1,0:T(8,128)S(1)} %get-tuple-element.23), channel_id=1, source_target_pairs={{0,1},{1,0},{2,3},{3,2},{4,5},{5,4},{6,7},{7,6},{8,9},{9,8},{10,11... | collective-permute-start | bytes 2101256 | tf_op jit(solution)/shard_map/ppermute | solution.py:285
  11.2 16.5 %collective-permute-start.1 = (f32[1296,128]{1,0:T(8,128)S(1)}, f32[1296,128]{1,0:T(8,128)S(1)}, u32[]{:S(2)}, u32[]{:S(2)}) collective-permute-start(f32[1296,128]{1,0:T(8,128)S(1)} %get-tuple-element.22.keep), channel_id=1, source_target_pairs={{0,6},{2,0},{4,2},{6,4},{1,7},{3,1},{5,3},{7,5},{8,14},{10,8},{12,... | collective-permute-start | bytes 1990664 | tf_op jit(solution)/shard_map/ppermute | solution.py:285
  13.7 17.3 %collective-permute-start.2 = (f32[1296,128]{1,0:T(8,128)S(1)}, f32[1296,128]{1,0:T(8,128)S(1)}, u32[]{:S(2)}, u32[]{:S(2)}) collective-permute-start(f32[1296,128]{1,0:T(8,128)S(1)} %get-tuple-element.22.keep), channel_id=1, source_target_pairs={{0,2},{2,4},{4,6},{6,0},{1,3},{3,5},{5,7},{7,1},{8,10},{10,12},{12... | collective-permute-start | bytes 1990664 | tf_op jit(solution)/shard_map/ppermute | solution.py:285
  13.7 29.7 %collective-permute-start.3 = (f32[1296,128]{1,0:T(8,128)S(1)}, f32[1296,128]{1,0:T(8,128)S(1)}, u32[]{:S(2)}, u32[]{:S(2)}) collective-permute-start(f32[1296,128]{1,0:T(8,128)S(1)} %get-tuple-element.22.keep), channel_id=1, source_target_pairs={{0,4},{2,6},{4,0},{6,2},{1,5},{3,7},{5,1},{7,3},{8,12},{10,14},{12... | collective-permute-start | bytes 1990664 | tf_op jit(solution)/shard_map/ppermute | solution.py:285
  43.4 19.9 %collective-permute-start.5 = (f32[1368,128]{1,0:T(8,128)S(1)}, f32[1368,128]{1,0:T(8,128)S(1)}, u32[]{:S(2)}, u32[]{:S(2)}) collective-permute-start(f32[1368,128]{1,0:T(8,128)S(1)} %collective-permute-done.came), channel_id=1, source_target_pairs={{0,248},{8,0},{16,8},{24,16},{32,24},{40,32},{48,40},{56,48},{64,5... | collective-permute-start | bytes 2101256 | tf_op jit(solution)/shard_map/ppermute | solution.py:285
  46.4 16.8 %collective-permute-start.4 = (f32[1296,128]{1,0:T(8,128)S(1)}, f32[1296,128]{1,0:T(8,128)S(1)}, u32[]{:S(2)}, u32[]{:S(2)}) collective-permute-start(f32[1296,128]{1,0:T(8,128)S(1)} %get-tuple-element.22.keep), channel_id=1, source_target_pairs={{0,248},{8,0},{16,8},{24,16},{32,24},{40,32},{48,40},{56,48},{64,5... | collective-permute-start | bytes 1990664 | tf_op jit(solution)/shard_map/ppermute | solution.py:285
  47.8 29.1 %collective-permute-start.8 = (f32[1368,128]{1,0:T(8,128)S(1)}, f32[1368,128]{1,0:T(8,128)S(1)}, u32[]{:S(2)}, u32[]{:S(2)}) collective-permute-start(f32[1368,128]{1,0:T(8,128)S(1)} %collective-permute-done.came), channel_id=1, source_target_pairs={{0,6},{2,0},{4,2},{6,4},{1,7},{3,1},{5,3},{7,5},{8,14},{10,8},{12,... | collective-permute-start | bytes 2101256 | tf_op jit(solution)/shard_map/ppermute | solution.py:285
  47.9 29.1 %collective-permute-start.9 = (f32[1368,128]{1,0:T(8,128)S(1)}, f32[1368,128]{1,0:T(8,128)S(1)}, u32[]{:S(2)}, u32[]{:S(2)}) collective-permute-start(f32[1368,128]{1,0:T(8,128)S(1)} %collective-permute-done.came), channel_id=1, source_target_pairs={{0,2},{2,4},{4,6},{6,0},{1,3},{3,5},{5,7},{7,1},{8,10},{10,12},{12... | collective-permute-start | bytes 2101256 | tf_op jit(solution)/shard_map/ppermute | solution.py:285
  49.3 32.6 %collective-permute-start.11 = (f32[1368,128]{1,0:T(8,128)S(1)}, f32[1368,128]{1,0:T(8,128)S(1)}, u32[]{:S(2)}, u32[]{:S(2)}) collective-permute-start(f32[1368,128]{1,0:T(8,128)S(1)} %collective-permute-done.came), channel_id=1, source_target_pairs={{0,4},{2,6},{4,0},{6,2},{1,5},{3,7},{5,1},{7,3},{8,12},{10,14},{12... | collective-permute-start | bytes 2101256 | tf_op jit(solution)/shard_map/ppermute | solution.py:285
  76.3 10.2 %collective-permute-start.7 = (f32[3,24,768]{2,1,0:T(8,128)S(1)}, f32[3,24,768]{2,1,0:T(8,128)S(1)}, u32[]{:S(2)}, u32[]{:S(2)}) collective-permute-start(f32[3,24,768]{2,1,0:T(8,128)S(1)} %get-tuple-element.34), channel_id=1, source_target_pairs={{0,8},{8,0},{1,9},{9,1},{2,10},{10,2},{3,11},{11,3},{4,12},{12,4},... | collective-permute-start | bytes 663560 | tf_op jit(solution)/shard_map/ppermute | solution.py:285
  81.3 5.2 %collective-permute-start.10 = (f32[2,24,768]{2,1,0:T(8,128)S(1)}, f32[2,24,768]{2,1,0:T(8,128)S(1)}, u32[]{:S(2)}, u32[]{:S(2)}) collective-permute-start(f32[2,24,768]{2,1,0:T(8,128)S(1)} %get-tuple-element.36), channel_id=1, source_target_pairs={{0,8},{8,0},{1,9},{9,1},{2,10},{10,2},{3,11},{11,3},{4,12},{12,4},... | collective-permute-start | bytes 442376 | tf_op jit(solution)/shard_map/ppermute | solution.py:285
  81.6 4.9 %collective-permute-start.6 = (f32[2,24,768]{2,1,0:T(8,128)S(1)}, f32[2,24,768]{2,1,0:T(8,128)S(1)}, u32[]{:S(2)}, u32[]{:S(2)}) collective-permute-start(f32[2,24,768]{2,1,0:T(8,128)S(1)} %get-tuple-element.28), channel_id=1, source_target_pairs={{0,8},{8,0},{1,9},{9,1},{2,10},{10,2},{3,11},{11,3},{4,12},{12,4},... | collective-permute-start | bytes 442376 | tf_op jit(solution)/shard_map/ppermute | solution.py:285
  85.0 1.5 %collective-permute-start.12 = (f32[1,24,768]{2,1,0:T(8,128)S(1)}, f32[1,24,768]{2,1,0:T(8,128)S(1)}, u32[]{:S(2)}, u32[]{:S(2)}) collective-permute-start(f32[1,24,768]{2,1,0:T(8,128)S(1)} %get-tuple-element.38), channel_id=1, source_target_pairs={{0,8},{8,0},{1,9},{9,1},{2,10},{10,2},{3,11},{11,3},{4,12},{12,4},... | collective-permute-start | bytes 221192 | tf_op jit(solution)/shard_map/ppermute | solution.py:285
  86.6 34.2 %copy-start.1 = (s32[3]{0:T(128)S(1)}, s32[3]{0:T(128)}, u32[]{:S(2)}) copy-start(s32[3]{0:T(128)} %direction_ref.1) | copy-start | bytes 40

commit v6 on v5

--- a/solution.py
+++ b/solution.py
@@ -17,7 +17,7 @@
 VMEM_BYTES = 44 * 1024 * 1024
 
 
-def cut_kernel(vec_ref, link_ref, keep_ref, send_ref, halo_ref, link_out_ref):
+def cut_kernel(vec_ref, keep_ref, send_ref, halo_ref):
     zh = lax.axis_index("zh")
     for out_ref, other_ref, begin in ((keep_ref, send_ref.at[ROWS:], zh), (send_ref, halo_ref, 1 - zh)):
         for tile in range(TILES):
@@ -31,9 +31,12 @@
             even = vec_ref[pair * 48:pair * 48 + 24, at]
             odd = vec_ref[pair * 48 + 24:pair * 48 + 48, at]
             other_ref[pair * 24:pair * 24 + 24] = jnp.where(lane < LY, even, pltpu.roll(odd, LY, 1))
+
+def link_kernel(link_ref, out_ref):
+    zh = lax.axis_index("zh")
     for tile in range(TILES):
         at = pl.ds(pl.multiple_of(zh * HALF + tile * 128, 128), 128)
-        link_out_ref[tile, :54] = link_ref[:, at]
+        out_ref[tile, :54] = link_ref[:, at]
 
 
 def wrapped(value, period):
@@ -70,12 +73,37 @@
     return high, (value - high.astype(jnp.float32)).astype(jnp.bfloat16)
 
 
-def build_right(keep_ref, came_ref, halo_ref, zkeep_ref, zcame_ref, link_ref, right_ref):
+def load(first_ref, second_ref, reim, tile, color):
+    row = reim * 648 + tile * 72 + color * 24
+    return jnp.concatenate([first_ref[row:row + 24], second_ref[row:row + 24]], axis=0)
+
+
+def put(right_ref, fields, reim, k, tile, color, value):
+    row = (reim * fields + k) * 48
+    column = (tile * 3 + color) * 128
+    high, low = split(value)
+    right_ref[row:row + 48, column:column + 128] = high
+    right_ref[96 * fields + row:96 * fields + row + 48, column:column + 128] = low
+
+
+def transport(right_ref, fields, k, tile, far, link_ref, direction):
+    for row in range(3):
+        re = None
+        im = None
+        for column in range(3):
+            at = direction * 18 + row * 3 + column
+            ur = link_ref[tile, at:at + 1, :]
+            ui = link_ref[tile, at + 9:at + 10, :]
+            more_re = ur * far[0][column] - ui * far[1][column]
+            more_im = ur * far[1][column] + ui * far[0][column]
+            re = more_re if re is None else re + more_re
+            im = more_im if im is None else im + more_im
+        put(right_ref, fields, 0, k, tile, row, re)
+        put(right_ref, fields, 1, k, tile, row, im)
+
+
+def build_plane(keep_ref, came_ref, halo_ref, link_ref, right_ref):
     lane = lax.broadcasted_iota(jnp.int32, (48, 128), 1)
-
-    def load(first_ref, second_ref, reim, tile, color):
-        row = reim * 648 + tile * 72 + color * 24
-        return jnp.concatenate([first_ref[row:row + 24], second_ref[row:row + 24]], axis=0)
 
     def beyond_x(reim, tile, color):
         here = pltpu.roll(load(keep_ref, came_ref, reim, tile, color), 80, 1)
@@ -105,40 +133,26 @@
             value = jnp.where(lane == 127, after, value)
         return value
 
-    def beyond_z(reim, tile, color):
-        return load(zkeep_ref, zcame_ref, reim, tile, color)
-
-    def put(reim, k, tile, color, value):
-        row = reim * 192 + k * 48
-        column = (tile * 3 + color) * 128
-        high, low = split(value)
-        right_ref[row:row + 48, column:column + 128] = high
-        right_ref[384 + row:384 + row + 48, column:column + 128] = low
-
     def build(tile):
         for color in range(3):
             for reim in range(2):
-                put(reim, 0, tile, color, load(keep_ref, came_ref, reim, tile, color))
-        for direction, beyond in enumerate((beyond_x, beyond_y, beyond_z)):
+                put(right_ref, 3, reim, 0, tile, color, load(keep_ref, came_ref, reim, tile, color))
+        for direction, beyond in enumerate((beyond_x, beyond_y)):
             far = [[beyond(reim, tile, color) for color in range(3)] for reim in range(2)]
-            for row in range(3):
-                re = None
-                im = None
-                for column in range(3):
-                    at = direction * 18 + row * 3 + column
-                    ur = link_ref[tile, at:at + 1, :]
-                    ui = link_ref[tile, at + 9:at + 10, :]
-                    more_re = ur * far[0][column] - ui * far[1][column]
-                    more_im = ur * far[1][column] + ui * far[0][column]
-                    re = more_re if re is None else re + more_re
-                    im = more_im if im is None else im + more_im
-                put(0, direction + 1, tile, row, re)
-                put(1, direction + 1, tile, row, im)
+            transport(right_ref, 3, direction + 1, tile, far, link_ref, direction)
 
     return build
 
 
-def multiply(blocks, phase_ref, right_ref, away_ref, stay_ref, high_ref, low_ref, build=None):
+def build_z(zkeep_ref, zcame_ref, link_ref, right_ref):
+    def build(tile):
+        far = [[load(zkeep_ref, zcame_ref, reim, tile, color) for color in range(3)] for reim in range(2)]
+        transport(right_ref, 1, 0, tile, far, link_ref, 2)
+
+    return build
+
+
+def multiply(blocks, phase_ref, rights, first, away_ref, stay_ref, high_ref, low_ref, build=None, offset=0):
     count = len(blocks)
     rows = 24 * count
 
@@ -171,61 +185,96 @@
             left, right, (((1,), (1,)), ((), ())), preferred_element_type=jnp.float32
         )
 
+    def joined(parts):
+        return parts[0] if len(parts) == 1 else jnp.concatenate(parts, axis=0)
+
+    widths = [ref.shape[0] // 4 for ref in rights]
+    count_high = 2 * sum(widths)
     prepare(0)
     total = None
     for chunk in range(3):
         if chunk < 2:
             prepare(chunk + 1)
         part = slice(chunk * HALF, (chunk + 1) * HALF)
-        both = times(high_ref[:, part], right_ref[:, part])
-        more = both[:, :384] + both[:, 384:] + times(low_ref[:, part], right_ref[:384, part])
+        highs = [ref[:2 * width, part] for ref, width in zip(rights, widths)]
+        lows = [ref[2 * width:, part] for ref, width in zip(rights, widths)]
+        both = times(high_ref[:, part], joined(highs + lows))
+        more = both[:, :count_high] + both[:, count_high:] + times(low_ref[:, part], joined(highs))
         total = more if total is None else total + more
     for index in range(4):
         out_ref = (away_ref, stay_ref)[index // 2]
         base = 2 * rows * index
         top = total[base:base + rows]
         low = total[base + rows:base + 2 * rows]
-        product = (top[:, :192] - low[:, 192:], low[:, :192] + top[:, 192:])
-        for reim in range(2):
-            column = (2 * (index % 2) + reim) * 192
-            for sub in range(count):
-                out_ref[sub, :, column:column + 192] = product[reim][sub * 24:sub * 24 + 24]
-
-
-def own_kernel(keep, came, halo, zkeep, zcame, link, phase, right, away, stay, high, low):
-    build = build_right(keep, came, halo, zkeep, zcame, link, right)
-    multiply([keep, came], phase, right, away, stay, high, low, build)
-
-
-def kept_kernel(after, before, far, phase, right, away, stay, high, low):
-    multiply([after, before, far], phase, right, away, stay, high, low)
-
-
-def came_kernel(after, before, phase, right, away, stay, high, low):
-    multiply([after, before], phase, right, away, stay, high, low)
-
-
-def far_kernel(far, phase, right, away, stay, high, low):
-    multiply([far], phase, right, away, stay, high, low)
+        begin = 0
+        to = first * 48
+        for width in widths:
+            mid = begin + width
+            end = mid + width
+            product = (top[:, begin:mid] - low[:, mid:end], low[:, begin:mid] + top[:, mid:end])
+            for reim in range(2):
+                column = (2 * (index % 2) + reim) * 192 + to
+                for sub in range(count):
+                    out_ref[offset + sub, :, column:column + width] = product[reim][sub * 24:sub * 24 + 24]
+            begin = end
+            to += width
+
+
+def own_kernel(keep, came, halo, link, phase, right, away, stay, high, low):
+    build = build_plane(keep, came, halo, link, right)
+    multiply([keep, came], phase, (right,), 0, away, stay, high, low, build)
+
+
+def kept_kernel(after, before, far, zkeep, zcame, link, phase, right, zright, away, stay, high, low):
+    build = build_z(zkeep, zcame, link, zright)
+    multiply([after, before, far], phase, (right, zright), 0, away, stay, high, low, build)
+
+
+def forward_kernel(after, before, away, first, second):
+    first[...] = after[:648]
+    second[...] = before[648:ROWS]
+
+
+class Halves:
+    def __init__(self, real, imag):
+        self.parts = (real, imag)
+
+    def __getitem__(self, rows):
+        return self.parts[rows.start // 648][rows.start % 648:rows.start % 648 + 24]
+
+
+def came_kernel(
+    keep, came, after, before, own_away, own_stay, phase, right, zright,
+    away, stay, own_high, own_low, high, low,
+):
+    away[:2] = own_away[...]
+    stay[:2] = own_stay[...]
+    multiply([keep, came], phase, (zright,), 3, away, stay, own_high, own_low)
+    multiply([after, before], phase, (right, zright), 0, away, stay, high, low, offset=2)
+
+
+def far_kernel(real, imag, phase, right, zright, away, stay, high, low):
+    multiply([Halves(real, imag)], phase, (right, zright), 0, away, stay, high, low)
 
 
 def add_kernel(*refs):
     x = lax.axis_index("x")
+    y = lax.axis_index("y")
     zh = lax.axis_index("zh")
-    out_ref = refs[8]
-    order = (((0, 0), (0, 1)), ((1, 0), (3, 0), (2, 0)), ((1, 1), (3, 1)), ((2, 1),))
+    outs, held = refs[6:10], refs[10]
+    order = (((1, 0), (3, 0), (2, 0)), ((0, 0), (0, 1), (1, 1), (3, 1)), ((2, 1),))
     for call_at, blocks in enumerate(order):
         for sub, (distance, came) in enumerate(blocks):
-            to = lax.rem(x + distance, 4)
+            to = lax.rem(x + distance - y + 4, 4)
             half = 1 - zh if came else zh
-            out_ref[to, pl.ds(pl.multiple_of(half * 24, 8), 24)] = (
-                refs[2 * call_at][sub] + refs[2 * call_at + 1][sub]
-            )
-
-
-def pack_kernel(part_ref, out_ref):
+            held[to, pl.ds(pl.multiple_of(half * 24, 8), 24)] = refs[2 * call_at][sub] + refs[2 * call_at + 1][sub]
+    for step in range(4):
+        outs[step][...] = held[step]
+
+
+def pack_kernel(first, second, third, fourth, out_ref):
     zh = lax.axis_index("zh")
-    total = part_ref[0] + part_ref[1] + part_ref[2] + part_ref[3]
+    total = first[...] + second[...] + third[...] + fourth[...]
     for came in range(2):
         pieces = []
         for piece in range(16):
@@ -264,7 +313,7 @@
 
 def call(kernel, name, outs, operands, scratch=(), scalars=0, micros=1):
     out_shape = tuple(
-        jax.ShapeDtypeStruct(shape, jnp.bfloat16 if shape == (768, DEPTH) else jnp.float32) for shape in outs
+        jax.ShapeDtypeStruct(shape, jnp.bfloat16 if shape[-1] == DEPTH else jnp.float32) for shape in outs
     )
     return pl.pallas_call(
         kernel,
@@ -291,42 +340,52 @@
 
 def local(eigvecs, links, momenta, directions):
     flat = (ROWS, 128)
-    keep, send, halo, link = call(
-        cut_kernel, "cut", [flat, (ROWS + 72, 128), (72, 128), (TILES, 56, 128)],
-        (eigvecs.reshape(144, 2304), links.reshape(54, 2304)),
+    keep, send, halo = call(
+        cut_kernel, "cut", [flat, (ROWS + 72, 128), (72, 128)], (eigvecs.reshape(144, 2304),)
     )
     came = along(send, "zh", 1)
     keep_after = along(keep, "x", -1)
     keep_before = along(keep, "x", 1)
     zkeep = along(keep, SITE, -1)
     phase, = call(phase_kernel, "phase", [(TILES, 8, 128)], (momenta,), (), 1)
-    keep_far = along(keep, "x", 2)
-    came, keep_after, keep_before, keep_far = lax.optimization_barrier((came, keep_after, keep_before, keep_far))
+    link, = call(link_kernel, "link", [(TILES, 56, 128)], (links.reshape(54, 2304),))
+    later, link, phase = lax.optimization_barrier((keep, link, phase))
+    keep_far = along(later, "x", 2)
+    came, keep_after, keep_before, keep_far, zkeep = lax.optimization_barrier(
+        (came, keep_after, keep_before, keep_far, zkeep)
+    )
     zcame = along(came, SITE, -1)
     came_after = along(came, "x", -1)
     came_before = along(came, "x", 1)
-    came_far = along(came, "x", 2)
 
     def parts(count):
         return [(count, 24, 768)] * 2
 
-    right, away, stay = call(
-        own_kernel, "own", [(768, DEPTH)] + parts(2),
-        (keep, came, halo, zkeep, zcame, link, phase), left_scratch(2), 0, 9,
+    right, own_away, own_stay = call(
+        own_kernel, "own", [(576, DEPTH)] + parts(2), (keep, came, halo, link, phase), left_scratch(2), 0, 6,
+    )
+    zright, away, stay = call(
+        kept_kernel, "kept", [(192, DEPTH)] + parts(3),
+        (keep_after, keep_before, keep_far, zkeep, zcame, link, phase, right), left_scratch(3), 0, 6,
     )
     products = [(away, stay)]
+    half = (648, 128)
+    first, second = call(forward_kernel, "forward", [half, half], (came_after, came_before, away))
+    came_far = (along(first, "x", -1), along(second, "x", 1))
     products.append(call(
-        kept_kernel, "kept", parts(3), (keep_after, keep_before, keep_far, phase, right), left_scratch(3), 0, 8
+        came_kernel, "came", parts(4),
+        (keep, came, came_after, came_before, own_away, own_stay, phase, right, zright),
+        left_scratch(2) * 2, 0, 7,
     ))
     products.append(call(
-        came_kernel, "came", parts(2), (came_after, came_before, phase, right), left_scratch(2), 0, 6
+        far_kernel, "far", parts(1), (*came_far, phase, right, zright), left_scratch(1), 0, 3
     ))
-    products.append(call(far_kernel, "far", parts(1), (came_far, phase, right), left_scratch(1), 0, 4))
     terms = []
     for away, stay in products:
         terms += [stay, along(away, "core", 1)]
-    ready, = call(add_kernel, "add", [(4, 48, 768)], terms)
-    packed, = call(pack_kernel, "pack", [(16, 8, 384)], (lax.all_to_all(ready, "y", 0, 0),))
+    ready = call(add_kernel, "add", [(48, 768)] * 4, terms, [pltpu.VMEM((4, 48, 768), jnp.float32)])
+    sums = [ready[0]] + [along(ready[step], "y", step) for step in range(1, 4)]
+    packed, = call(pack_kernel, "pack", [(16, 8, 384)], sums)
     mixed = lax.all_to_all(packed, ("zl", "zh", "core"), 0, 0)
     return call(last_kernel, "last", [(4, 4, 2, 6, 24)], (directions, mixed), (), 1)[0]
 

time: 122 us -> 115 us (0.943)
  blocking collectives: 34 us -> 18 us
  starting transfers between devices: 21.3 us -> 29.1 us
  Pallas kernels: 22.4 us -> 24.9 us
  waiting for transfers between devices: 40.6 us -> 38.6 us
    all_to_all x1 -> x0, blocking collectives: 17.1 us -> none  [local(): lax.all_to_all(ready, 'y', 0, 0)]
    ppermute x13 -> x16, starting transfers between devices: 21.3 us -> 29.1 us  [along(): lax.ppermute(value, axis, [(i, (i + step) % count) for i in range(count)])]
    pallas_call x9 -> x11, Pallas kernels: 22.4 us -> 24.9 us  [call(): pl.pallas_call(kernel, out_shape=out_shape, in_specs=[pl.BlockSpec(memory...]
    ppermute x13 -> x16, waiting for transfers between devices: 40.6 us -> 38.6 us  [along(): lax.ppermute(value, axis, [(i, (i + step) % count) for i in range(count)])]
  transfers between devices with their start and end apart: 13 -> 16, of which waited for: 5 -> 8; matrix products, arithmetic and copies ran while one was open for 0% -> 1% of each run, Pallas kernels for 17% -> 21%
where the time goes in v6:
time: 115 us
  waiting for transfers between devices  38.6 us (34%)
  starting transfers between devices  29.1 us (25%)
  Pallas kernels  24.9 us (22%)
  blocking collectives  18 us (16%)
  local copies, waits for them, and re-layouts  2.75 us (2%)
  other arithmetic  1.47 us (1%)
    ppermute x16, waiting for transfers between devices, along(): lax.ppermute(value, axis, [(i, (i + step) % count) for i in range(count)])  38.6 us
    ppermute x16, starting transfers between devices, along(): lax.ppermute(value, axis, [(i, (i + step) % count) for i in range(count)])  29.1 us
    pallas_call x11, Pallas kernels, call(): pl.pallas_call(kernel, out_shape=out_shape, in_specs=[pl.BlockSpec(memory...  24.9 us
    all_to_all x1, blocking collectives, local(): mixed = lax.all_to_all(packed, ('zl', 'zh', 'core'), 0, 0)  18 us
  transfers between devices with their start and end apart: 16, of which 8 were waited for; matrix products, arithmetic and copies ran while one was open for 1% of the time, Pallas kernels for 21%

profile of v6, /device:TPU:1, one launch (start us, length us, event | category | flops | bytes accessed | tf_op | source)
XLA Modules:
  0.0 114.9 jit_solution(871775824309765296)
XLA Ops:
  0.0 1.4 %copy.6 = f32[2,3,24,1,2304]{4,2,3,1,0:T(8,128)S(1)} copy(f32[2,3,24,1,2304]{4,3,2,1,0:T(1,128)} %param.4) | data formatting | bytes 2654208
  1.4 0.0 copy-start.2
  1.4 0.1 cut.1
  1.6 7.8 %collective-permute-start = (f32[1368,128]{1,0:T(8,128)S(1)}, f32[1368,128]{1,0:T(8,128)S(1)}, u32[]{:S(2)}, u32[]{:S(2)}) collective-permute-start(f32[1368,128]{1,0:T(8,128)S(1)} %get-tuple-element.32), channel_id=1, source_target_pairs={{0,1},{1,0},{2,3},{3,2},{4,5},{5,4},{6,7},{7,6},{8,9},{9,8},{10,11... | collective-permute-start | bytes 2101256 | tf_op jit(solution)/shard_map/ppermute | solution.py:334
  9.4 0.0 copy-done.2
  9.4 1.5 %reduce = f32[3,2,3,3,2304]{4,3,2,1,0:T(4,128)S(1)} reduce(f32[3,2,3,3,1,2304]{5,4,3,2,1,0:T(1,128)S(1)} %copy-done.2, f32[]{:T(128)} %constant.2), dimensions={4}, to_apply=%param.5.reduce_sub_computation | reduce | bytes 995332 | tf_op args[1]
  10.9 0.0 copy-start
  10.9 0.2 reshape.7.link_ref
  11.2 0.4 copy-done
  11.6 0.7 phase.1
  12.3 2.8 %collective-permute-start.3 = (f32[1296,128]{1,0:T(8,128)S(1)}, f32[1296,128]{1,0:T(8,128)S(1)}, u32[]{:S(2)}, u32[]{:S(2)}) collective-permute-start(f32[1296,128]{1,0:T(8,128)S(1)} %get-tuple-element.34.keep), channel_id=1, source_target_pairs={{0,4},{2,6},{4,0},{6,2},{1,5},{3,7},{5,1},{7,3},{8,12},{10,14},{12... | collective-permute-start | bytes 1990664 | tf_op jit(solution)/shard_map/ppermute | solution.py:334
  15.1 0.9 collective-permute-start.1
  16.0 0.6 collective-permute-start.2
  16.6 1.8 %collective-permute-start.4 = (f32[1296,128]{1,0:T(8,128)S(1)}, f32[1296,128]{1,0:T(8,128)S(1)}, u32[]{:S(2)}, u32[]{:S(2)}) collective-permute-start(f32[1296,128]{1,0:T(8,128)S(1)} %get-tuple-element.34.keep), channel_id=1, source_target_pairs={{0,248},{8,0},{16,8},{24,16},{32,24},{40,32},{48,40},{56,48},{64,5... | collective-permute-start | bytes 1990664 | tf_op jit(solution)/shard_map/ppermute | solution.py:334
  18.4 11.0 %collective-permute-done.3.far = f32[1296,128]{1,0:T(8,128)S(1)} collective-permute-done((f32[1296,128]{1,0:T(8,128)S(1)}, f32[1296,128]{1,0:T(8,128)S(1)}, u32[]{:S(2)}, u32[]{:S(2)}) %collective-permute-start.3) | collective-permute-done | bytes 663584 | tf_op jit(solution)/shard_map/ppermute | solution.py:334
  29.4 14.6 %collective-permute-done.1.after = f32[1296,128]{1,0:T(8,128)S(1)} collective-permute-done((f32[1296,128]{1,0:T(8,128)S(1)}, f32[1296,128]{1,0:T(8,128)S(1)}, u32[]{:S(2)}, u32[]{:S(2)}) %collective-permute-start.1) | collective-permute-done | bytes 663584 | tf_op jit(solution)/shard_map/ppermute | solution.py:334
  44.0 0.9 collective-permute-done.2.before
  44.9 3.3 %collective-permute-done.4.zkeep = f32[1296,128]{1,0:T(8,128)S(1)} collective-permute-done((f32[1296,128]{1,0:T(8,128)S(1)}, f32[1296,128]{1,0:T(8,128)S(1)}, u32[]{:S(2)}, u32[]{:S(2)}) %collective-permute-start.4) | collective-permute-done | bytes 663584 | tf_op jit(solution)/shard_map/ppermute | solution.py:334
  48.2 0.0 collective-permute-done.came
  48.2 0.0 collective-permute-start.5
  48.2 2.5 %collective-permute-start.7 = (f32[1368,128]{1,0:T(8,128)S(1)}, f32[1368,128]{1,0:T(8,128)S(1)}, u32[]{:S(2)}, u32[]{:S(2)}) collective-permute-start(f32[1368,128]{1,0:T(8,128)S(1)} %collective-permute-done.came), channel_id=1, source_target_pairs={{0,6},{2,0},{4,2},{6,4},{1,7},{3,1},{5,3},{7,5},{8,14},{10,8},{12,... | collective-permute-start | bytes 2101256 | tf_op jit(solution)/shard_map/ppermute | solution.py:334
  50.7 0.0 collective-permute-start.8
  50.7 6.2 %own.1 = (bf16[576,3456]{1,0:T(8,128)(2,1)S(1)}, f32[2,24,768]{2,1,0:T(8,128)S(1)}, f32[2,24,768]{2,1,0:T(8,128)S(1)}) custom-call(f32[1296,128]{1,0:T(8,128)S(1)} %get-tuple-element.34.keep, f32[1368,128]{1,0:T(8,128)S(1)} %collective-permute-done.came, f32[72,128]{1,0:T(8,128)S(1)} %get-tuple-element.42.halo, f32[9,56,128]{2,1,0:T(8,128)S(1)} %link.1, ...), custom_call_target="tpu_custom_call" | custom-call | flops 1800000000 | bytes 5399999 | tf_op jit(solution)/shard_map/own/pallas_call | solution.py:318
  56.9 2.1 %collective-permute-done.5.zcame = f32[1368,128]{1,0:T(8,128)S(1)} collective-permute-done((f32[1368,128]{1,0:T(8,128)S(1)}, f32[1368,128]{1,0:T(8,128)S(1)}, u32[]{:S(2)}, u32[]{:S(2)}) %collective-permute-start.5) | collective-permute-done | bytes 700448 | tf_op jit(solution)/shard_map/ppermute | solution.py:334
  59.0 7.0 %kept.1 = (bf16[192,3456]{1,0:T(8,128)(2,1)S(1)}, f32[3,24,768]{2,1,0:T(8,128)S(1)}, f32[3,24,768]{2,1,0:T(8,128)S(1)}) custom-call(f32[1296,128]{1,0:T(8,128)S(1)} %collective-permute-done.1.after, f32[1296,128]{1,0:T(8,128)S(1)} %collective-permute-done.2.before, f32[1296,128]{1,0:T(8,128)S(1)} %collective-permute-done.3.far, ...), custom_call_target="tpu_custom_call" | custom-call | flops 1800000000 | bytes 5399999 | tf_op jit(solution)/shard_map/kept/pallas_call | solution.py:318
  66.0 0.0 collective-permute-done.7.after
  66.0 0.0 collective-permute-done.8.before
  66.1 2.8 %collective-permute-start.10 = (f32[648,128]{1,0:T(8,128)S(1)}, f32[648,128]{1,0:T(8,128)S(1)}, u32[]{:S(2)}, u32[]{:S(2)}) collective-permute-start(f32[648,128]{1,0:T(8,128)S(1)} %get-tuple-element.51), channel_id=1, source_target_pairs={{0,6},{2,0},{4,2},{6,4},{1,7},{3,1},{5,3},{7,5},{8,14},{10,8},{12,... | collective-permute-start | bytes 995336 | tf_op jit(solution)/shard_map/ppermute | solution.py:334
  68.8 0.0 collective-permute-start.11
  68.8 6.6 %came.1 = (f32[4,24,768]{2,1,0:T(8,128)S(1)}, f32[4,24,768]{2,1,0:T(8,128)S(1)}) custom-call(f32[1296,128]{1,0:T(8,128)S(1)} %get-tuple-element.34.keep, f32[1368,128]{1,0:T(8,128)S(1)} %collective-permute-done.came, f32[1368,128]{1,0:T(8,128)S(1)} %collective-permute-done.7.after, f32[1368,128]{1,0:T(8,128)S(1)} %collective-permute-done.8.before, ...), custom_call_target="tpu_custom_call" | custom-call | flops 2100000000 | bytes 6300000 | tf_op jit(solution)/shard_map/came/pallas_call | solution.py:318
  75.5 3.6 %collective-permute-start.9 = (f32[4,24,768]{2,1,0:T(8,128)S(1)}, f32[4,24,768]{2,1,0:T(8,128)S(1)}, u32[]{:S(2)}, u32[]{:S(2)}) collective-permute-start(f32[4,24,768]{2,1,0:T(8,128)S(1)} %get-tuple-element.50), channel_id=1, source_target_pairs={{0,8},{8,0},{1,9},{9,1},{2,10},{10,2},{3,11},{11,3},{4,12},{12,4},... | collective-permute-start | bytes 884744 | tf_op jit(solution)/shard_map/ppermute | solution.py:334
  79.1 0.1 collective-permute-start.6
  79.2 0.0 collective-permute-done.10.real
  79.2 0.0 collective-permute-done.11.imag
  79.2 3.0 %far.1 = (f32[1,24,768]{2,1,0:T(8,128)S(1)}, f32[1,24,768]{2,1,0:T(8,128)S(1)}) custom-call(f32[648,128]{1,0:T(8,128)S(1)} %collective-permute-done.10.real, f32[648,128]{1,0:T(8,128)S(1)} %collective-permute-done.11.imag, f32[9,8,128]{2,1,0:T(8,128)S(1)} %phase.1, bf16[576,3456]{1,0:T(8,128)(2,1)S(1)} %get-tuple-element.43.right, ...), custom_call_target="tpu_custom_call" | custom-call | flops 900000000 | bytes 2699999 | tf_op jit(solution)/shard_map/far/pallas_call | solution.py:318
  82.2 1.6 %collective-permute-start.12 = (f32[1,24,768]{2,1,0:T(8,128)S(1)}, f32[1,24,768]{2,1,0:T(8,128)S(1)}, u32[]{:S(2)}, u32[]{:S(2)}) collective-permute-start(f32[1,24,768]{2,1,0:T(8,128)S(1)} %get-tuple-element.54), channel_id=1, source_target_pairs={{0,8},{8,0},{1,9},{9,1},{2,10},{10,2},{3,11},{11,3},{4,12},{12,4},... | collective-permute-start | bytes 221192 | tf_op jit(solution)/shard_map/ppermute | solution.py:334
  83.8 0.0 collective-permute-done.6.refs_1_
  83.8 0.0 collective-permute-done.9.refs_3_
  83.8 0.9 collective-permute-done.12.refs_5_
  84.7 0.0 copy-start.1
  84.7 0.1 add.2
  84.8 0.9 collective-permute-start.13
  85.8 2.6 %collective-permute-start.14 = (f32[48,768]{1,0:T(8,128)S(1)}, f32[48,768]{1,0:T(8,128)S(1)}, u32[]{:S(2)}, u32[]{:S(2)}) collective-permute-start(f32[48,768]{1,0:T(8,128)S(1)} %get-tuple-element.57), channel_id=1, source_target_pairs={{0,128},{64,192},{128,0},{192,64},{1,129},{65,193},{129,1},{193,65... | collective-permute-start | bytes 442376 | tf_op jit(solution)/shard_map/ppermute | solution.py:334
  88.4 1.1 collective-permute-start.15
  89.5 1.7 %collective-permute-done.13.second = f32[48,768]{1,0:T(8,128)S(1)} collective-permute-done((f32[48,768]{1,0:T(8,128)S(1)}, f32[48,768]{1,0:T(8,128)S(1)}, u32[]{:S(2)}, u32[]{:S(2)}) %collective-permute-start.13) | collective-permute-done | bytes 147488 | tf_op jit(solution)/shard_map/ppermute | solution.py:334
  91.2 4.0 %collective-permute-done.14.third = f32[48,768]{1,0:T(8,128)S(1)} collective-permute-done((f32[48,768]{1,0:T(8,128)S(1)}, f32[48,768]{1,0:T(8,128)S(1)}, u32[]{:S(2)}, u32[]{:S(2)}) %collective-permute-start.14) | collective-permute-done | bytes 147488 | tf_op jit(solution)/shard_map/ppermute | solution.py:334
  95.2 0.0 collective-permute-done.15.fourth
  95.2 0.2 pack.1
  95.4 18.0 %all_to_all.5.part_ref = f32[16,8,384]{2,1,0:T(8,128)S(1)} all-to-all(f32[16,8,384]{2,1,0:T(8,128)S(1)} %pack.1), channel_id=1, replica_groups=mesh['y'=4,'zl'=4,'core'=2,'x'=4,'zh'=2] {'zl','zh','core'}, dimensions={0} | all-to-all | bytes 393216 | tf_op jit(solution)/shard_map/all_to_all | solution.py:389
  113.4 0.0 copy-done.1
  113.4 0.8 last.1
  114.2 0.7 copy.5
  (2 shorter events, 0.1 us)
Async XLA Ops:
  1.4 8.0 %copy-start.2 = (f32[3,2,3,3,1,2304]{5,4,3,2,1,0:T(1,128)S(1)}, f32[3,2,3,3,1,2304]{5,4,3,2,1,0:T(1,128)}, u32[]{:S(2)}) copy-start(f32[3,2,3,3,1,2304]{5,4,3,2,1,0:T(1,128)} %param.5) | copy-start | bytes 1492996
  1.6 46.6 %collective-permute-start = (f32[1368,128]{1,0:T(8,128)S(1)}, f32[1368,128]{1,0:T(8,128)S(1)}, u32[]{:S(2)}, u32[]{:S(2)}) collective-permute-start(f32[1368,128]{1,0:T(8,128)S(1)} %get-tuple-element.32), channel_id=1, source_target_pairs={{0,1},{1,0},{2,3},{3,2},{4,5},{5,4},{6,7},{7,6},{8,9},{9,8},{10,11... | collective-permute-start | bytes 2101256 | tf_op jit(solution)/shard_map/ppermute | solution.py:334
  10.9 0.7 copy-start
  12.3 17.1 %collective-permute-start.3 = (f32[1296,128]{1,0:T(8,128)S(1)}, f32[1296,128]{1,0:T(8,128)S(1)}, u32[]{:S(2)}, u32[]{:S(2)}) collective-permute-start(f32[1296,128]{1,0:T(8,128)S(1)} %get-tuple-element.34.keep), channel_id=1, source_target_pairs={{0,4},{2,6},{4,0},{6,2},{1,5},{3,7},{5,1},{7,3},{8,12},{10,14},{12... | collective-permute-start | bytes 1990664 | tf_op jit(solution)/shard_map/ppermute | solution.py:334
  15.1 28.9 %collective-permute-start.1 = (f32[1296,128]{1,0:T(8,128)S(1)}, f32[1296,128]{1,0:T(8,128)S(1)}, u32[]{:S(2)}, u32[]{:S(2)}) collective-permute-start(f32[1296,128]{1,0:T(8,128)S(1)} %get-tuple-element.34.keep), channel_id=1, source_target_pairs={{0,6},{2,0},{4,2},{6,4},{1,7},{3,1},{5,3},{7,5},{8,14},{10,8},{12,... | collective-permute-start | bytes 1990664 | tf_op jit(solution)/shard_map/ppermute | solution.py:334
  16.0 28.9 %collective-permute-start.2 = (f32[1296,128]{1,0:T(8,128)S(1)}, f32[1296,128]{1,0:T(8,128)S(1)}, u32[]{:S(2)}, u32[]{:S(2)}) collective-permute-start(f32[1296,128]{1,0:T(8,128)S(1)} %get-tuple-element.34.keep), channel_id=1, source_target_pairs={{0,2},{2,4},{4,6},{6,0},{1,3},{3,5},{5,7},{7,1},{8,10},{10,12},{12... | collective-permute-start | bytes 1990664 | tf_op jit(solution)/shard_map/ppermute | solution.py:334
  16.6 31.6 %collective-permute-start.4 = (f32[1296,128]{1,0:T(8,128)S(1)}, f32[1296,128]{1,0:T(8,128)S(1)}, u32[]{:S(2)}, u32[]{:S(2)}) collective-permute-start(f32[1296,128]{1,0:T(8,128)S(1)} %get-tuple-element.34.keep), channel_id=1, source_target_pairs={{0,248},{8,0},{16,8},{24,16},{32,24},{40,32},{48,40},{56,48},{64,5... | collective-permute-start | bytes 1990664 | tf_op jit(solution)/shard_map/ppermute | solution.py:334
  48.2 10.8 %collective-permute-start.5 = (f32[1368,128]{1,0:T(8,128)S(1)}, f32[1368,128]{1,0:T(8,128)S(1)}, u32[]{:S(2)}, u32[]{:S(2)}) collective-permute-start(f32[1368,128]{1,0:T(8,128)S(1)} %collective-permute-done.came), channel_id=1, source_target_pairs={{0,248},{8,0},{16,8},{24,16},{32,24},{40,32},{48,40},{56,48},{64,5... | collective-permute-start | bytes 2101256 | tf_op jit(solution)/shard_map/ppermute | solution.py:334
  48.2 17.8 %collective-permute-start.7 = (f32[1368,128]{1,0:T(8,128)S(1)}, f32[1368,128]{1,0:T(8,128)S(1)}, u32[]{:S(2)}, u32[]{:S(2)}) collective-permute-start(f32[1368,128]{1,0:T(8,128)S(1)} %collective-permute-done.came), channel_id=1, source_target_pairs={{0,6},{2,0},{4,2},{6,4},{1,7},{3,1},{5,3},{7,5},{8,14},{10,8},{12,... | collective-permute-start | bytes 2101256 | tf_op jit(solution)/shard_map/ppermute | solution.py:334
  50.7 15.3 %collective-permute-start.8 = (f32[1368,128]{1,0:T(8,128)S(1)}, f32[1368,128]{1,0:T(8,128)S(1)}, u32[]{:S(2)}, u32[]{:S(2)}) collective-permute-start(f32[1368,128]{1,0:T(8,128)S(1)} %collective-permute-done.came), channel_id=1, source_target_pairs={{0,2},{2,4},{4,6},{6,0},{1,3},{3,5},{5,7},{7,1},{8,10},{10,12},{12... | collective-permute-start | bytes 2101256 | tf_op jit(solution)/shard_map/ppermute | solution.py:334
  66.1 13.1 %collective-permute-start.10 = (f32[648,128]{1,0:T(8,128)S(1)}, f32[648,128]{1,0:T(8,128)S(1)}, u32[]{:S(2)}, u32[]{:S(2)}) collective-permute-start(f32[648,128]{1,0:T(8,128)S(1)} %get-tuple-element.51), channel_id=1, source_target_pairs={{0,6},{2,0},{4,2},{6,4},{1,7},{3,1},{5,3},{7,5},{8,14},{10,8},{12,... | collective-permute-start | bytes 995336 | tf_op jit(solution)/shard_map/ppermute | solution.py:334
  68.8 10.3 %collective-permute-start.11 = (f32[648,128]{1,0:T(8,128)S(1)}, f32[648,128]{1,0:T(8,128)S(1)}, u32[]{:S(2)}, u32[]{:S(2)}) collective-permute-start(f32[648,128]{1,0:T(8,128)S(1)} %get-tuple-element.52), channel_id=1, source_target_pairs={{0,2},{2,4},{4,6},{6,0},{1,3},{3,5},{5,7},{7,1},{8,10},{10,12},{12... | collective-permute-start | bytes 995336 | tf_op jit(solution)/shard_map/ppermute | solution.py:334
  75.5 8.4 %collective-permute-start.9 = (f32[4,24,768]{2,1,0:T(8,128)S(1)}, f32[4,24,768]{2,1,0:T(8,128)S(1)}, u32[]{:S(2)}, u32[]{:S(2)}) collective-permute-start(f32[4,24,768]{2,1,0:T(8,128)S(1)} %get-tuple-element.50), channel_id=1, source_target_pairs={{0,8},{8,0},{1,9},{9,1},{2,10},{10,2},{3,11},{11,3},{4,12},{12,4},... | collective-permute-start | bytes 884744 | tf_op jit(solution)/shard_map/ppermute | solution.py:334
  79.1 4.7 %collective-permute-start.6 = (f32[3,24,768]{2,1,0:T(8,128)S(1)}, f32[3,24,768]{2,1,0:T(8,128)S(1)}, u32[]{:S(2)}, u32[]{:S(2)}) collective-permute-start(f32[3,24,768]{2,1,0:T(8,128)S(1)} %get-tuple-element.45.away), channel_id=1, source_target_pairs={{0,8},{8,0},{1,9},{9,1},{2,10},{10,2},{3,11},{11,3},{4,12},{12,4},... | collective-permute-start | bytes 663560 | tf_op jit(solution)/shard_map/ppermute | solution.py:334
  82.2 2.5 %collective-permute-start.12 = (f32[1,24,768]{2,1,0:T(8,128)S(1)}, f32[1,24,768]{2,1,0:T(8,128)S(1)}, u32[]{:S(2)}, u32[]{:S(2)}) collective-permute-start(f32[1,24,768]{2,1,0:T(8,128)S(1)} %get-tuple-element.54), channel_id=1, source_target_pairs={{0,8},{8,0},{1,9},{9,1},{2,10},{10,2},{3,11},{11,3},{4,12},{12,4},... | collective-permute-start | bytes 221192 | tf_op jit(solution)/shard_map/ppermute | solution.py:334
  84.7 28.6 %copy-start.1 = (s32[3]{0:T(128)S(1)}, s32[3]{0:T(128)}, u32[]{:S(2)}) copy-start(s32[3]{0:T(128)} %direction_ref.1) | copy-start | bytes 40
  84.8 6.4 %collective-permute-start.13 = (f32[48,768]{1,0:T(8,128)S(1)}, f32[48,768]{1,0:T(8,128)S(1)}, u32[]{:S(2)}, u32[]{:S(2)}) collective-permute-start(f32[48,768]{1,0:T(8,128)S(1)} %get-tuple-element.56), channel_id=1, source_target_pairs={{0,64},{64,128},{128,192},{192,0},{1,65},{65,129},{129,193},{193,1... | collective-permute-start | bytes 442376 | tf_op jit(solution)/shard_map/ppermute | solution.py:334
  85.8 9.4 %collective-permute-start.14 = (f32[48,768]{1,0:T(8,128)S(1)}, f32[48,768]{1,0:T(8,128)S(1)}, u32[]{:S(2)}, u32[]{:S(2)}) collective-permute-start(f32[48,768]{1,0:T(8,128)S(1)} %get-tuple-element.57), channel_id=1, source_target_pairs={{0,128},{64,192},{128,0},{192,64},{1,129},{65,193},{129,1},{193,65... | collective-permute-start | bytes 442376 | tf_op jit(solution)/shard_map/ppermute | solution.py:334
  88.4 6.8 %collective-permute-start.15 = (f32[48,768]{1,0:T(8,128)S(1)}, f32[48,768]{1,0:T(8,128)S(1)}, u32[]{:S(2)}, u32[]{:S(2)}) collective-permute-start(f32[48,768]{1,0:T(8,128)S(1)} %get-tuple-element.58), channel_id=1, source_target_pairs={{0,192},{64,0},{128,64},{192,128},{1,193},{65,1},{129,65},{193,129... | collective-permute-start | bytes 442376 | tf_op jit(solution)/shard_map/ppermute | solution.py:334

commit v7 on v6

--- a/solution.py
+++ b/solution.py
@@ -14,7 +14,7 @@
 ROWS = 1296
 DEPTH = 3456
 SITE = ("y", "zl", "core")
-VMEM_BYTES = 44 * 1024 * 1024
+VMEM_BYTES = 26 * 1024 * 1024
 
 
 def cut_kernel(vec_ref, keep_ref, send_ref, halo_ref):
@@ -190,10 +190,11 @@
 
     widths = [ref.shape[0] // 4 for ref in rights]
     count_high = 2 * sum(widths)
-    prepare(0)
+    if blocks[0] is not None:
+        prepare(0)
     total = None
     for chunk in range(3):
-        if chunk < 2:
+        if chunk < 2 and blocks[0] is not None:
             prepare(chunk + 1)
         part = slice(chunk * HALF, (chunk + 1) * HALF)
         highs = [ref[:2 * width, part] for ref, width in zip(rights, widths)]
@@ -225,9 +226,23 @@
     multiply([keep, came], phase, (right,), 0, away, stay, high, low, build)
 
 
-def kept_kernel(after, before, far, zkeep, zcame, link, phase, right, zright, away, stay, high, low):
+def kept_kernel(after, before, real, imag, phase, right, away, stay, high, low):
+    multiply([after, before, Halves(real, imag)], phase, (right,), 0, away, stay, high, low)
+
+
+def z_kernel(
+    own_away, own_stay, own_high, own_low, kept_away, kept_stay, kept_high, kept_low,
+    zkeep, zcame, link, zright, away, stay,
+):
+    away[:2] = own_away[...]
+    away[2:] = kept_away[...]
+    stay[:2] = own_stay[...]
+    stay[2:] = kept_stay[...]
     build = build_z(zkeep, zcame, link, zright)
-    multiply([after, before, far], phase, (right, zright), 0, away, stay, high, low, build)
+    for tile in range(TILES):
+        build(tile)
+    multiply([None] * 2, None, (zright,), 3, away, stay, own_high, own_low)
+    multiply([None] * 3, None, (zright,), 3, away, stay, kept_high, kept_low, offset=2)
 
 
 def forward_kernel(after, before, away, first, second):
@@ -243,14 +258,8 @@
         return self.parts[rows.start // 648][rows.start % 648:rows.start % 648 + 24]
 
 
-def came_kernel(
-    keep, came, after, before, own_away, own_stay, phase, right, zright,
-    away, stay, own_high, own_low, high, low,
-):
-    away[:2] = own_away[...]
-    stay[:2] = own_stay[...]
-    multiply([keep, came], phase, (zright,), 3, away, stay, own_high, own_low)
-    multiply([after, before], phase, (right, zright), 0, away, stay, high, low, offset=2)
+def came_kernel(after, before, phase, right, zright, away, stay, high, low):
+    multiply([after, before], phase, (right, zright), 0, away, stay, high, low)
 
 
 def far_kernel(real, imag, phase, right, zright, away, stay, high, low):
@@ -262,7 +271,7 @@
     y = lax.axis_index("y")
     zh = lax.axis_index("zh")
     outs, held = refs[6:10], refs[10]
-    order = (((1, 0), (3, 0), (2, 0)), ((0, 0), (0, 1), (1, 1), (3, 1)), ((2, 1),))
+    order = (((0, 0), (0, 1), (1, 0), (3, 0), (2, 0)), ((1, 1), (3, 1)), ((2, 1),))
     for call_at, blocks in enumerate(order):
         for sub, (distance, came) in enumerate(blocks):
             to = lax.rem(x + distance - y + 4, 4)
@@ -284,10 +293,9 @@
         half = 1 - zh if came else zh
         for zl in range(4):
             for core in range(2):
-                begin = zl * 12 + core * 6
-                to = zl * 4 + half * 2 + core
-                out_ref[to, :6] = packed[begin:begin + 6]
-                out_ref[to, 6:] = jnp.zeros((2, 384), jnp.float32)
+                for row in range(6):
+                    at = zl * 12 + core * 6 + row
+                    out_ref[zl * 4 + half * 2 + core, :, row * 384:(row + 1) * 384] = packed[at:at + 1]
 
 
 def last_kernel(direction_ref, part_ref, out_ref):
@@ -295,7 +303,7 @@
         total = part_ref[core]
         for source in range(1, 8):
             total = total + part_ref[2 * source + core]
-        total = total[:6]
+        total = jnp.concatenate([total[:, row * 384:(row + 1) * 384] for row in range(6)], axis=0)
         for p in range(2):
             for reim in range(2):
                 begin = p * 192 + reim * 96
@@ -346,36 +354,37 @@
     came = along(send, "zh", 1)
     keep_after = along(keep, "x", -1)
     keep_before = along(keep, "x", 1)
-    zkeep = along(keep, SITE, -1)
     phase, = call(phase_kernel, "phase", [(TILES, 8, 128)], (momenta,), (), 1)
     link, = call(link_kernel, "link", [(TILES, 56, 128)], (links.reshape(54, 2304),))
-    later, link, phase = lax.optimization_barrier((keep, link, phase))
-    keep_far = along(later, "x", 2)
-    came, keep_after, keep_before, keep_far, zkeep = lax.optimization_barrier(
-        (came, keep_after, keep_before, keep_far, zkeep)
+    first, second, link, phase = lax.optimization_barrier((keep_after[:648], keep_before[648:], link, phase))
+    keep_far = (along(first, "x", -1), along(second, "x", 1))
+    came, keep_after, keep_before, keep_far, later = lax.optimization_barrier(
+        (came, keep_after, keep_before, keep_far, keep)
     )
     zcame = along(came, SITE, -1)
+    zkeep = along(later, SITE, -1)
     came_after = along(came, "x", -1)
     came_before = along(came, "x", 1)
 
     def parts(count):
         return [(count, 24, 768)] * 2
 
-    right, own_away, own_stay = call(
-        own_kernel, "own", [(576, DEPTH)] + parts(2), (keep, came, halo, link, phase), left_scratch(2), 0, 6,
-    )
+    right, *own = call(
+        own_kernel, "own", [(576, DEPTH)] + parts(2) + [(384, DEPTH)] * 2, (keep, came, halo, link, phase), (), 0, 6,
+    )
+    kept = call(
+        kept_kernel, "kept", parts(3) + [(576, DEPTH)] * 2,
+        (keep_after, keep_before, *keep_far, phase, right), (), 0, 6,
+    )
+    half = (648, 128)
+    first, second = call(forward_kernel, "forward", [half, half], (came_after, came_before, kept[0]))
+    came_far = (along(first, "x", -1), along(second, "x", 1))
     zright, away, stay = call(
-        kept_kernel, "kept", [(192, DEPTH)] + parts(3),
-        (keep_after, keep_before, keep_far, zkeep, zcame, link, phase, right), left_scratch(3), 0, 6,
+        z_kernel, "zfield", [(192, DEPTH)] + parts(5), (*own, *kept, zkeep, zcame, link), (), 0, 5
     )
     products = [(away, stay)]
-    half = (648, 128)
-    first, second = call(forward_kernel, "forward", [half, half], (came_after, came_before, away))
-    came_far = (along(first, "x", -1), along(second, "x", 1))
     products.append(call(
-        came_kernel, "came", parts(4),
-        (keep, came, came_after, came_before, own_away, own_stay, phase, right, zright),
-        left_scratch(2) * 2, 0, 7,
+        came_kernel, "came", parts(2), (came_after, came_before, phase, right, zright), left_scratch(2), 0, 4,
     ))
     products.append(call(
         far_kernel, "far", parts(1), (*came_far, phase, right, zright), left_scratch(1), 0, 3
@@ -385,7 +394,7 @@
         terms += [stay, along(away, "core", 1)]
     ready = call(add_kernel, "add", [(48, 768)] * 4, terms, [pltpu.VMEM((4, 48, 768), jnp.float32)])
     sums = [ready[0]] + [along(ready[step], "y", step) for step in range(1, 4)]
-    packed, = call(pack_kernel, "pack", [(16, 8, 384)], sums)
+    packed, = call(pack_kernel, "pack", [(16, 1, 2304)], sums)
     mixed = lax.all_to_all(packed, ("zl", "zh", "core"), 0, 0)
     return call(last_kernel, "last", [(4, 4, 2, 6, 24)], (directions, mixed), (), 1)[0]
 

time: 115 us -> 111 us (0.965)
  waiting for transfers between devices: 38.6 us -> 21.1 us
  starting transfers between devices: 29.1 us -> 35.7 us
  Pallas kernels: 24.9 us -> 28.1 us
  blocking collectives: 18 us -> 19.8 us
    ppermute x16 -> x17, waiting for transfers between devices: 38.6 us -> 21.1 us  [along(): lax.ppermute(value, axis, [(i, (i + step) % count) for i in range(count)])]
    ppermute x16 -> x17, starting transfers between devices: 29.1 us -> 35.7 us  [along(): lax.ppermute(value, axis, [(i, (i + step) % count) for i in range(count)])]
    pallas_call x11 -> x12, Pallas kernels: 24.9 us -> 28.1 us  [call(): pl.pallas_call(kernel, out_shape=out_shape, in_specs=[pl.BlockSpec(memory...]
    all_to_all x1, blocking collectives: 18 us -> 19.8 us  [local(): mixed = lax.all_to_all(packed, ('zl', 'zh', 'core'), 0, 0)]
  transfers between devices with their start and end apart: 16 -> 17, of which waited for: 8 -> 8; matrix products, arithmetic and copies ran while one was open for 1% -> 3% of each run, Pallas kernels for 21% -> 24%
where the time goes in v7:
time: 111 us
  starting transfers between devices  35.7 us (32%)
  Pallas kernels  28.1 us (25%)
  waiting for transfers between devices  21.1 us (19%)
  blocking collectives  19.8 us (18%)
  local copies, waits for them, and re-layouts  3.56 us (3%)
  other arithmetic  2.35 us (2%)
    ppermute x17, starting transfers between devices, along(): lax.ppermute(value, axis, [(i, (i + step) % count) for i in range(count)])  35.7 us
    pallas_call x12, Pallas kernels, call(): pl.pallas_call(kernel, out_shape=out_shape, in_specs=[pl.BlockSpec(memory...  28.1 us
    ppermute x17, waiting for transfers between devices, along(): lax.ppermute(value, axis, [(i, (i + step) % count) for i in range(count)])  21.1 us
    all_to_all x1, blocking collectives, local(): mixed = lax.all_to_all(packed, ('zl', 'zh', 'core'), 0, 0)  19.8 us
    unnamed x1, other arithmetic  2.35 us
  transfers between devices with their start and end apart: 17, of which 8 were waited for; matrix products, arithmetic and copies ran while one was open for 3% of the time, Pallas kernels for 24%

profile of v7, /device:TPU:1, one launch (start us, length us, event | category | flops | bytes accessed | tf_op | source)
XLA Modules:
  0.0 110.8 jit_solution(14692507465414998737)
XLA Ops:
  0.0 0.0 copy-start.2
  0.0 1.5 %copy.6 = f32[2,3,24,1,2304]{4,2,3,1,0:T(8,128)S(1)} copy(f32[2,3,24,1,2304]{4,3,2,1,0:T(1,128)} %param.4) | data formatting | bytes 2654208
  1.5 0.0 copy-start
  1.5 1.0 cut.1
  2.4 3.3 %collective-permute-start.1 = (f32[1296,128]{1,0:T(8,128)}, f32[1296,128]{1,0:T(8,128)S(1)}, u32[]{:S(2)}, u32[]{:S(2)}) collective-permute-start(f32[1296,128]{1,0:T(8,128)} %get-tuple-element.61.keep), channel_id=1, source_target_pairs={{0,6},{2,0},{4,2},{6,4},{1,7},{3,1},{5,3},{7,5},{8,14},{10,8},{12,... | collective-permute-start | bytes 1990664 | tf_op jit(solution)/shard_map/ppermute | solution.py:342
  5.7 0.0 collective-permute-start.2
  5.8 6.9 %collective-permute-start = (f32[1368,128]{1,0:T(8,128)S(1)}, f32[1368,128]{1,0:T(8,128)S(1)}, u32[]{:S(2)}, u32[]{:S(2)}) collective-permute-start(f32[1368,128]{1,0:T(8,128)S(1)} %get-tuple-element.41), channel_id=1, source_target_pairs={{0,1},{1,0},{2,3},{3,2},{4,5},{5,4},{6,7},{7,6},{8,9},{9,8},{10,11... | collective-permute-start | bytes 2101256 | tf_op jit(solution)/shard_map/ppermute | solution.py:342
  12.7 0.0 copy-done.2
  12.7 2.3 %reduce = f32[3,2,3,3,2304]{4,3,2,1,0:T(4,128)} reduce(f32[3,2,3,3,1,2304]{5,4,3,2,1,0:T(1,128)S(1)} %copy-done.2, f32[]{:T(128)} %constant.2), dimensions={4}, to_apply=%param.5.reduce_sub_computation | reduce | bytes 995332 | tf_op args[1]
  15.0 1.3 %reshape.7.link_ref = f32[54,2304]{1,0:T(8,128)S(1)} reshape(f32[3,2,3,3,2304]{4,3,2,1,0:T(4,128)} %reduce) | data formatting | bytes 995328 | tf_op jit(solution)/shard_map/reshape | solution.py:358
  16.4 0.0 copy-done
  16.4 0.7 phase.1
  17.1 2.5 %collective-permute-done.1.after = f32[1296,128]{1,0:T(8,128)S(1)} collective-permute-done((f32[1296,128]{1,0:T(8,128)}, f32[1296,128]{1,0:T(8,128)S(1)}, u32[]{:S(2)}, u32[]{:S(2)}) %collective-permute-start.1) | collective-permute-done | bytes 663584 | tf_op jit(solution)/shard_map/ppermute | solution.py:342
  19.7 3.0 %collective-permute-done.2.before = f32[1296,128]{1,0:T(8,128)S(1)} collective-permute-done((f32[1296,128]{1,0:T(8,128)}, f32[1296,128]{1,0:T(8,128)S(1)}, u32[]{:S(2)}, u32[]{:S(2)}) %collective-permute-start.2) | collective-permute-done | bytes 663584 | tf_op jit(solution)/shard_map/ppermute | solution.py:342
  22.7 0.4 collective-permute-start.3
  23.1 1.1 collective-permute-start.4
  24.2 6.9 %collective-permute-done.came = f32[1368,128]{1,0:T(8,128)S(1)} collective-permute-done((f32[1368,128]{1,0:T(8,128)S(1)}, f32[1368,128]{1,0:T(8,128)S(1)}, u32[]{:S(2)}, u32[]{:S(2)}) %collective-permute-start) | collective-permute-done | bytes 700448 | tf_op jit(solution)/shard_map/ppermute | solution.py:342
  31.1 0.0 collective-permute-done.3.real
  31.1 0.7 collective-permute-done.4.imag
  31.8 1.7 %collective-permute-start.8 = (f32[1368,128]{1,0:T(8,128)S(1)}, f32[1368,128]{1,0:T(8,128)S(1)}, u32[]{:S(2)}, u32[]{:S(2)}) collective-permute-start(f32[1368,128]{1,0:T(8,128)S(1)} %collective-permute-done.came), channel_id=1, source_target_pairs={{0,6},{2,0},{4,2},{6,4},{1,7},{3,1},{5,3},{7,5},{8,14},{10,8},{12,... | collective-permute-start | bytes 2101256 | tf_op jit(solution)/shard_map/ppermute | solution.py:342
  33.4 0.0 collective-permute-start.9
  33.4 12.5 %collective-permute-start.6 = (f32[1368,128]{1,0:T(8,128)S(1)}, f32[1368,128]{1,0:T(8,128)S(1)}, u32[]{:S(2)}, u32[]{:S(2)}) collective-permute-start(f32[1368,128]{1,0:T(8,128)S(1)} %collective-permute-done.came), channel_id=1, source_target_pairs={{0,248},{8,0},{16,8},{24,16},{32,24},{40,32},{48,40},{56,48},{64,5... | collective-permute-start | bytes 2101256 | tf_op jit(solution)/shard_map/ppermute | solution.py:342
  46.0 0.0 collective-permute-start.5
  46.0 7.3 %own.1 = (bf16[576,3456]{1,0:T(8,128)(2,1)S(1)}, f32[2,24,768]{2,1,0:T(8,128)S(1)}, f32[2,24,768]{2,1,0:T(8,128)S(1)}, bf16[384,3456]{1,0:T(8,128)(2,1)S(1)}, bf16[384,3456]{1,0:T(8,128)(2,1)S(1)}) custom-call(f32[1296,128]{1,0:T(8,128)} %get-tuple-element.61.keep, f32[1368,128]{1,0:T(8,128)S(1)} %collective-permute-done.came, ...), custom_call_target="tpu_custom_call" | custom-call | flops 1800000000 | bytes 5399999 | tf_op jit(solution)/shard_map/own/pallas_call | solution.py:326
  53.3 6.4 %kept.1 = (f32[3,24,768]{2,1,0:T(8,128)S(1)}, f32[3,24,768]{2,1,0:T(8,128)S(1)}, bf16[576,3456]{1,0:T(8,128)(2,1)S(1)}, bf16[576,3456]{1,0:T(8,128)(2,1)S(1)}) custom-call(f32[1296,128]{1,0:T(8,128)S(1)} %collective-permute-done.1.after, f32[1296,128]{1,0:T(8,128)S(1)} %collective-permute-done.2.before, f32[648,128]{1,0:T(8,128)S(1)} %collective-permute-done.3.real, ...), custom_call_target="tpu_custom_call" | custom-call | flops 1800000000 | bytes 5399999 | tf_op jit(solution)/shard_map/kept/pallas_call | solution.py:326
  59.7 0.0 collective-permute-done.8.after
  59.7 0.0 collective-permute-done.9.before
  59.7 3.0 %collective-permute-start.11 = (f32[648,128]{1,0:T(8,128)S(1)}, f32[648,128]{1,0:T(8,128)S(1)}, u32[]{:S(2)}, u32[]{:S(2)}) collective-permute-start(f32[648,128]{1,0:T(8,128)S(1)} %get-tuple-element.67), channel_id=1, source_target_pairs={{0,6},{2,0},{4,2},{6,4},{1,7},{3,1},{5,3},{7,5},{8,14},{10,8},{12,... | collective-permute-start | bytes 995336 | tf_op jit(solution)/shard_map/ppermute | solution.py:342
  62.8 0.0 collective-permute-start.12
  62.8 1.5 %collective-permute-done.5.zkeep = f32[1296,128]{1,0:T(8,128)S(1)} collective-permute-done((f32[1296,128]{1,0:T(8,128)}, f32[1296,128]{1,0:T(8,128)S(1)}, u32[]{:S(2)}, u32[]{:S(2)}) %collective-permute-start.5) | collective-permute-done | bytes 663584 | tf_op jit(solution)/shard_map/ppermute | solution.py:342
  64.2 0.0 collective-permute-done.6.zcame
  64.2 4.3 %zfield.1 = (bf16[192,3456]{1,0:T(8,128)(2,1)S(1)}, f32[5,24,768]{2,1,0:T(8,128)S(1)}, f32[5,24,768]{2,1,0:T(8,128)S(1)}) custom-call(f32[2,24,768]{2,1,0:T(8,128)S(1)} %get-tuple-element.48.own_away, f32[2,24,768]{2,1,0:T(8,128)S(1)} %get-tuple-element.49.own_stay, bf16[384,3456]{1,0:T(8,128)(2,1)S(1)} %get-tuple-element.50.own_high, ...), custom_call_target="tpu_custom_call" | custom-call | flops 1500000000 | bytes 4500000 | tf_op jit(solution)/shard_map/zfield/pallas_call | solution.py:326
  68.5 0.1 collective-permute-start.7
  68.6 4.3 %came.1 = (f32[2,24,768]{2,1,0:T(8,128)S(1)}, f32[2,24,768]{2,1,0:T(8,128)S(1)}) custom-call(f32[1368,128]{1,0:T(8,128)S(1)} %collective-permute-done.8.after, f32[1368,128]{1,0:T(8,128)S(1)} %collective-permute-done.9.before, f32[9,8,128]{2,1,0:T(8,128)S(1)} %phase.1, bf16[576,3456]{1,0:T(8,128)(2,1)S(1)} %get-tuple-element.56.right, ...), custom_call_target="tpu_custom_call" | custom-call | flops 1200000000 | bytes 3600000 | tf_op jit(solution)/shard_map/came/pallas_call | solution.py:326
  72.9 0.0 copy-start.1
  72.9 0.6 collective-permute-start.10
  73.5 0.0 collective-permute-done.11.real
  73.5 0.0 collective-permute-done.12.imag
  73.5 3.0 %far.1 = (f32[1,24,768]{2,1,0:T(8,128)S(1)}, f32[1,24,768]{2,1,0:T(8,128)S(1)}) custom-call(f32[648,128]{1,0:T(8,128)S(1)} %collective-permute-done.11.real, f32[648,128]{1,0:T(8,128)S(1)} %collective-permute-done.12.imag, f32[9,8,128]{2,1,0:T(8,128)S(1)} %phase.1, bf16[576,3456]{1,0:T(8,128)(2,1)S(1)} %get-tuple-element.56.right, ...), custom_call_target="tpu_custom_call" | custom-call | flops 900000000 | bytes 2699999 | tf_op jit(solution)/shard_map/far/pallas_call | solution.py:326
  76.5 0.8 collective-permute-start.13
  77.3 0.0 collective-permute-done.10.refs_3_
  77.3 0.0 collective-permute-done.7.refs_1_
  77.3 0.9 collective-permute-done.13.refs_5_
  78.2 0.1 add.2
  78.3 1.6 %collective-permute-start.14 = (f32[48,768]{1,0:T(8,128)S(1)}, f32[48,768]{1,0:T(8,128)S(1)}, u32[]{:S(2)}, u32[]{:S(2)}) collective-permute-start(f32[48,768]{1,0:T(8,128)S(1)} %get-tuple-element.72), channel_id=1, source_target_pairs={{0,64},{64,128},{128,192},{192,0},{1,65},{65,129},{129,193},{193,1... | collective-permute-start | bytes 442376 | tf_op jit(solution)/shard_map/ppermute | solution.py:342
  79.9 2.6 %collective-permute-start.15 = (f32[48,768]{1,0:T(8,128)S(1)}, f32[48,768]{1,0:T(8,128)S(1)}, u32[]{:S(2)}, u32[]{:S(2)}) collective-permute-start(f32[48,768]{1,0:T(8,128)S(1)} %get-tuple-element.73), channel_id=1, source_target_pairs={{0,128},{64,192},{128,0},{192,64},{1,129},{65,193},{129,1},{193,65... | collective-permute-start | bytes 442376 | tf_op jit(solution)/shard_map/ppermute | solution.py:342
  82.5 1.1 collective-permute-start.16
  83.6 1.4 %collective-permute-done.14.second = f32[48,768]{1,0:T(8,128)S(1)} collective-permute-done((f32[48,768]{1,0:T(8,128)S(1)}, f32[48,768]{1,0:T(8,128)S(1)}, u32[]{:S(2)}, u32[]{:S(2)}) %collective-permute-start.14) | collective-permute-done | bytes 147488 | tf_op jit(solution)/shard_map/ppermute | solution.py:342
  85.0 4.3 %collective-permute-done.15.third = f32[48,768]{1,0:T(8,128)S(1)} collective-permute-done((f32[48,768]{1,0:T(8,128)S(1)}, f32[48,768]{1,0:T(8,128)S(1)}, u32[]{:S(2)}, u32[]{:S(2)}) %collective-permute-start.15) | collective-permute-done | bytes 147488 | tf_op jit(solution)/shard_map/ppermute | solution.py:342
  89.3 0.0 collective-permute-done.16.fourth
  89.3 0.2 pack.1
  89.5 19.8 %all_to_all.5.part_ref = f32[16,1,2304]{2,1,0:T(1,128)S(1)} all-to-all(f32[16,1,2304]{2,1,0:T(1,128)S(1)} %pack.1), channel_id=1, replica_groups=mesh['y'=4,'zl'=4,'core'=2,'x'=4,'zh'=2] {'zl','zh','core'}, dimensions={0} | all-to-all | bytes 294912 | tf_op jit(solution)/shard_map/all_to_all | solution.py:398
  109.3 0.0 copy-done.1
  109.3 0.8 last.1
  110.1 0.7 copy.5
  (4 shorter events, 0.1 us)
Async XLA Ops:
  0.0 12.7 %copy-start.2 = (f32[3,2,3,3,1,2304]{5,4,3,2,1,0:T(1,128)S(1)}, f32[3,2,3,3,1,2304]{5,4,3,2,1,0:T(1,128)}, u32[]{:S(2)}) copy-start(f32[3,2,3,3,1,2304]{5,4,3,2,1,0:T(1,128)} %param.5) | copy-start | bytes 1492996
  1.5 14.9 %copy-start = (s32[4,3]{1,0:T(4,128)S(1)}, s32[4,3]{1,0:T(4,128)}, u32[]{:S(2)}) copy-start(s32[4,3]{1,0:T(4,128)} %mom_ref.1) | copy-start | bytes 148
  2.4 17.2 %collective-permute-start.1 = (f32[1296,128]{1,0:T(8,128)}, f32[1296,128]{1,0:T(8,128)S(1)}, u32[]{:S(2)}, u32[]{:S(2)}) collective-permute-start(f32[1296,128]{1,0:T(8,128)} %get-tuple-element.61.keep), channel_id=1, source_target_pairs={{0,6},{2,0},{4,2},{6,4},{1,7},{3,1},{5,3},{7,5},{8,14},{10,8},{12,... | collective-permute-start | bytes 1990664 | tf_op jit(solution)/shard_map/ppermute | solution.py:342
  5.7 16.9 %collective-permute-start.2 = (f32[1296,128]{1,0:T(8,128)}, f32[1296,128]{1,0:T(8,128)S(1)}, u32[]{:S(2)}, u32[]{:S(2)}) collective-permute-start(f32[1296,128]{1,0:T(8,128)} %get-tuple-element.61.keep), channel_id=1, source_target_pairs={{0,2},{2,4},{4,6},{6,0},{1,3},{3,5},{5,7},{7,1},{8,10},{10,12},{12... | collective-permute-start | bytes 1990664 | tf_op jit(solution)/shard_map/ppermute | solution.py:342
  5.8 25.3 %collective-permute-start = (f32[1368,128]{1,0:T(8,128)S(1)}, f32[1368,128]{1,0:T(8,128)S(1)}, u32[]{:S(2)}, u32[]{:S(2)}) collective-permute-start(f32[1368,128]{1,0:T(8,128)S(1)} %get-tuple-element.41), channel_id=1, source_target_pairs={{0,1},{1,0},{2,3},{3,2},{4,5},{5,4},{6,7},{7,6},{8,9},{9,8},{10,11... | collective-permute-start | bytes 2101256 | tf_op jit(solution)/shard_map/ppermute | solution.py:342
  22.7 8.4 %collective-permute-start.3 = (f32[648,128]{1,0:T(8,128)S(1)}, f32[648,128]{1,0:T(8,128)S(1)}, u32[]{:S(2)}, u32[]{:S(2)}) collective-permute-start(f32[648,128]{1,0:T(8,128)S(1)} %slice.8), channel_id=1, source_target_pairs={{0,6},{2,0},{4,2},{6,4},{1,7},{3,1},{5,3},{7,5},{8,14},{10,8},{12,... | collective-permute-start | bytes 995336 | tf_op jit(solution)/shard_map/ppermute | solution.py:342
  23.1 8.7 %collective-permute-start.4 = (f32[648,128]{1,0:T(8,128)S(1)}, f32[648,128]{1,0:T(8,128)S(1)}, u32[]{:S(2)}, u32[]{:S(2)}) collective-permute-start(f32[648,128]{1,0:T(8,128)S(1)} %slice.9), channel_id=1, source_target_pairs={{0,2},{2,4},{4,6},{6,0},{1,3},{3,5},{5,7},{7,1},{8,10},{10,12},{12... | collective-permute-start | bytes 995336 | tf_op jit(solution)/shard_map/ppermute | solution.py:342
  31.8 27.9 %collective-permute-start.8 = (f32[1368,128]{1,0:T(8,128)S(1)}, f32[1368,128]{1,0:T(8,128)S(1)}, u32[]{:S(2)}, u32[]{:S(2)}) collective-permute-start(f32[1368,128]{1,0:T(8,128)S(1)} %collective-permute-done.came), channel_id=1, source_target_pairs={{0,6},{2,0},{4,2},{6,4},{1,7},{3,1},{5,3},{7,5},{8,14},{10,8},{12,... | collective-permute-start | bytes 2101256 | tf_op jit(solution)/shard_map/ppermute | solution.py:342
  33.4 26.2 %collective-permute-start.9 = (f32[1368,128]{1,0:T(8,128)S(1)}, f32[1368,128]{1,0:T(8,128)S(1)}, u32[]{:S(2)}, u32[]{:S(2)}) collective-permute-start(f32[1368,128]{1,0:T(8,128)S(1)} %collective-permute-done.came), channel_id=1, source_target_pairs={{0,2},{2,4},{4,6},{6,0},{1,3},{3,5},{5,7},{7,1},{8,10},{10,12},{12... | collective-permute-start | bytes 2101256 | tf_op jit(solution)/shard_map/ppermute | solution.py:342
  33.4 30.8 %collective-permute-start.6 = (f32[1368,128]{1,0:T(8,128)S(1)}, f32[1368,128]{1,0:T(8,128)S(1)}, u32[]{:S(2)}, u32[]{:S(2)}) collective-permute-start(f32[1368,128]{1,0:T(8,128)S(1)} %collective-permute-done.came), channel_id=1, source_target_pairs={{0,248},{8,0},{16,8},{24,16},{32,24},{40,32},{48,40},{56,48},{64,5... | collective-permute-start | bytes 2101256 | tf_op jit(solution)/shard_map/ppermute | solution.py:342
  46.0 18.3 %collective-permute-start.5 = (f32[1296,128]{1,0:T(8,128)}, f32[1296,128]{1,0:T(8,128)S(1)}, u32[]{:S(2)}, u32[]{:S(2)}) collective-permute-start(f32[1296,128]{1,0:T(8,128)} %get-tuple-element.61.keep), channel_id=1, source_target_pairs={{0,248},{8,0},{16,8},{24,16},{32,24},{40,32},{48,40},{56,48},{64,5... | collective-permute-start | bytes 1990664 | tf_op jit(solution)/shard_map/ppermute | solution.py:342
  59.7 13.8 %collective-permute-start.11 = (f32[648,128]{1,0:T(8,128)S(1)}, f32[648,128]{1,0:T(8,128)S(1)}, u32[]{:S(2)}, u32[]{:S(2)}) collective-permute-start(f32[648,128]{1,0:T(8,128)S(1)} %get-tuple-element.67), channel_id=1, source_target_pairs={{0,6},{2,0},{4,2},{6,4},{1,7},{3,1},{5,3},{7,5},{8,14},{10,8},{12,... | collective-permute-start | bytes 995336 | tf_op jit(solution)/shard_map/ppermute | solution.py:342
  62.8 10.8 %collective-permute-start.12 = (f32[648,128]{1,0:T(8,128)S(1)}, f32[648,128]{1,0:T(8,128)S(1)}, u32[]{:S(2)}, u32[]{:S(2)}) collective-permute-start(f32[648,128]{1,0:T(8,128)S(1)} %get-tuple-element.68), channel_id=1, source_target_pairs={{0,2},{2,4},{4,6},{6,0},{1,3},{3,5},{5,7},{7,1},{8,10},{10,12},{12... | collective-permute-start | bytes 995336 | tf_op jit(solution)/shard_map/ppermute | solution.py:342
  68.5 8.7 %collective-permute-start.7 = (f32[5,24,768]{2,1,0:T(8,128)S(1)}, f32[5,24,768]{2,1,0:T(8,128)S(1)}, u32[]{:S(2)}, u32[]{:S(2)}) collective-permute-start(f32[5,24,768]{2,1,0:T(8,128)S(1)} %get-tuple-element.63), channel_id=1, source_target_pairs={{0,8},{8,0},{1,9},{9,1},{2,10},{10,2},{3,11},{11,3},{4,12},{12,4},... | collective-permute-start | bytes 1105928 | tf_op jit(solution)/shard_map/ppermute | solution.py:342
  72.9 36.4 %copy-start.1 = (s32[3]{0:T(128)S(1)}, s32[3]{0:T(128)}, u32[]{:S(2)}) copy-start(s32[3]{0:T(128)} %direction_ref.1) | copy-start | bytes 40
  72.9 4.3 %collective-permute-start.10 = (f32[2,24,768]{2,1,0:T(8,128)S(1)}, f32[2,24,768]{2,1,0:T(8,128)S(1)}, u32[]{:S(2)}, u32[]{:S(2)}) collective-permute-start(f32[2,24,768]{2,1,0:T(8,128)S(1)} %get-tuple-element.66), channel_id=1, source_target_pairs={{0,8},{8,0},{1,9},{9,1},{2,10},{10,2},{3,11},{11,3},{4,12},{12,4},... | collective-permute-start | bytes 442376 | tf_op jit(solution)/shard_map/ppermute | solution.py:342
  76.5 1.7 %collective-permute-start.13 = (f32[1,24,768]{2,1,0:T(8,128)S(1)}, f32[1,24,768]{2,1,0:T(8,128)S(1)}, u32[]{:S(2)}, u32[]{:S(2)}) collective-permute-start(f32[1,24,768]{2,1,0:T(8,128)S(1)} %get-tuple-element.70), channel_id=1, source_target_pairs={{0,8},{8,0},{1,9},{9,1},{2,10},{10,2},{3,11},{11,3},{4,12},{12,4},... | collective-permute-start | bytes 221192 | tf_op jit(solution)/shard_map/ppermute | solution.py:342
  78.3 6.7 %collective-permute-start.14 = (f32[48,768]{1,0:T(8,128)S(1)}, f32[48,768]{1,0:T(8,128)S(1)}, u32[]{:S(2)}, u32[]{:S(2)}) collective-permute-start(f32[48,768]{1,0:T(8,128)S(1)} %get-tuple-element.72), channel_id=1, source_target_pairs={{0,64},{64,128},{128,192},{192,0},{1,65},{65,129},{129,193},{193,1... | collective-permute-start | bytes 442376 | tf_op jit(solution)/shard_map/ppermute | solution.py:342
  79.9 9.4 %collective-permute-start.15 = (f32[48,768]{1,0:T(8,128)S(1)}, f32[48,768]{1,0:T(8,128)S(1)}, u32[]{:S(2)}, u32[]{:S(2)}) collective-permute-start(f32[48,768]{1,0:T(8,128)S(1)} %get-tuple-element.73), channel_id=1, source_target_pairs={{0,128},{64,192},{128,0},{192,64},{1,129},{65,193},{129,1},{193,65... | collective-permute-start | bytes 442376 | tf_op jit(solution)/shard_map/ppermute | solution.py:342
  82.5 6.8 %collective-permute-start.16 = (f32[48,768]{1,0:T(8,128)S(1)}, f32[48,768]{1,0:T(8,128)S(1)}, u32[]{:S(2)}, u32[]{:S(2)}) collective-permute-start(f32[48,768]{1,0:T(8,128)S(1)} %get-tuple-element.74), channel_id=1, source_target_pairs={{0,192},{64,0},{128,64},{192,128},{1,193},{65,1},{129,65},{193,129... | collective-permute-start | bytes 442376 | tf_op jit(solution)/shard_map/ppermute | solution.py:342

commit v8 on v7

--- a/solution.py
+++ b/solution.py
@@ -152,33 +152,36 @@
     return build
 
 
+def make_left(blocks, phase_ref, high_ref, low_ref, tile):
+    rows = 24 * len(blocks)
+    for index in range(4):
+        cosv = phase_ref[tile, index:index + 1, :]
+        sinv = phase_ref[tile, 4 + index:5 + index, :]
+        for color in range(3):
+            row = tile * 72 + color * 24
+            left_real = []
+            left_imag = []
+            for block in blocks:
+                a = block[row:row + 24]
+                b = block[row + 648:row + 672]
+                left_real.append(a * cosv - b * sinv)
+                left_imag.append(-(a * sinv + b * cosv))
+            high, low = split(jnp.concatenate(left_real + left_imag, axis=0))
+            column = tile * 384 + color * 128
+            high_ref[2 * rows * index:2 * rows * (index + 1), column:column + 128] = high
+            low_ref[2 * rows * index:2 * rows * (index + 1), column:column + 128] = low
+
+
 def multiply(blocks, phase_ref, rights, first, away_ref, stay_ref, high_ref, low_ref, build=None, offset=0):
     count = len(blocks)
     rows = 24 * count
-
-    def make_left(tile):
-        for index in range(4):
-            cosv = phase_ref[tile, index:index + 1, :]
-            sinv = phase_ref[tile, 4 + index:5 + index, :]
-            for color in range(3):
-                row = tile * 72 + color * 24
-                left_real = []
-                left_imag = []
-                for block in blocks:
-                    a = block[row:row + 24]
-                    b = block[row + 648:row + 672]
-                    left_real.append(a * cosv - b * sinv)
-                    left_imag.append(-(a * sinv + b * cosv))
-                high, low = split(jnp.concatenate(left_real + left_imag, axis=0))
-                column = tile * 384 + color * 128
-                high_ref[2 * rows * index:2 * rows * (index + 1), column:column + 128] = high
-                low_ref[2 * rows * index:2 * rows * (index + 1), column:column + 128] = low
+    bounds = (0, TILES) if blocks[0] is None else (0, 2, 6, TILES)
 
     def prepare(chunk):
-        for tile in range(3 * chunk, 3 * chunk + 3):
+        for tile in range(bounds[chunk], bounds[chunk + 1]):
             if build is not None:
                 build(tile)
-            make_left(tile)
+            make_left(blocks, phase_ref, high_ref, low_ref, tile)
 
     def times(left, right):
         return lax.dot_general(
@@ -193,10 +196,10 @@
     if blocks[0] is not None:
         prepare(0)
     total = None
-    for chunk in range(3):
-        if chunk < 2 and blocks[0] is not None:
+    for chunk in range(len(bounds) - 1):
+        if chunk + 2 < len(bounds) and blocks[0] is not None:
             prepare(chunk + 1)
-        part = slice(chunk * HALF, (chunk + 1) * HALF)
+        part = slice(bounds[chunk] * 384, bounds[chunk + 1] * 384)
         highs = [ref[:2 * width, part] for ref, width in zip(rights, widths)]
         lows = [ref[2 * width:, part] for ref, width in zip(rights, widths)]
         both = times(high_ref[:, part], joined(highs + lows))
@@ -221,13 +224,20 @@
             to += width
 
 
-def own_kernel(keep, came, halo, link, phase, right, away, stay, high, low):
+def own_kernel(keep, came, halo, link, phase, token, right, away, stay, high, low):
     build = build_plane(keep, came, halo, link, right)
     multiply([keep, came], phase, (right,), 0, away, stay, high, low, build)
 
 
-def kept_kernel(after, before, real, imag, phase, right, away, stay, high, low):
-    multiply([after, before, Halves(real, imag)], phase, (right,), 0, away, stay, high, low)
+def left_kernel(after, before, real, imag, phase_ref, high_ref, low_ref, token_ref):
+    blocks = [after, before, Halves(real, imag)]
+    for tile in range(TILES):
+        make_left(blocks, phase_ref, high_ref, low_ref, tile)
+    token_ref[...] = phase_ref[0] + phase_ref[1]
+
+
+def kept_kernel(high, low, right, away, stay):
+    multiply([None] * 3, None, (right,), 0, away, stay, high, low)
 
 
 def z_kernel(
@@ -358,9 +368,10 @@
     link, = call(link_kernel, "link", [(TILES, 56, 128)], (links.reshape(54, 2304),))
     first, second, link, phase = lax.optimization_barrier((keep_after[:648], keep_before[648:], link, phase))
     keep_far = (along(first, "x", -1), along(second, "x", 1))
-    came, keep_after, keep_before, keep_far, later = lax.optimization_barrier(
-        (came, keep_after, keep_before, keep_far, keep)
+    kept_high, kept_low, token = call(
+        left_kernel, "left", [(576, DEPTH)] * 2 + [(8, 128)], (keep_after, keep_before, *keep_far, phase)
     )
+    came, later, token = lax.optimization_barrier((came, keep, token))
     zcame = along(came, SITE, -1)
     zkeep = along(later, SITE, -1)
     came_after = along(came, "x", -1)
@@ -370,17 +381,14 @@
         return [(count, 24, 768)] * 2
 
     right, *own = call(
-        own_kernel, "own", [(576, DEPTH)] + parts(2) + [(384, DEPTH)] * 2, (keep, came, halo, link, phase), (), 0, 6,
+        own_kernel, "own", [(576, DEPTH)] + parts(2) + [(384, DEPTH)] * 2, (keep, came, halo, link, phase, token), (), 0, 6,
     )
-    kept = call(
-        kept_kernel, "kept", parts(3) + [(576, DEPTH)] * 2,
-        (keep_after, keep_before, *keep_far, phase, right), (), 0, 6,
-    )
+    kept = call(kept_kernel, "kept", parts(3), (kept_high, kept_low, right), (), 0, 6)
     half = (648, 128)
     first, second = call(forward_kernel, "forward", [half, half], (came_after, came_before, kept[0]))
     came_far = (along(first, "x", -1), along(second, "x", 1))
     zright, away, stay = call(
-        z_kernel, "zfield", [(192, DEPTH)] + parts(5), (*own, *kept, zkeep, zcame, link), (), 0, 5
+        z_kernel, "zfield", [(192, DEPTH)] + parts(5), (*own, *kept, kept_high, kept_low, zkeep, zcame, link), (), 0, 5
     )
     products = [(away, stay)]
     products.append(call(

time: 111 us -> 109 us (0.982)
  starting transfers between devices: 35.7 us -> 32.7 us
  waiting for transfers between devices: 21.1 us -> 22.5 us
    ppermute x17, starting transfers between devices: 35.7 us -> 32.7 us  [along(): lax.ppermute(value, axis, [(i, (i + step) % count) for i in range(count)])]
    ppermute x17, waiting for transfers between devices: 21.1 us -> 22.5 us  [along(): lax.ppermute(value, axis, [(i, (i + step) % count) for i in range(count)])]
    pallas_call x12 -> x13, Pallas kernels: 28.1 us -> 28.9 us  [call(): pl.pallas_call(kernel, out_shape=out_shape, in_specs=[pl.BlockSpec(memory...]
  transfers between devices with their start and end apart: 17 -> 17, of which waited for: 8 -> 8; matrix products, arithmetic and copies ran while one was open for 3% -> 3% of each run, Pallas kernels for 24% -> 25%
where the time goes in v8:
time: 109 us
  starting transfers between devices  32.7 us (30%)
  Pallas kernels  28.9 us (27%)
  waiting for transfers between devices  22.5 us (21%)
  blocking collectives  18.9 us (17%)
  local copies, waits for them, and re-layouts  3.56 us (3%)
  other arithmetic  2.34 us (2%)
    ppermute x17, starting transfers between devices, along(): lax.ppermute(value, axis, [(i, (i + step) % count) for i in range(count)])  32.7 us
    pallas_call x13, Pallas kernels, call(): pl.pallas_call(kernel, out_shape=out_shape, in_specs=[pl.BlockSpec(memory...  28.9 us
    ppermute x17, waiting for transfers between devices, along(): lax.ppermute(value, axis, [(i, (i + step) % count) for i in range(count)])  22.5 us
    all_to_all x1, blocking collectives, local(): mixed = lax.all_to_all(packed, ('zl', 'zh', 'core'), 0, 0)  18.9 us
    unnamed x1, other arithmetic  2.34 us
  transfers between devices with their start and end apart: 17, of which 8 were waited for; matrix products, arithmetic and copies ran while one was open for 3% of the time, Pallas kernels for 25%

profile of v8, /device:TPU:1, one launch (start us, length us, event | category | flops | bytes accessed | tf_op | source)
XLA Modules:
  0.0 109.1 jit_solution(5424102400493260382)
XLA Ops:
  0.0 0.0 copy-start.2
  0.0 1.5 %copy.6 = f32[2,3,24,1,2304]{4,2,3,1,0:T(8,128)S(1)} copy(f32[2,3,24,1,2304]{4,3,2,1,0:T(1,128)} %param.4) | data formatting | bytes 2654208
  1.5 0.0 copy-start
  1.5 1.0 cut.1
  2.4 3.3 %collective-permute-start.1 = (f32[1296,128]{1,0:T(8,128)}, f32[1296,128]{1,0:T(8,128)S(1)}, u32[]{:S(2)}, u32[]{:S(2)}) collective-permute-start(f32[1296,128]{1,0:T(8,128)} %get-tuple-element.57.keep), channel_id=1, source_target_pairs={{0,6},{2,0},{4,2},{6,4},{1,7},{3,1},{5,3},{7,5},{8,14},{10,8},{12,... | collective-permute-start | bytes 1990664 | tf_op jit(solution)/shard_map/ppermute | solution.py:352
  5.7 0.0 collective-permute-start.2
  5.7 6.9 %collective-permute-start = (f32[1368,128]{1,0:T(8,128)S(1)}, f32[1368,128]{1,0:T(8,128)S(1)}, u32[]{:S(2)}, u32[]{:S(2)}) collective-permute-start(f32[1368,128]{1,0:T(8,128)S(1)} %get-tuple-element.39), channel_id=1, source_target_pairs={{0,1},{1,0},{2,3},{3,2},{4,5},{5,4},{6,7},{7,6},{8,9},{9,8},{10,11... | collective-permute-start | bytes 2101256 | tf_op jit(solution)/shard_map/ppermute | solution.py:352
  12.7 0.0 copy-done.2
  12.7 2.3 %reduce = f32[3,2,3,3,2304]{4,3,2,1,0:T(4,128)} reduce(f32[3,2,3,3,1,2304]{5,4,3,2,1,0:T(1,128)S(1)} %copy-done.2, f32[]{:T(128)} %constant.2), dimensions={4}, to_apply=%param.5.reduce_sub_computation | reduce | bytes 995332 | tf_op args[1]
  15.0 1.3 %reshape.7.link_ref = f32[54,2304]{1,0:T(8,128)S(1)} reshape(f32[3,2,3,3,2304]{4,3,2,1,0:T(4,128)} %reduce) | data formatting | bytes 995328 | tf_op jit(solution)/shard_map/reshape | solution.py:368
  16.4 0.0 copy-done
  16.4 0.7 phase.1.phase_ref
  17.1 2.5 %collective-permute-done.1.after = f32[1296,128]{1,0:T(8,128)S(1)} collective-permute-done((f32[1296,128]{1,0:T(8,128)}, f32[1296,128]{1,0:T(8,128)S(1)}, u32[]{:S(2)}, u32[]{:S(2)}) %collective-permute-start.1) | collective-permute-done | bytes 663584 | tf_op jit(solution)/shard_map/ppermute | solution.py:352
  19.7 3.0 %collective-permute-done.2.before = f32[1296,128]{1,0:T(8,128)S(1)} collective-permute-done((f32[1296,128]{1,0:T(8,128)}, f32[1296,128]{1,0:T(8,128)S(1)}, u32[]{:S(2)}, u32[]{:S(2)}) %collective-permute-start.2) | collective-permute-done | bytes 663584 | tf_op jit(solution)/shard_map/ppermute | solution.py:352
  22.6 0.4 collective-permute-start.3
  23.1 1.1 %collective-permute-start.4 = (f32[648,128]{1,0:T(8,128)S(1)}, f32[648,128]{1,0:T(8,128)S(1)}, u32[]{:S(2)}, u32[]{:S(2)}) collective-permute-start(f32[648,128]{1,0:T(8,128)S(1)} %slice.9), channel_id=1, source_target_pairs={{0,2},{2,4},{4,6},{6,0},{1,3},{3,5},{5,7},{7,1},{8,10},{10,12},{12... | collective-permute-start | bytes 995336 | tf_op jit(solution)/shard_map/ppermute | solution.py:352
  24.2 6.0 %collective-permute-done.3.real = f32[648,128]{1,0:T(8,128)S(1)} collective-permute-done((f32[648,128]{1,0:T(8,128)S(1)}, f32[648,128]{1,0:T(8,128)S(1)}, u32[]{:S(2)}, u32[]{:S(2)}) %collective-permute-start.3) | collective-permute-done | bytes 331808 | tf_op jit(solution)/shard_map/ppermute | solution.py:352
  30.2 1.6 %collective-permute-done.4.imag = f32[648,128]{1,0:T(8,128)S(1)} collective-permute-done((f32[648,128]{1,0:T(8,128)S(1)}, f32[648,128]{1,0:T(8,128)S(1)}, u32[]{:S(2)}, u32[]{:S(2)}) %collective-permute-start.4) | collective-permute-done | bytes 331808 | tf_op jit(solution)/shard_map/ppermute | solution.py:352
  31.8 2.3 %left.1 = (bf16[576,3456]{1,0:T(8,128)(2,1)S(1)}, bf16[576,3456]{1,0:T(8,128)(2,1)S(1)}, f32[8,128]{1,0:T(8,128)S(1)}) custom-call(f32[1296,128]{1,0:T(8,128)S(1)} %collective-permute-done.1.after, f32[1296,128]{1,0:T(8,128)S(1)} %collective-permute-done.2.before, f32[648,128]{1,0:T(8,128)S(1)} %collective-permute-done.3.real, ...), custom_call_target="tpu_custom_call" | custom-call | flops 300000000 | bytes 900000 | tf_op jit(solution)/shard_map/left/pallas_call | solution.py:336
  34.0 0.0 collective-permute-done.came
  34.1 0.4 collective-permute-start.8
  34.4 1.2 %collective-permute-start.9 = (f32[1368,128]{1,0:T(8,128)S(1)}, f32[1368,128]{1,0:T(8,128)S(1)}, u32[]{:S(2)}, u32[]{:S(2)}) collective-permute-start(f32[1368,128]{1,0:T(8,128)S(1)} %collective-permute-done.came), channel_id=1, source_target_pairs={{0,2},{2,4},{4,6},{6,0},{1,3},{3,5},{5,7},{7,1},{8,10},{10,12},{12... | collective-permute-start | bytes 2101256 | tf_op jit(solution)/shard_map/ppermute | solution.py:352
  35.6 10.4 %collective-permute-start.6 = (f32[1368,128]{1,0:T(8,128)S(1)}, f32[1368,128]{1,0:T(8,128)S(1)}, u32[]{:S(2)}, u32[]{:S(2)}) collective-permute-start(f32[1368,128]{1,0:T(8,128)S(1)} %collective-permute-done.came), channel_id=1, source_target_pairs={{0,248},{8,0},{16,8},{24,16},{32,24},{40,32},{48,40},{56,48},{64,5... | collective-permute-start | bytes 2101256 | tf_op jit(solution)/shard_map/ppermute | solution.py:352
  46.0 0.0 collective-permute-start.5
  46.0 7.1 %own.1 = (bf16[576,3456]{1,0:T(8,128)(2,1)S(1)}, f32[2,24,768]{2,1,0:T(8,128)S(1)}, f32[2,24,768]{2,1,0:T(8,128)S(1)}, bf16[384,3456]{1,0:T(8,128)(2,1)S(1)}, bf16[384,3456]{1,0:T(8,128)(2,1)S(1)}) custom-call(f32[1296,128]{1,0:T(8,128)} %get-tuple-element.57.keep, f32[1368,128]{1,0:T(8,128)S(1)} %collective-permute-done.came, ...), custom_call_target="tpu_custom_call" | custom-call | flops 1800000000 | bytes 5399999 | tf_op jit(solution)/shard_map/own/pallas_call | solution.py:336
  53.0 5.7 %kept.1 = (f32[3,24,768]{2,1,0:T(8,128)S(1)}, f32[3,24,768]{2,1,0:T(8,128)S(1)}) custom-call(bf16[576,3456]{1,0:T(8,128)(2,1)S(1)} %get-tuple-element.52.high.kept_high, bf16[576,3456]{1,0:T(8,128)(2,1)S(1)} %get-tuple-element.53.low.kept_low, bf16[576,3456]{1,0:T(8,128)(2,1)S(1)} %get-tuple-element.54.right), custom_call_target="tpu_custom_call" | custom-call | flops 1800000000 | bytes 5399999 | tf_op jit(solution)/shard_map/kept/pallas_call | solution.py:336
  58.7 0.0 collective-permute-done.8.after
  58.7 0.0 collective-permute-done.9.before
  58.8 3.0 %collective-permute-start.11 = (f32[648,128]{1,0:T(8,128)S(1)}, f32[648,128]{1,0:T(8,128)S(1)}, u32[]{:S(2)}, u32[]{:S(2)}) collective-permute-start(f32[648,128]{1,0:T(8,128)S(1)} %get-tuple-element.63), channel_id=1, source_target_pairs={{0,6},{2,0},{4,2},{6,4},{1,7},{3,1},{5,3},{7,5},{8,14},{10,8},{12,... | collective-permute-start | bytes 995336 | tf_op jit(solution)/shard_map/ppermute | solution.py:352
  61.8 0.0 collective-permute-start.12
  61.8 2.4 %collective-permute-done.5.zkeep = f32[1296,128]{1,0:T(8,128)S(1)} collective-permute-done((f32[1296,128]{1,0:T(8,128)}, f32[1296,128]{1,0:T(8,128)S(1)}, u32[]{:S(2)}, u32[]{:S(2)}) %collective-permute-start.5) | collective-permute-done | bytes 663584 | tf_op jit(solution)/shard_map/ppermute | solution.py:352
  64.2 0.0 collective-permute-done.6.zcame
  64.2 4.1 %zfield.1 = (bf16[192,3456]{1,0:T(8,128)(2,1)S(1)}, f32[5,24,768]{2,1,0:T(8,128)S(1)}, f32[5,24,768]{2,1,0:T(8,128)S(1)}) custom-call(f32[2,24,768]{2,1,0:T(8,128)S(1)} %get-tuple-element.48.own_away, f32[2,24,768]{2,1,0:T(8,128)S(1)} %get-tuple-element.49.own_stay, bf16[384,3456]{1,0:T(8,128)(2,1)S(1)} %get-tuple-element.50.own_high, ...), custom_call_target="tpu_custom_call" | custom-call | flops 1500000000 | bytes 4500000 | tf_op jit(solution)/shard_map/zfield/pallas_call | solution.py:336
  68.3 0.1 collective-permute-start.7
  68.4 4.0 %came.1 = (f32[2,24,768]{2,1,0:T(8,128)S(1)}, f32[2,24,768]{2,1,0:T(8,128)S(1)}) custom-call(f32[1368,128]{1,0:T(8,128)S(1)} %collective-permute-done.8.after, f32[1368,128]{1,0:T(8,128)S(1)} %collective-permute-done.9.before, f32[9,8,128]{2,1,0:T(8,128)S(1)} %phase.1.phase_ref, bf16[576,3456]{1,0:T(8,128)(2,1)S(1)} %get-tuple-element.54.right, ...), custom_call_target="tpu_custom_call" | custom-call | flops 1200000000 | bytes 3600000 | tf_op jit(solution)/shard_map/came/pallas_call | solution.py:336
  72.5 0.0 copy-start.1
  72.5 0.6 collective-permute-start.10
  73.1 0.0 collective-permute-done.11.real
  73.1 0.0 collective-permute-done.12.imag
  73.1 2.9 %far.1 = (f32[1,24,768]{2,1,0:T(8,128)S(1)}, f32[1,24,768]{2,1,0:T(8,128)S(1)}) custom-call(f32[648,128]{1,0:T(8,128)S(1)} %collective-permute-done.11.real, f32[648,128]{1,0:T(8,128)S(1)} %collective-permute-done.12.imag, f32[9,8,128]{2,1,0:T(8,128)S(1)} %phase.1.phase_ref, bf16[576,3456]{1,0:T(8,128)(2,1)S(1)} %get-tuple-element.54.right, ...), custom_call_target="tpu_custom_call" | custom-call | flops 900000000 | bytes 2699999 | tf_op jit(solution)/shard_map/far/pallas_call | solution.py:336
  75.9 0.2 collective-permute-start.13
  76.2 0.0 collective-permute-done.10.refs_3_
  76.2 0.0 collective-permute-done.7.refs_1_
  76.2 1.1 %collective-permute-done.13.refs_5_ = f32[1,24,768]{2,1,0:T(8,128)S(1)} collective-permute-done((f32[1,24,768]{2,1,0:T(8,128)S(1)}, f32[1,24,768]{2,1,0:T(8,128)S(1)}, u32[]{:S(2)}, u32[]{:S(2)}) %collective-permute-start.13) | collective-permute-done | bytes 73760 | tf_op jit(solution)/shard_map/ppermute | solution.py:352
  77.3 0.1 add.2
  77.4 1.4 %collective-permute-start.14 = (f32[48,768]{1,0:T(8,128)S(1)}, f32[48,768]{1,0:T(8,128)S(1)}, u32[]{:S(2)}, u32[]{:S(2)}) collective-permute-start(f32[48,768]{1,0:T(8,128)S(1)} %get-tuple-element.68), channel_id=1, source_target_pairs={{0,64},{64,128},{128,192},{192,0},{1,65},{65,129},{129,193},{193,1... | collective-permute-start | bytes 442376 | tf_op jit(solution)/shard_map/ppermute | solution.py:352
  78.8 2.6 %collective-permute-start.15 = (f32[48,768]{1,0:T(8,128)S(1)}, f32[48,768]{1,0:T(8,128)S(1)}, u32[]{:S(2)}, u32[]{:S(2)}) collective-permute-start(f32[48,768]{1,0:T(8,128)S(1)} %get-tuple-element.69), channel_id=1, source_target_pairs={{0,128},{64,192},{128,0},{192,64},{1,129},{65,193},{129,1},{193,65... | collective-permute-start | bytes 442376 | tf_op jit(solution)/shard_map/ppermute | solution.py:352
  81.4 1.1 collective-permute-start.16
  82.5 1.7 %collective-permute-done.14.second = f32[48,768]{1,0:T(8,128)S(1)} collective-permute-done((f32[48,768]{1,0:T(8,128)S(1)}, f32[48,768]{1,0:T(8,128)S(1)}, u32[]{:S(2)}, u32[]{:S(2)}) %collective-permute-start.14) | collective-permute-done | bytes 147488 | tf_op jit(solution)/shard_map/ppermute | solution.py:352
  84.1 4.3 %collective-permute-done.15.third = f32[48,768]{1,0:T(8,128)S(1)} collective-permute-done((f32[48,768]{1,0:T(8,128)S(1)}, f32[48,768]{1,0:T(8,128)S(1)}, u32[]{:S(2)}, u32[]{:S(2)}) %collective-permute-start.15) | collective-permute-done | bytes 147488 | tf_op jit(solution)/shard_map/ppermute | solution.py:352
  88.4 0.0 collective-permute-done.16.fourth
  88.4 0.2 pack.1
  88.6 18.9 %all_to_all.5.part_ref = f32[16,1,2304]{2,1,0:T(1,128)S(1)} all-to-all(f32[16,1,2304]{2,1,0:T(1,128)S(1)} %pack.1), channel_id=1, replica_groups=mesh['y'=4,'zl'=4,'core'=2,'x'=4,'zh'=2] {'zl','zh','core'}, dimensions={0} | all-to-all | bytes 294912 | tf_op jit(solution)/shard_map/all_to_all | solution.py:406
  107.6 0.0 copy-done.1
  107.6 0.8 last.1
  108.4 0.7 copy.5
  (4 shorter events, 0.1 us)
Async XLA Ops:
  0.0 12.7 %copy-start.2 = (f32[3,2,3,3,1,2304]{5,4,3,2,1,0:T(1,128)S(1)}, f32[3,2,3,3,1,2304]{5,4,3,2,1,0:T(1,128)}, u32[]{:S(2)}) copy-start(f32[3,2,3,3,1,2304]{5,4,3,2,1,0:T(1,128)} %param.5) | copy-start | bytes 1492996
  1.5 14.9 %copy-start = (s32[4,3]{1,0:T(4,128)S(1)}, s32[4,3]{1,0:T(4,128)}, u32[]{:S(2)}) copy-start(s32[4,3]{1,0:T(4,128)} %mom_ref.1) | copy-start | bytes 148
  2.4 17.2 %collective-permute-start.1 = (f32[1296,128]{1,0:T(8,128)}, f32[1296,128]{1,0:T(8,128)S(1)}, u32[]{:S(2)}, u32[]{:S(2)}) collective-permute-start(f32[1296,128]{1,0:T(8,128)} %get-tuple-element.57.keep), channel_id=1, source_target_pairs={{0,6},{2,0},{4,2},{6,4},{1,7},{3,1},{5,3},{7,5},{8,14},{10,8},{12,... | collective-permute-start | bytes 1990664 | tf_op jit(solution)/shard_map/ppermute | solution.py:352
  5.7 16.9 %collective-permute-start.2 = (f32[1296,128]{1,0:T(8,128)}, f32[1296,128]{1,0:T(8,128)S(1)}, u32[]{:S(2)}, u32[]{:S(2)}) collective-permute-start(f32[1296,128]{1,0:T(8,128)} %get-tuple-element.57.keep), channel_id=1, source_target_pairs={{0,2},{2,4},{4,6},{6,0},{1,3},{3,5},{5,7},{7,1},{8,10},{10,12},{12... | collective-permute-start | bytes 1990664 | tf_op jit(solution)/shard_map/ppermute | solution.py:352
  5.7 28.3 %collective-permute-start = (f32[1368,128]{1,0:T(8,128)S(1)}, f32[1368,128]{1,0:T(8,128)S(1)}, u32[]{:S(2)}, u32[]{:S(2)}) collective-permute-start(f32[1368,128]{1,0:T(8,128)S(1)} %get-tuple-element.39), channel_id=1, source_target_pairs={{0,1},{1,0},{2,3},{3,2},{4,5},{5,4},{6,7},{7,6},{8,9},{9,8},{10,11... | collective-permute-start | bytes 2101256 | tf_op jit(solution)/shard_map/ppermute | solution.py:352
  22.6 7.5 %collective-permute-start.3 = (f32[648,128]{1,0:T(8,128)S(1)}, f32[648,128]{1,0:T(8,128)S(1)}, u32[]{:S(2)}, u32[]{:S(2)}) collective-permute-start(f32[648,128]{1,0:T(8,128)S(1)} %slice.8), channel_id=1, source_target_pairs={{0,6},{2,0},{4,2},{6,4},{1,7},{3,1},{5,3},{7,5},{8,14},{10,8},{12,... | collective-permute-start | bytes 995336 | tf_op jit(solution)/shard_map/ppermute | solution.py:352
  23.1 8.7 %collective-permute-start.4 = (f32[648,128]{1,0:T(8,128)S(1)}, f32[648,128]{1,0:T(8,128)S(1)}, u32[]{:S(2)}, u32[]{:S(2)}) collective-permute-start(f32[648,128]{1,0:T(8,128)S(1)} %slice.9), channel_id=1, source_target_pairs={{0,2},{2,4},{4,6},{6,0},{1,3},{3,5},{5,7},{7,1},{8,10},{10,12},{12... | collective-permute-start | bytes 995336 | tf_op jit(solution)/shard_map/ppermute | solution.py:352
  34.1 24.7 %collective-permute-start.8 = (f32[1368,128]{1,0:T(8,128)S(1)}, f32[1368,128]{1,0:T(8,128)S(1)}, u32[]{:S(2)}, u32[]{:S(2)}) collective-permute-start(f32[1368,128]{1,0:T(8,128)S(1)} %collective-permute-done.came), channel_id=1, source_target_pairs={{0,6},{2,0},{4,2},{6,4},{1,7},{3,1},{5,3},{7,5},{8,14},{10,8},{12,... | collective-permute-start | bytes 2101256 | tf_op jit(solution)/shard_map/ppermute | solution.py:352
  34.4 24.3 %collective-permute-start.9 = (f32[1368,128]{1,0:T(8,128)S(1)}, f32[1368,128]{1,0:T(8,128)S(1)}, u32[]{:S(2)}, u32[]{:S(2)}) collective-permute-start(f32[1368,128]{1,0:T(8,128)S(1)} %collective-permute-done.came), channel_id=1, source_target_pairs={{0,2},{2,4},{4,6},{6,0},{1,3},{3,5},{5,7},{7,1},{8,10},{10,12},{12... | collective-permute-start | bytes 2101256 | tf_op jit(solution)/shard_map/ppermute | solution.py:352
  35.6 28.6 %collective-permute-start.6 = (f32[1368,128]{1,0:T(8,128)S(1)}, f32[1368,128]{1,0:T(8,128)S(1)}, u32[]{:S(2)}, u32[]{:S(2)}) collective-permute-start(f32[1368,128]{1,0:T(8,128)S(1)} %collective-permute-done.came), channel_id=1, source_target_pairs={{0,248},{8,0},{16,8},{24,16},{32,24},{40,32},{48,40},{56,48},{64,5... | collective-permute-start | bytes 2101256 | tf_op jit(solution)/shard_map/ppermute | solution.py:352
  46.0 18.3 %collective-permute-start.5 = (f32[1296,128]{1,0:T(8,128)}, f32[1296,128]{1,0:T(8,128)S(1)}, u32[]{:S(2)}, u32[]{:S(2)}) collective-permute-start(f32[1296,128]{1,0:T(8,128)} %get-tuple-element.57.keep), channel_id=1, source_target_pairs={{0,248},{8,0},{16,8},{24,16},{32,24},{40,32},{48,40},{56,48},{64,5... | collective-permute-start | bytes 1990664 | tf_op jit(solution)/shard_map/ppermute | solution.py:352
  58.8 14.3 %collective-permute-start.11 = (f32[648,128]{1,0:T(8,128)S(1)}, f32[648,128]{1,0:T(8,128)S(1)}, u32[]{:S(2)}, u32[]{:S(2)}) collective-permute-start(f32[648,128]{1,0:T(8,128)S(1)} %get-tuple-element.63), channel_id=1, source_target_pairs={{0,6},{2,0},{4,2},{6,4},{1,7},{3,1},{5,3},{7,5},{8,14},{10,8},{12,... | collective-permute-start | bytes 995336 | tf_op jit(solution)/shard_map/ppermute | solution.py:352
  61.8 11.3 %collective-permute-start.12 = (f32[648,128]{1,0:T(8,128)S(1)}, f32[648,128]{1,0:T(8,128)S(1)}, u32[]{:S(2)}, u32[]{:S(2)}) collective-permute-start(f32[648,128]{1,0:T(8,128)S(1)} %get-tuple-element.64), channel_id=1, source_target_pairs={{0,2},{2,4},{4,6},{6,0},{1,3},{3,5},{5,7},{7,1},{8,10},{10,12},{12... | collective-permute-start | bytes 995336 | tf_op jit(solution)/shard_map/ppermute | solution.py:352
  68.3 7.9 %collective-permute-start.7 = (f32[5,24,768]{2,1,0:T(8,128)S(1)}, f32[5,24,768]{2,1,0:T(8,128)S(1)}, u32[]{:S(2)}, u32[]{:S(2)}) collective-permute-start(f32[5,24,768]{2,1,0:T(8,128)S(1)} %get-tuple-element.59), channel_id=1, source_target_pairs={{0,8},{8,0},{1,9},{9,1},{2,10},{10,2},{3,11},{11,3},{4,12},{12,4},... | collective-permute-start | bytes 1105928 | tf_op jit(solution)/shard_map/ppermute | solution.py:352
  72.5 35.1 %copy-start.1 = (s32[3]{0:T(128)S(1)}, s32[3]{0:T(128)}, u32[]{:S(2)}) copy-start(s32[3]{0:T(128)} %direction_ref.1) | copy-start | bytes 40
  72.5 3.7 %collective-permute-start.10 = (f32[2,24,768]{2,1,0:T(8,128)S(1)}, f32[2,24,768]{2,1,0:T(8,128)S(1)}, u32[]{:S(2)}, u32[]{:S(2)}) collective-permute-start(f32[2,24,768]{2,1,0:T(8,128)S(1)} %get-tuple-element.62), channel_id=1, source_target_pairs={{0,8},{8,0},{1,9},{9,1},{2,10},{10,2},{3,11},{11,3},{4,12},{12,4},... | collective-permute-start | bytes 442376 | tf_op jit(solution)/shard_map/ppermute | solution.py:352
  75.9 1.4 %collective-permute-start.13 = (f32[1,24,768]{2,1,0:T(8,128)S(1)}, f32[1,24,768]{2,1,0:T(8,128)S(1)}, u32[]{:S(2)}, u32[]{:S(2)}) collective-permute-start(f32[1,24,768]{2,1,0:T(8,128)S(1)} %get-tuple-element.66), channel_id=1, source_target_pairs={{0,8},{8,0},{1,9},{9,1},{2,10},{10,2},{3,11},{11,3},{4,12},{12,4},... | collective-permute-start | bytes 221192 | tf_op jit(solution)/shard_map/ppermute | solution.py:352
  77.4 6.7 %collective-permute-start.14 = (f32[48,768]{1,0:T(8,128)S(1)}, f32[48,768]{1,0:T(8,128)S(1)}, u32[]{:S(2)}, u32[]{:S(2)}) collective-permute-start(f32[48,768]{1,0:T(8,128)S(1)} %get-tuple-element.68), channel_id=1, source_target_pairs={{0,64},{64,128},{128,192},{192,0},{1,65},{65,129},{129,193},{193,1... | collective-permute-start | bytes 442376 | tf_op jit(solution)/shard_map/ppermute | solution.py:352
  78.8 9.6 %collective-permute-start.15 = (f32[48,768]{1,0:T(8,128)S(1)}, f32[48,768]{1,0:T(8,128)S(1)}, u32[]{:S(2)}, u32[]{:S(2)}) collective-permute-start(f32[48,768]{1,0:T(8,128)S(1)} %get-tuple-element.69), channel_id=1, source_target_pairs={{0,128},{64,192},{128,0},{192,64},{1,129},{65,193},{129,1},{193,65... | collective-permute-start | bytes 442376 | tf_op jit(solution)/shard_map/ppermute | solution.py:352
  81.4 7.0 %collective-permute-start.16 = (f32[48,768]{1,0:T(8,128)S(1)}, f32[48,768]{1,0:T(8,128)S(1)}, u32[]{:S(2)}, u32[]{:S(2)}) collective-permute-start(f32[48,768]{1,0:T(8,128)S(1)} %get-tuple-element.70), channel_id=1, source_target_pairs={{0,192},{64,0},{128,64},{192,128},{1,193},{65,1},{129,65},{193,129... | collective-permute-start | bytes 442376 | tf_op jit(solution)/shard_map/ppermute | solution.py:352

commit v9 on v8

--- a/solution.py
+++ b/solution.py
@@ -175,7 +175,7 @@
 def multiply(blocks, phase_ref, rights, first, away_ref, stay_ref, high_ref, low_ref, build=None, offset=0):
     count = len(blocks)
     rows = 24 * count
-    bounds = (0, TILES) if blocks[0] is None else (0, 2, 6, TILES)
+    bounds = (0, TILES) if blocks[0] is None else (0, 1, 3, 5, 7, TILES)
 
     def prepare(chunk):
         for tile in range(bounds[chunk], bounds[chunk + 1]):

time: 109 us -> 109 us (level)
  transfers between devices with their start and end apart: 17 -> 17, of which waited for: 8 -> 8; matrix products, arithmetic and copies ran while one was open for 3% -> 3% of each run, Pallas kernels for 25% -> 24%
where the time goes in v9:
time: 109 us
  starting transfers between devices  32.5 us (30%)
  Pallas kernels  28.7 us (26%)
  waiting for transfers between devices  22.9 us (21%)
  blocking collectives  18.7 us (17%)
  local copies, waits for them, and re-layouts  3.56 us (3%)
  other arithmetic  2.34 us (2%)
    ppermute x17, starting transfers between devices, along(): lax.ppermute(value, axis, [(i, (i + step) % count) for i in range(count)])  32.5 us
    pallas_call x13, Pallas kernels, call(): pl.pallas_call(kernel, out_shape=out_shape, in_specs=[pl.BlockSpec(memory...  28.7 us
    ppermute x17, waiting for transfers between devices, along(): lax.ppermute(value, axis, [(i, (i + step) % count) for i in range(count)])  22.9 us
    all_to_all x1, blocking collectives, local(): mixed = lax.all_to_all(packed, ('zl', 'zh', 'core'), 0, 0)  18.7 us
    unnamed x1, other arithmetic  2.34 us
  transfers between devices with their start and end apart: 17, of which 8 were waited for; matrix products, arithmetic and copies ran while one was open for 3% of the time, Pallas kernels for 24%

profile of v9, /device:TPU:1, one launch (start us, length us, event | category | flops | bytes accessed | tf_op | source)
XLA Modules:
  0.0 108.9 jit_solution(7479854475513826417)
XLA Ops:
  0.0 0.0 copy-start.2
  0.0 1.5 %copy.6 = f32[2,3,24,1,2304]{4,2,3,1,0:T(8,128)S(1)} copy(f32[2,3,24,1,2304]{4,3,2,1,0:T(1,128)} %param.4) | data formatting | bytes 2654208
  1.5 0.0 copy-start
  1.5 1.0 cut.1
  2.4 3.3 %collective-permute-start.1 = (f32[1296,128]{1,0:T(8,128)}, f32[1296,128]{1,0:T(8,128)S(1)}, u32[]{:S(2)}, u32[]{:S(2)}) collective-permute-start(f32[1296,128]{1,0:T(8,128)} %get-tuple-element.57.keep), channel_id=1, source_target_pairs={{0,6},{2,0},{4,2},{6,4},{1,7},{3,1},{5,3},{7,5},{8,14},{10,8},{12,... | collective-permute-start | bytes 1990664 | tf_op jit(solution)/shard_map/ppermute | solution.py:352
  5.7 0.0 collective-permute-start.2
  5.7 6.9 %collective-permute-start = (f32[1368,128]{1,0:T(8,128)S(1)}, f32[1368,128]{1,0:T(8,128)S(1)}, u32[]{:S(2)}, u32[]{:S(2)}) collective-permute-start(f32[1368,128]{1,0:T(8,128)S(1)} %get-tuple-element.39), channel_id=1, source_target_pairs={{0,1},{1,0},{2,3},{3,2},{4,5},{5,4},{6,7},{7,6},{8,9},{9,8},{10,11... | collective-permute-start | bytes 2101256 | tf_op jit(solution)/shard_map/ppermute | solution.py:352
  12.7 0.0 copy-done.2
  12.7 2.3 %reduce = f32[3,2,3,3,2304]{4,3,2,1,0:T(4,128)} reduce(f32[3,2,3,3,1,2304]{5,4,3,2,1,0:T(1,128)S(1)} %copy-done.2, f32[]{:T(128)} %constant.2), dimensions={4}, to_apply=%param.5.reduce_sub_computation | reduce | bytes 995332 | tf_op args[1]
  15.0 1.3 %reshape.7.link_ref = f32[54,2304]{1,0:T(8,128)S(1)} reshape(f32[3,2,3,3,2304]{4,3,2,1,0:T(4,128)} %reduce) | data formatting | bytes 995328 | tf_op jit(solution)/shard_map/reshape | solution.py:368
  16.4 0.0 copy-done
  16.4 0.7 phase.1.phase_ref
  17.1 2.5 %collective-permute-done.1.after = f32[1296,128]{1,0:T(8,128)S(1)} collective-permute-done((f32[1296,128]{1,0:T(8,128)}, f32[1296,128]{1,0:T(8,128)S(1)}, u32[]{:S(2)}, u32[]{:S(2)}) %collective-permute-start.1) | collective-permute-done | bytes 663584 | tf_op jit(solution)/shard_map/ppermute | solution.py:352
  19.7 3.0 %collective-permute-done.2.before = f32[1296,128]{1,0:T(8,128)S(1)} collective-permute-done((f32[1296,128]{1,0:T(8,128)}, f32[1296,128]{1,0:T(8,128)S(1)}, u32[]{:S(2)}, u32[]{:S(2)}) %collective-permute-start.2) | collective-permute-done | bytes 663584 | tf_op jit(solution)/shard_map/ppermute | solution.py:352
  22.6 0.4 collective-permute-start.3
  23.1 1.1 %collective-permute-start.4 = (f32[648,128]{1,0:T(8,128)S(1)}, f32[648,128]{1,0:T(8,128)S(1)}, u32[]{:S(2)}, u32[]{:S(2)}) collective-permute-start(f32[648,128]{1,0:T(8,128)S(1)} %slice.9), channel_id=1, source_target_pairs={{0,2},{2,4},{4,6},{6,0},{1,3},{3,5},{5,7},{7,1},{8,10},{10,12},{12... | collective-permute-start | bytes 995336 | tf_op jit(solution)/shard_map/ppermute | solution.py:352
  24.2 6.0 %collective-permute-done.3.real = f32[648,128]{1,0:T(8,128)S(1)} collective-permute-done((f32[648,128]{1,0:T(8,128)S(1)}, f32[648,128]{1,0:T(8,128)S(1)}, u32[]{:S(2)}, u32[]{:S(2)}) %collective-permute-start.3) | collective-permute-done | bytes 331808 | tf_op jit(solution)/shard_map/ppermute | solution.py:352
  30.2 1.6 %collective-permute-done.4.imag = f32[648,128]{1,0:T(8,128)S(1)} collective-permute-done((f32[648,128]{1,0:T(8,128)S(1)}, f32[648,128]{1,0:T(8,128)S(1)}, u32[]{:S(2)}, u32[]{:S(2)}) %collective-permute-start.4) | collective-permute-done | bytes 331808 | tf_op jit(solution)/shard_map/ppermute | solution.py:352
  31.8 2.3 %left.1 = (bf16[576,3456]{1,0:T(8,128)(2,1)S(1)}, bf16[576,3456]{1,0:T(8,128)(2,1)S(1)}, f32[8,128]{1,0:T(8,128)S(1)}) custom-call(f32[1296,128]{1,0:T(8,128)S(1)} %collective-permute-done.1.after, f32[1296,128]{1,0:T(8,128)S(1)} %collective-permute-done.2.before, f32[648,128]{1,0:T(8,128)S(1)} %collective-permute-done.3.real, ...), custom_call_target="tpu_custom_call" | custom-call | flops 300000000 | bytes 900000 | tf_op jit(solution)/shard_map/left/pallas_call | solution.py:336
  34.0 0.0 collective-permute-done.came
  34.1 0.4 collective-permute-start.8
  34.4 1.2 %collective-permute-start.9 = (f32[1368,128]{1,0:T(8,128)S(1)}, f32[1368,128]{1,0:T(8,128)S(1)}, u32[]{:S(2)}, u32[]{:S(2)}) collective-permute-start(f32[1368,128]{1,0:T(8,128)S(1)} %collective-permute-done.came), channel_id=1, source_target_pairs={{0,2},{2,4},{4,6},{6,0},{1,3},{3,5},{5,7},{7,1},{8,10},{10,12},{12... | collective-permute-start | bytes 2101256 | tf_op jit(solution)/shard_map/ppermute | solution.py:352
  35.6 10.4 %collective-permute-start.6 = (f32[1368,128]{1,0:T(8,128)S(1)}, f32[1368,128]{1,0:T(8,128)S(1)}, u32[]{:S(2)}, u32[]{:S(2)}) collective-permute-start(f32[1368,128]{1,0:T(8,128)S(1)} %collective-permute-done.came), channel_id=1, source_target_pairs={{0,248},{8,0},{16,8},{24,16},{32,24},{40,32},{48,40},{56,48},{64,5... | collective-permute-start | bytes 2101256 | tf_op jit(solution)/shard_map/ppermute | solution.py:352
  46.0 0.0 collective-permute-start.5
  46.0 6.8 %own.1 = (bf16[576,3456]{1,0:T(8,128)(2,1)S(1)}, f32[2,24,768]{2,1,0:T(8,128)S(1)}, f32[2,24,768]{2,1,0:T(8,128)S(1)}, bf16[384,3456]{1,0:T(8,128)(2,1)S(1)}, bf16[384,3456]{1,0:T(8,128)(2,1)S(1)}) custom-call(f32[1296,128]{1,0:T(8,128)} %get-tuple-element.57.keep, f32[1368,128]{1,0:T(8,128)S(1)} %collective-permute-done.came, ...), custom_call_target="tpu_custom_call" | custom-call | flops 1800000000 | bytes 5399999 | tf_op jit(solution)/shard_map/own/pallas_call | solution.py:336
  52.8 5.7 %kept.1 = (f32[3,24,768]{2,1,0:T(8,128)S(1)}, f32[3,24,768]{2,1,0:T(8,128)S(1)}) custom-call(bf16[576,3456]{1,0:T(8,128)(2,1)S(1)} %get-tuple-element.52.high.kept_high, bf16[576,3456]{1,0:T(8,128)(2,1)S(1)} %get-tuple-element.53.low.kept_low, bf16[576,3456]{1,0:T(8,128)(2,1)S(1)} %get-tuple-element.54.right), custom_call_target="tpu_custom_call" | custom-call | flops 1800000000 | bytes 5399999 | tf_op jit(solution)/shard_map/kept/pallas_call | solution.py:336
  58.5 0.0 collective-permute-done.8.after
  58.5 0.0 collective-permute-done.9.before
  58.5 3.0 %collective-permute-start.11 = (f32[648,128]{1,0:T(8,128)S(1)}, f32[648,128]{1,0:T(8,128)S(1)}, u32[]{:S(2)}, u32[]{:S(2)}) collective-permute-start(f32[648,128]{1,0:T(8,128)S(1)} %get-tuple-element.63), channel_id=1, source_target_pairs={{0,6},{2,0},{4,2},{6,4},{1,7},{3,1},{5,3},{7,5},{8,14},{10,8},{12,... | collective-permute-start | bytes 995336 | tf_op jit(solution)/shard_map/ppermute | solution.py:352
  61.6 0.0 collective-permute-start.12
  61.6 2.6 %collective-permute-done.5.zkeep = f32[1296,128]{1,0:T(8,128)S(1)} collective-permute-done((f32[1296,128]{1,0:T(8,128)}, f32[1296,128]{1,0:T(8,128)S(1)}, u32[]{:S(2)}, u32[]{:S(2)}) %collective-permute-start.5) | collective-permute-done | bytes 663584 | tf_op jit(solution)/shard_map/ppermute | solution.py:352
  64.2 0.0 collective-permute-done.6.zcame
  64.2 4.1 %zfield.1 = (bf16[192,3456]{1,0:T(8,128)(2,1)S(1)}, f32[5,24,768]{2,1,0:T(8,128)S(1)}, f32[5,24,768]{2,1,0:T(8,128)S(1)}) custom-call(f32[2,24,768]{2,1,0:T(8,128)S(1)} %get-tuple-element.48.own_away, f32[2,24,768]{2,1,0:T(8,128)S(1)} %get-tuple-element.49.own_stay, bf16[384,3456]{1,0:T(8,128)(2,1)S(1)} %get-tuple-element.50.own_high, ...), custom_call_target="tpu_custom_call" | custom-call | flops 1500000000 | bytes 4500000 | tf_op jit(solution)/shard_map/zfield/pallas_call | solution.py:336
  68.3 0.1 collective-permute-start.7
  68.4 4.1 %came.1 = (f32[2,24,768]{2,1,0:T(8,128)S(1)}, f32[2,24,768]{2,1,0:T(8,128)S(1)}) custom-call(f32[1368,128]{1,0:T(8,128)S(1)} %collective-permute-done.8.after, f32[1368,128]{1,0:T(8,128)S(1)} %collective-permute-done.9.before, f32[9,8,128]{2,1,0:T(8,128)S(1)} %phase.1.phase_ref, bf16[576,3456]{1,0:T(8,128)(2,1)S(1)} %get-tuple-element.54.right, ...), custom_call_target="tpu_custom_call" | custom-call | flops 1200000000 | bytes 3600000 | tf_op jit(solution)/shard_map/came/pallas_call | solution.py:336
  72.5 0.0 copy-start.1
  72.5 0.6 collective-permute-start.10
  73.1 0.0 collective-permute-done.11.real
  73.1 0.0 collective-permute-done.12.imag
  73.1 2.9 %far.1 = (f32[1,24,768]{2,1,0:T(8,128)S(1)}, f32[1,24,768]{2,1,0:T(8,128)S(1)}) custom-call(f32[648,128]{1,0:T(8,128)S(1)} %collective-permute-done.11.real, f32[648,128]{1,0:T(8,128)S(1)} %collective-permute-done.12.imag, f32[9,8,128]{2,1,0:T(8,128)S(1)} %phase.1.phase_ref, bf16[576,3456]{1,0:T(8,128)(2,1)S(1)} %get-tuple-element.54.right, ...), custom_call_target="tpu_custom_call" | custom-call | flops 900000000 | bytes 2699999 | tf_op jit(solution)/shard_map/far/pallas_call | solution.py:336
  76.0 0.1 collective-permute-start.13
  76.1 0.0 collective-permute-done.10.refs_3_
  76.1 0.0 collective-permute-done.7.refs_1_
  76.1 1.2 %collective-permute-done.13.refs_5_ = f32[1,24,768]{2,1,0:T(8,128)S(1)} collective-permute-done((f32[1,24,768]{2,1,0:T(8,128)S(1)}, f32[1,24,768]{2,1,0:T(8,128)S(1)}, u32[]{:S(2)}, u32[]{:S(2)}) %collective-permute-start.13) | collective-permute-done | bytes 73760 | tf_op jit(solution)/shard_map/ppermute | solution.py:352
  77.4 0.1 add.2
  77.5 1.4 %collective-permute-start.14 = (f32[48,768]{1,0:T(8,128)S(1)}, f32[48,768]{1,0:T(8,128)S(1)}, u32[]{:S(2)}, u32[]{:S(2)}) collective-permute-start(f32[48,768]{1,0:T(8,128)S(1)} %get-tuple-element.68), channel_id=1, source_target_pairs={{0,64},{64,128},{128,192},{192,0},{1,65},{65,129},{129,193},{193,1... | collective-permute-start | bytes 442376 | tf_op jit(solution)/shard_map/ppermute | solution.py:352
  78.8 2.6 %collective-permute-start.15 = (f32[48,768]{1,0:T(8,128)S(1)}, f32[48,768]{1,0:T(8,128)S(1)}, u32[]{:S(2)}, u32[]{:S(2)}) collective-permute-start(f32[48,768]{1,0:T(8,128)S(1)} %get-tuple-element.69), channel_id=1, source_target_pairs={{0,128},{64,192},{128,0},{192,64},{1,129},{65,193},{129,1},{193,65... | collective-permute-start | bytes 442376 | tf_op jit(solution)/shard_map/ppermute | solution.py:352
  81.5 1.1 collective-permute-start.16
  82.5 1.7 %collective-permute-done.14.second = f32[48,768]{1,0:T(8,128)S(1)} collective-permute-done((f32[48,768]{1,0:T(8,128)S(1)}, f32[48,768]{1,0:T(8,128)S(1)}, u32[]{:S(2)}, u32[]{:S(2)}) %collective-permute-start.14) | collective-permute-done | bytes 147488 | tf_op jit(solution)/shard_map/ppermute | solution.py:352
  84.2 4.3 %collective-permute-done.15.third = f32[48,768]{1,0:T(8,128)S(1)} collective-permute-done((f32[48,768]{1,0:T(8,128)S(1)}, f32[48,768]{1,0:T(8,128)S(1)}, u32[]{:S(2)}, u32[]{:S(2)}) %collective-permute-start.15) | collective-permute-done | bytes 147488 | tf_op jit(solution)/shard_map/ppermute | solution.py:352
  88.5 0.0 collective-permute-done.16.fourth
  88.5 0.2 pack.1
  88.7 18.7 %all_to_all.5.part_ref = f32[16,1,2304]{2,1,0:T(1,128)S(1)} all-to-all(f32[16,1,2304]{2,1,0:T(1,128)S(1)} %pack.1), channel_id=1, replica_groups=mesh['y'=4,'zl'=4,'core'=2,'x'=4,'zh'=2] {'zl','zh','core'}, dimensions={0} | all-to-all | bytes 294912 | tf_op jit(solution)/shard_map/all_to_all | solution.py:406
  107.4 0.0 copy-done.1
  107.4 0.8 last.1
  108.2 0.7 copy.5
  (4 shorter events, 0.1 us)
Async XLA Ops:
  0.0 12.7 %copy-start.2 = (f32[3,2,3,3,1,2304]{5,4,3,2,1,0:T(1,128)S(1)}, f32[3,2,3,3,1,2304]{5,4,3,2,1,0:T(1,128)}, u32[]{:S(2)}) copy-start(f32[3,2,3,3,1,2304]{5,4,3,2,1,0:T(1,128)} %param.5) | copy-start | bytes 1492996
  1.5 14.9 %copy-start = (s32[4,3]{1,0:T(4,128)S(1)}, s32[4,3]{1,0:T(4,128)}, u32[]{:S(2)}) copy-start(s32[4,3]{1,0:T(4,128)} %mom_ref.1) | copy-start | bytes 148
  2.4 17.2 %collective-permute-start.1 = (f32[1296,128]{1,0:T(8,128)}, f32[1296,128]{1,0:T(8,128)S(1)}, u32[]{:S(2)}, u32[]{:S(2)}) collective-permute-start(f32[1296,128]{1,0:T(8,128)} %get-tuple-element.57.keep), channel_id=1, source_target_pairs={{0,6},{2,0},{4,2},{6,4},{1,7},{3,1},{5,3},{7,5},{8,14},{10,8},{12,... | collective-permute-start | bytes 1990664 | tf_op jit(solution)/shard_map/ppermute | solution.py:352
  5.7 16.9 %collective-permute-start.2 = (f32[1296,128]{1,0:T(8,128)}, f32[1296,128]{1,0:T(8,128)S(1)}, u32[]{:S(2)}, u32[]{:S(2)}) collective-permute-start(f32[1296,128]{1,0:T(8,128)} %get-tuple-element.57.keep), channel_id=1, source_target_pairs={{0,2},{2,4},{4,6},{6,0},{1,3},{3,5},{5,7},{7,1},{8,10},{10,12},{12... | collective-permute-start | bytes 1990664 | tf_op jit(solution)/shard_map/ppermute | solution.py:352
  5.7 28.3 %collective-permute-start = (f32[1368,128]{1,0:T(8,128)S(1)}, f32[1368,128]{1,0:T(8,128)S(1)}, u32[]{:S(2)}, u32[]{:S(2)}) collective-permute-start(f32[1368,128]{1,0:T(8,128)S(1)} %get-tuple-element.39), channel_id=1, source_target_pairs={{0,1},{1,0},{2,3},{3,2},{4,5},{5,4},{6,7},{7,6},{8,9},{9,8},{10,11... | collective-permute-start | bytes 2101256 | tf_op jit(solution)/shard_map/ppermute | solution.py:352
  22.6 7.5 %collective-permute-start.3 = (f32[648,128]{1,0:T(8,128)S(1)}, f32[648,128]{1,0:T(8,128)S(1)}, u32[]{:S(2)}, u32[]{:S(2)}) collective-permute-start(f32[648,128]{1,0:T(8,128)S(1)} %slice.8), channel_id=1, source_target_pairs={{0,6},{2,0},{4,2},{6,4},{1,7},{3,1},{5,3},{7,5},{8,14},{10,8},{12,... | collective-permute-start | bytes 995336 | tf_op jit(solution)/shard_map/ppermute | solution.py:352
  23.1 8.7 %collective-permute-start.4 = (f32[648,128]{1,0:T(8,128)S(1)}, f32[648,128]{1,0:T(8,128)S(1)}, u32[]{:S(2)}, u32[]{:S(2)}) collective-permute-start(f32[648,128]{1,0:T(8,128)S(1)} %slice.9), channel_id=1, source_target_pairs={{0,2},{2,4},{4,6},{6,0},{1,3},{3,5},{5,7},{7,1},{8,10},{10,12},{12... | collective-permute-start | bytes 995336 | tf_op jit(solution)/shard_map/ppermute | solution.py:352
  34.1 24.4 %collective-permute-start.8 = (f32[1368,128]{1,0:T(8,128)S(1)}, f32[1368,128]{1,0:T(8,128)S(1)}, u32[]{:S(2)}, u32[]{:S(2)}) collective-permute-start(f32[1368,128]{1,0:T(8,128)S(1)} %collective-permute-done.came), channel_id=1, source_target_pairs={{0,6},{2,0},{4,2},{6,4},{1,7},{3,1},{5,3},{7,5},{8,14},{10,8},{12,... | collective-permute-start | bytes 2101256 | tf_op jit(solution)/shard_map/ppermute | solution.py:352
  34.4 24.1 %collective-permute-start.9 = (f32[1368,128]{1,0:T(8,128)S(1)}, f32[1368,128]{1,0:T(8,128)S(1)}, u32[]{:S(2)}, u32[]{:S(2)}) collective-permute-start(f32[1368,128]{1,0:T(8,128)S(1)} %collective-permute-done.came), channel_id=1, source_target_pairs={{0,2},{2,4},{4,6},{6,0},{1,3},{3,5},{5,7},{7,1},{8,10},{10,12},{12... | collective-permute-start | bytes 2101256 | tf_op jit(solution)/shard_map/ppermute | solution.py:352
  35.6 28.6 %collective-permute-start.6 = (f32[1368,128]{1,0:T(8,128)S(1)}, f32[1368,128]{1,0:T(8,128)S(1)}, u32[]{:S(2)}, u32[]{:S(2)}) collective-permute-start(f32[1368,128]{1,0:T(8,128)S(1)} %collective-permute-done.came), channel_id=1, source_target_pairs={{0,248},{8,0},{16,8},{24,16},{32,24},{40,32},{48,40},{56,48},{64,5... | collective-permute-start | bytes 2101256 | tf_op jit(solution)/shard_map/ppermute | solution.py:352
  46.0 18.3 %collective-permute-start.5 = (f32[1296,128]{1,0:T(8,128)}, f32[1296,128]{1,0:T(8,128)S(1)}, u32[]{:S(2)}, u32[]{:S(2)}) collective-permute-start(f32[1296,128]{1,0:T(8,128)} %get-tuple-element.57.keep), channel_id=1, source_target_pairs={{0,248},{8,0},{16,8},{24,16},{32,24},{40,32},{48,40},{56,48},{64,5... | collective-permute-start | bytes 1990664 | tf_op jit(solution)/shard_map/ppermute | solution.py:352
  58.5 14.6 %collective-permute-start.11 = (f32[648,128]{1,0:T(8,128)S(1)}, f32[648,128]{1,0:T(8,128)S(1)}, u32[]{:S(2)}, u32[]{:S(2)}) collective-permute-start(f32[648,128]{1,0:T(8,128)S(1)} %get-tuple-element.63), channel_id=1, source_target_pairs={{0,6},{2,0},{4,2},{6,4},{1,7},{3,1},{5,3},{7,5},{8,14},{10,8},{12,... | collective-permute-start | bytes 995336 | tf_op jit(solution)/shard_map/ppermute | solution.py:352
  61.6 11.5 %collective-permute-start.12 = (f32[648,128]{1,0:T(8,128)S(1)}, f32[648,128]{1,0:T(8,128)S(1)}, u32[]{:S(2)}, u32[]{:S(2)}) collective-permute-start(f32[648,128]{1,0:T(8,128)S(1)} %get-tuple-element.64), channel_id=1, source_target_pairs={{0,2},{2,4},{4,6},{6,0},{1,3},{3,5},{5,7},{7,1},{8,10},{10,12},{12... | collective-permute-start | bytes 995336 | tf_op jit(solution)/shard_map/ppermute | solution.py:352
  68.3 7.8 %collective-permute-start.7 = (f32[5,24,768]{2,1,0:T(8,128)S(1)}, f32[5,24,768]{2,1,0:T(8,128)S(1)}, u32[]{:S(2)}, u32[]{:S(2)}) collective-permute-start(f32[5,24,768]{2,1,0:T(8,128)S(1)} %get-tuple-element.59), channel_id=1, source_target_pairs={{0,8},{8,0},{1,9},{9,1},{2,10},{10,2},{3,11},{11,3},{4,12},{12,4},... | collective-permute-start | bytes 1105928 | tf_op jit(solution)/shard_map/ppermute | solution.py:352
  72.5 34.9 %copy-start.1 = (s32[3]{0:T(128)S(1)}, s32[3]{0:T(128)}, u32[]{:S(2)}) copy-start(s32[3]{0:T(128)} %direction_ref.1) | copy-start | bytes 40
  72.5 3.6 %collective-permute-start.10 = (f32[2,24,768]{2,1,0:T(8,128)S(1)}, f32[2,24,768]{2,1,0:T(8,128)S(1)}, u32[]{:S(2)}, u32[]{:S(2)}) collective-permute-start(f32[2,24,768]{2,1,0:T(8,128)S(1)} %get-tuple-element.62), channel_id=1, source_target_pairs={{0,8},{8,0},{1,9},{9,1},{2,10},{10,2},{3,11},{11,3},{4,12},{12,4},... | collective-permute-start | bytes 442376 | tf_op jit(solution)/shard_map/ppermute | solution.py:352
  76.0 1.4 %collective-permute-start.13 = (f32[1,24,768]{2,1,0:T(8,128)S(1)}, f32[1,24,768]{2,1,0:T(8,128)S(1)}, u32[]{:S(2)}, u32[]{:S(2)}) collective-permute-start(f32[1,24,768]{2,1,0:T(8,128)S(1)} %get-tuple-element.66), channel_id=1, source_target_pairs={{0,8},{8,0},{1,9},{9,1},{2,10},{10,2},{3,11},{11,3},{4,12},{12,4},... | collective-permute-start | bytes 221192 | tf_op jit(solution)/shard_map/ppermute | solution.py:352
  77.5 6.7 %collective-permute-start.14 = (f32[48,768]{1,0:T(8,128)S(1)}, f32[48,768]{1,0:T(8,128)S(1)}, u32[]{:S(2)}, u32[]{:S(2)}) collective-permute-start(f32[48,768]{1,0:T(8,128)S(1)} %get-tuple-element.68), channel_id=1, source_target_pairs={{0,64},{64,128},{128,192},{192,0},{1,65},{65,129},{129,193},{193,1... | collective-permute-start | bytes 442376 | tf_op jit(solution)/shard_map/ppermute | solution.py:352
  78.8 9.6 %collective-permute-start.15 = (f32[48,768]{1,0:T(8,128)S(1)}, f32[48,768]{1,0:T(8,128)S(1)}, u32[]{:S(2)}, u32[]{:S(2)}) collective-permute-start(f32[48,768]{1,0:T(8,128)S(1)} %get-tuple-element.69), channel_id=1, source_target_pairs={{0,128},{64,192},{128,0},{192,64},{1,129},{65,193},{129,1},{193,65... | collective-permute-start | bytes 442376 | tf_op jit(solution)/shard_map/ppermute | solution.py:352
  81.5 7.0 %collective-permute-start.16 = (f32[48,768]{1,0:T(8,128)S(1)}, f32[48,768]{1,0:T(8,128)S(1)}, u32[]{:S(2)}, u32[]{:S(2)}) collective-permute-start(f32[48,768]{1,0:T(8,128)S(1)} %get-tuple-element.70), channel_id=1, source_target_pairs={{0,192},{64,0},{128,64},{192,128},{1,193},{65,1},{129,65},{193,129... | collective-permute-start | bytes 442376 | tf_op jit(solution)/shard_map/ppermute | solution.py:352
